TPU v7x, 32 devices: a whole 2x2x4 slice. The times are simulated.
32 devices in a mesh: gz: 8 (over z, y), gy: 4 (over x, core).
Axes of the slice: x: 2, y: 2, z: 4, core: 2. Of those that a mesh axis runs over, the one named last changes fastest.
Arguments:
- species_field: float32 [4, 512, 512, 512], P(None, 'gz', 'gy'), may hold values from -100 to 100
Outputs:
- core_tensor: float32 [4, 512, 4096], P(None, ('gz', 'gy'))
- basis_z: float32 [512, 64], replicated
- basis_y: float32 [512, 64], replicated
All inputs are finite; a program needn't handle non-finite values.
Results may differ from a plain program's by a relative error of at most 0.0003.
Values sent between devices are 32-bit elements; how exact they have to be, the bound alone decides.
No kernel may reach another device: no remote copies, remote signals or barrier semaphores. Data moves between devices by JAX's collectives and lax.ppermute only.
A program may use at most 320 MiB of HBM per device.

v0:
```python
import math

import jax
import jax.numpy as jnp
from jax import lax
from jax.sharding import PartitionSpec as P

GRID = 512
RANK = 64
ITERS = 4


def start_table(order, width):
    row_index = jnp.arange(order).astype(jnp.float32)
    col_index = jnp.arange(width).astype(jnp.float32)
    return jnp.cos(math.pi * (row_index[:, None] + 0.5) * col_index[None, :] / order)


def solve_factor(product, inner_gram):
    factor = jnp.linalg.cholesky(inner_gram)
    return lax.linalg.triangular_solve(
        factor, product, left_side=False, lower=True, transpose_a=True
    )


def inner_products(left, right):
    return lax.dot_general(left, right, (((0,), (0,)), ((), ())), precision=lax.Precision.HIGHEST)


def mode_products(left, right, mode):
    others = tuple((d for d in range(4) if d != mode))
    return lax.dot_general(
        left, right, ((others, others), ((), ())), precision=lax.Precision.HIGHEST
    )


def leaf_basis(fibres, mode):
    basis_now = start_table(GRID, RANK)
    gram_total = lax.psum(mode_products(fibres, fibres, mode), ("gz", "gy"))
    for iteration in range(ITERS):
        product = jnp.dot(gram_total, basis_now, precision=lax.Precision.HIGHEST)
        basis_now = solve_factor(product, inner_products(product, product))
    return basis_now


def body(species_field):
    fibres_z = lax.all_to_all(species_field, "gz", split_axis=2, concat_axis=1, tiled=True)
    basis_z = leaf_basis(fibres_z, 1)
    reduced = jnp.einsum("szyx,zr->sryx", fibres_z, basis_z, precision=lax.Precision.HIGHEST)
    mixed = lax.all_to_all(reduced, ("gz", "gy"), split_axis=3, concat_axis=2, tiled=True)
    count_gz = lax.axis_size("gz")
    count_gy = lax.axis_size("gy")
    shape_now = mixed.shape
    y_local = shape_now[2] // (count_gz * count_gy)
    blocks = mixed.reshape(shape_now[0], shape_now[1], count_gz, count_gy, y_local, shape_now[3])
    fibres_y = jnp.transpose(blocks, (0, 1, 3, 2, 4, 5)).reshape(shape_now)
    basis_y = leaf_basis(fibres_y, 2)
    core_tensor = jnp.einsum("sryx,yq->sxrq", fibres_y, basis_y, precision=lax.Precision.HIGHEST)
    core_tensor = core_tensor.reshape(fibres_y.shape[0], fibres_y.shape[3], RANK * RANK)
    return (core_tensor, basis_z, basis_y)


def solution(mesh):
    in_specs = (P(None, "gz", "gy", None),)
    out_specs = (P(None, ("gz", "gy"), None), P(), P())
    return jax.shard_map(body, mesh=mesh, in_specs=in_specs, out_specs=out_specs, check_vma=False)
```

profile of v0, /device:TPU:0, one launch (start us, length us, event | category | flops | bytes accessed | tf_op | source)
XLA Modules:
  0.0 2454.7 jit_solution(18091183311840595509)
XLA Ops:
  7.2 56.3 %copy.29 = f32[4,64,128,512]{3,1,0,2:T(8,128)} copy(f32[4,64,128,512]{3,2,1,0:T(8,128)} %param.4) | data formatting | bytes 134217728 | tf_op args[0]
  63.5 1461.3 %all_to_all.33 = f32[4,64,128,512]{3,1,0,2:T(8,128)} all-to-all(f32[4,64,128,512]{3,1,0,2:T(8,128)} %copy.29), channel_id=1, replica_groups=mesh['gz'=8,'gy'=4] {'gz'}, dimensions={2} | all-to-all | bytes 134217728 | tf_op jit(solution)/shard_map/all_to_all | solution.py:47
  1524.8 43.8 %copy.30 = f32[4,64,8,16,512]{4,1,2,3,0:T(8,128)} copy(f32[4,64,8,16,512]{4,1,0,3,2:T(8,128)} %bitcast) | data formatting | bytes 134217728 | tf_op jit(solution)/shard_map/all_to_all | solution.py:47
  1568.6 116.7 %convolution_bitcast_fusion.3 = f32[512,512]{1,0:T(8,128)} fusion(f32[4,512,16,512]{3,1,2,0:T(8,128)} %bitcast.2), kind=kOutput, calls=%fused_computation.3 | convolution fusion | flops 103079215104 | bytes 68157440 | tf_op jit(solution)/shard_map/dot_general | solution.py:32
  1685.6 128.8 %all-reduce.3.cloned.1.call-done = f32[512,512]{1,0:T(8,128)} async-done(((f32[512,512]{1,0:T(8,128)}), f32[512,512]{1,0:T(8,128)}) %all-reduce.3.cloned.1.call-update) | async-done | bytes 1048592 | tf_op jit(solution)/shard_map/psum | solution.py:39
  1814.4 3.3 fusion.1
  1818.1 5.8 cholesky.134
  1824.0 0.6 compare_reduce_fusion.7
  1824.6 0.7 fusion.10
  1825.3 4.9 custom-call.12
  1830.2 0.3 convolution_bitcast_fusion.9
  1830.5 2.4 fusion.53
  1833.2 5.8 cholesky.145
  1839.1 0.6 compare_reduce_fusion.6
  1839.7 0.7 fusion.11
  1840.4 4.9 custom-call.13
  1845.3 0.3 convolution_bitcast_fusion.8
  1845.6 2.4 fusion.55
  1848.4 5.8 cholesky.156
  1854.2 0.6 compare_reduce_fusion.5
  1854.9 0.7 fusion.12
  1855.6 4.9 custom-call.14
  1860.8 2.4 fusion.57
  1863.5 5.8 cholesky.167
  1869.4 0.6 compare_reduce_fusion.4
  1870.0 1.1 fusion.13
  1871.1 4.9 custom-call.15
  1876.0 0.3 fusion.27
  1876.4 48.3 %convolution_bitcast_fusion = f32[4,64,16,512]{3,1,2,0:T(8,128)} fusion(f32[4,512,16,512]{3,1,2,0:T(8,128)} %bitcast.2, f32[64,512]{1,0:T(8,128)S(1)} %fusion.27), kind=kOutput, calls=%fused_computation | convolution fusion | flops 12884901888 | bytes 75628544 | tf_op jit(solution)/shard_map/szyx,zr->sryx/dot_general | solution.py:49
  1924.6 16.2 copy.35
  1940.9 25.3 %reshape.76 = f32[32,1,65536]{2,1,0:T(1,128)} reshape(f32[512,4,16,64]{3,2,1,0:T(8,128)} %bitcast.169) | data formatting | bytes 16777216
  1966.2 187.4 %all_to_all.34 = f32[32,1,65536]{2,1,0:T(1,128)} all-to-all(f32[32,1,65536]{2,1,0:T(1,128)} %reshape.76), channel_id=1, replica_groups=mesh['gz'=8,'gy'=4] {'gz','gy'}, dimensions={0} | all-to-all | bytes 16777216 | tf_op jit(solution)/shard_map/all_to_all | solution.py:50
  2153.6 0.5 broadcast.80
  2154.1 25.1 %reduce.4 = f32[32,65536]{1,0:T(8,128)} reduce(f32[32,1,65536]{2,1,0:T(1,128)} %all_to_all.34, f32[]{:T(128)} %broadcast.80), dimensions={1}, to_apply=%all_to_all.28.reduce_sub_computation | reduce | bytes 16777220 | tf_op jit(solution)/shard_map/all_to_all | solution.py:50
  2179.2 12.2 reshape.77
  2191.4 15.9 copy.37
  2207.2 12.7 copy.38
  2219.9 17.4 convolution_bitcast_fusion.2
  2237.4 129.2 %all-reduce.5.cloned.1.call-done = f32[512,512]{1,0:T(8,128)} async-done(((f32[512,512]{1,0:T(8,128)}), f32[512,512]{1,0:T(8,128)}) %all-reduce.5.cloned.1.call-update) | async-done | bytes 1048592 | tf_op jit(solution)/shard_map/psum | solution.py:39
  2366.6 3.3 fusion
  2370.3 5.8 cholesky.178
  2376.1 0.6 compare_reduce_fusion.3
  2376.8 0.7 fusion.14
  2377.4 4.9 custom-call.16
  2382.7 2.4 fusion.60
  2385.4 5.8 cholesky.189
  2391.3 0.6 compare_reduce_fusion.2
  2391.9 0.7 fusion.15
  2392.6 4.9 custom-call.17
  2397.5 0.3 convolution_bitcast_fusion.5
  2397.8 2.4 fusion.62
  2400.6 5.8 cholesky.200
  2406.4 0.6 compare_reduce_fusion.1
  2407.1 0.7 fusion.16
  2407.7 4.9 custom-call.18
  2412.6 0.3 convolution_bitcast_fusion.4
  2413.0 2.4 fusion.64
  2415.7 5.8 cholesky.211
  2421.6 0.6 compare_reduce_fusion
  2422.2 0.7 fusion.17
  2422.9 5.1 custom-call.19
  2428.3 15.6 convolution_bitcast_fusion.1
  2443.9 1.9 copy.45
  2445.8 1.6 reshape.41
  (45 shorter events, 4.4 us)
Async XLA Ops:
  7.2 1807.3 %all-reduce.3.cloned.1.call-start = ((), (), s32[]{:S(2)}) async-start(), calls=%async_computation.2 | async-start | bytes 2097152 | tf_op jit(solution)/shard_map/psum | solution.py:39
  1685.3 681.3 %all-reduce.5.cloned.1.call-start = ((), (), s32[]{:S(2)}) async-start(), calls=%async_computation.3 | async-start | bytes 2097152 | tf_op jit(solution)/shard_map/psum | solution.py:39
  1876.3 48.3 %copy-start = (f32[64,512]{1,0:T(8,128)}, f32[64,512]{1,0:T(8,128)S(1)}, u32[]{:S(2)}) copy-start(f32[64,512]{1,0:T(8,128)S(1)} %fusion.27) | copy-start | bytes 393220
  2428.3 19.1 copy-start.1
Sparse Core Ops, SparseCore 0:
  1685.4 128.9 all-reduce.2
  2237.5 129.0 all-reduce.4
where the time goes:
time: 2460 us; the launch traced here: 2450 us
  blocking collectives  1650 us (67%)
  waiting for transfers between devices  258 us (10%)
  matrix products  223 us (9%)
  local copies, waits for them, and re-layouts  187 us (8%)
  other arithmetic  122 us (5%)
    all_to_all x1, blocking collectives, body(): lax.all_to_all(species_field, 'gz', split_axis=2, concat_axis=1, tiled=True)  1460 us
    psum x2, waiting for transfers between devices, leaf_basis(): gram_total = lax.psum(mode_products(fibres, fibres, mode), ('gz', 'gy'))  258 us
    all_to_all x1, blocking collectives, body(): lax.all_to_all(reduced, ('gz', 'gy'), split_axis=3, concat_axis=2, tiled=...  187 us
    dot_general x2, matrix products, mode_products(): lax.dot_general(left, right, ((others, others), ((), ())), precision=lax....  134 us
    unnamed x7, local copies, waits for them, and re-layouts  93.8 us
    another operation x24, other arithmetic, solve_factor(): factor = jnp.linalg.cholesky(inner_gram)  52.2 us
  transfers between devices with their start and end apart: 2, of which 2 were waited for; matrix products, arithmetic and copies ran while one was open for 0% of the time, Pallas kernels for 0%

commit v1 on v0

v1 whole, which is shorter than its diff:
```python
import functools
import math

import jax
import jax.numpy as jnp
from jax import lax
from jax.experimental import pallas as pl
from jax.experimental.pallas import tpu as pltpu
from jax.sharding import PartitionSpec as P

RANK = 64
ITERS = 4
CORES = 2
AXES = ("gz", "gy")
DEPTH = 6
MIB = 1 << 20
F32 = jnp.float32
BF16 = jnp.bfloat16


def start_table(order, width):
    row_index = jnp.arange(order).astype(jnp.float32)
    col_index = jnp.arange(width).astype(jnp.float32)
    return jnp.cos(math.pi * (row_index[:, None] + 0.5) * col_index[None, :] / order)


def tie(value, other):
    return lax.optimization_barrier((value, other))[0]


def split_bf16(value):
    high = value.astype(BF16)
    low = (value - high.astype(F32)).astype(BF16)
    return high, low


def dot_nn(left, right):
    return lax.dot_general(left, right, (((1,), (0,)), ((), ())), preferred_element_type=F32)


def dot_nt(left, right):
    return lax.dot_general(left, right, (((1,), (1,)), ((), ())), preferred_element_type=F32)


def dot_tn(left, right):
    return lax.dot_general(left, right, (((0,), (0,)), ((), ())), preferred_element_type=F32)


def pack_kernel(groups, width, me_ref, field_ref, *out_refs):
    turned = out_refs[-1]
    me = me_ref[0]
    for z in range(field_ref.shape[1]):
        turned[...] = field_ref[0, z].T
        for k in range(groups):
            start = pl.multiple_of((me ^ k) * width, width)
            out_refs[k][:, z, :] = turned[pl.ds(start, width), :]


def pack(field, me, species, groups):
    _, z_n, y_n, x_n = field.shape
    width = x_n // groups
    z_tile = 8
    return pl.pallas_call(
        functools.partial(pack_kernel, groups, width),
        grid_spec=pltpu.PrefetchScalarGridSpec(
            num_scalar_prefetch=1,
            grid=(z_n // z_tile,),
            in_specs=[pl.BlockSpec((1, z_tile, y_n, x_n), lambda i, m: (species, i, 0, 0))],
            out_specs=[pl.BlockSpec((width, z_tile, y_n), lambda i, m: (0, i, 0))] * groups,
            scratch_shapes=[pltpu.VMEM((x_n, y_n), F32)],
        ),
        out_shape=[jax.ShapeDtypeStruct((width, z_n, y_n), F32)] * groups,
        compiler_params=pltpu.CompilerParams(vmem_limit_bytes=24 * MIB),
        cost_estimate=pl.CostEstimate(
            flops=0, bytes_accessed=4 * 8 * z_n * y_n * x_n, transcendentals=0),
        name="pack",
    )(me, field)


def gram_z_kernel(groups, side, me_ref, prev_ref, *refs):
    pieces, out_ref, (high, low, sum_hh, sum_hl) = refs[:groups], refs[groups], refs[groups + 1:]
    step = pl.program_id(0)
    me_z = me_ref[0] // side
    x_tile, z_n, y_n = pieces[0].shape

    @pl.when(step == 0)
    def _():
        sum_hh[...] = jnp.zeros_like(sum_hh)
        sum_hl[...] = jnp.zeros_like(sum_hl)

    for k in range(groups):
        row = pl.multiple_of((me_z ^ (k // side)) * z_n, z_n)
        for x in range(x_tile):
            col = (x * side + k % side) * y_n
            high_part, low_part = split_bf16(pieces[k][x])
            high[pl.ds(row, z_n), col:col + y_n] = high_part
            low[pl.ds(row, z_n), col:col + y_n] = low_part
    sum_hh[...] += dot_nt(high[...], high[...])
    sum_hl[...] += dot_nt(high[...], low[...])

    @pl.when(step == pl.num_programs(0) - 1)
    def _():
        cross = sum_hl[...]
        out_ref[...] = prev_ref[...] + (sum_hh[...] + (cross + cross.T))


def gram_z_step(prev, pieces, me, side):
    groups = len(pieces)
    width, z_n, y_n = pieces[0].shape
    order = z_n * (groups // side)
    x_tile = 4
    depth = x_tile * side * y_n
    whole = pl.BlockSpec((order, order), lambda i, m: (0, 0))
    return pl.pallas_call(
        functools.partial(gram_z_kernel, groups, side),
        grid_spec=pltpu.PrefetchScalarGridSpec(
            num_scalar_prefetch=1,
            grid=(width // x_tile,),
            in_specs=[whole] + [pl.BlockSpec((x_tile, z_n, y_n), lambda i, m: (i, 0, 0))] * groups,
            out_specs=whole,
            scratch_shapes=[pltpu.VMEM((order, depth), BF16), pltpu.VMEM((order, depth), BF16),
                            pltpu.VMEM((order, order), F32), pltpu.VMEM((order, order), F32)],
        ),
        out_shape=jax.ShapeDtypeStruct((order, order), F32),
        compiler_params=pltpu.CompilerParams(vmem_limit_bytes=32 * MIB),
        cost_estimate=pl.CostEstimate(
            flops=4 * order * order * width * side * y_n,
            bytes_accessed=4 * groups * width * z_n * y_n, transcendentals=0),
        name="gram_z",
    )(me, prev, *pieces)


def basis_kernel(gz_n, me_ref, gram_ref, start_ref, basis_ref, turned_ref):
    rank, order = start_ref.shape
    highest = dict(precision=lax.Precision.HIGHEST, preferred_element_type=F32)
    row_id = lax.broadcasted_iota(jnp.int32, (rank, 1), 0)
    lane_id = lax.broadcasted_iota(jnp.int32, (rank, rank), 1)
    row_ids = lax.broadcasted_iota(jnp.int32, (rank, rank), 0)
    eye = jnp.where(lane_id == row_ids, 1.0, 0.0).astype(F32)

    def iterate(_, basis_t):
        product = lax.dot_general(basis_t, gram_ref[...], (((1,), (0,)), ((), ())), **highest)
        inner = lax.dot_general(product, product, (((1,), (1,)), ((), ())), **highest)
        work = jnp.concatenate([inner, eye], axis=1)
        for k in range(rank - 1):
            row = work[k:k + 1, :]
            scaled = row / work[k:k + 1, k:k + 1]
            factor = jnp.where(row_id > k, work[:, k:k + 1], 0.0)
            work = work - factor * scaled
        pivots = jnp.sum(jnp.where(lane_id == row_ids, work[:, :rank], 0.0), axis=1, keepdims=True)
        inverse = work[:, rank:] * (1.0 / jnp.sqrt(pivots))
        return lax.dot_general(inverse, product, (((1,), (0,)), ((), ())), **highest)

    basis_t = lax.fori_loop(0, ITERS, iterate, start_ref[...])
    basis_ref[...] = basis_t
    if gz_n > 1:
        me_z = me_ref[0]
        size = order // gz_n
        while size < order:
            parts = [basis_t[:, i:i + size] for i in range(0, order, size)]
            swapped = jnp.concatenate([parts[i ^ 1] for i in range(len(parts))], axis=1)
            bit = (me_z // (size // (order // gz_n))) % 2
            basis_t = jnp.where(bit == 1, swapped, basis_t)
            size *= 2
    turned_ref[...] = basis_t


def leaf_basis(gram, start_t, me_z, gz_n):
    rank, order = start_t.shape
    vmem = pl.BlockSpec(memory_space=pltpu.VMEM)
    return pl.pallas_call(
        functools.partial(basis_kernel, gz_n),
        in_specs=[pl.BlockSpec(memory_space=pltpu.SMEM), vmem, vmem],
        out_specs=[vmem, vmem],
        out_shape=[jax.ShapeDtypeStruct((rank, order), F32)] * 2,
        compiler_params=pltpu.CompilerParams(vmem_limit_bytes=24 * MIB),
        name="leaf_basis",
    )(me_z, gram, start_t)


def reduce_kernel(groups, side, pos_ref, basis_ref, *refs):
    pieces, out_ref = refs[:groups], refs[groups]
    rank = basis_ref.shape[0]
    me_x = pos_ref[1]
    x_tile, z_n, y_n = pieces[0].shape
    high, low = split_bf16(basis_ref[...])
    both = jnp.concatenate([high, low], axis=0)
    for x in range(x_tile):
        cols = [jnp.concatenate([pieces[k][x] for k in range(j, groups, side)], axis=0)
                for j in range(side)]
        field_high, field_low = split_bf16(jnp.concatenate(cols, axis=1))
        first = dot_nn(both, field_high)
        total = first[:rank] + (first[rank:] + dot_nn(high, field_low))
        for j in range(side):
            start = pl.multiple_of((me_x ^ j) * y_n, y_n)
            out_ref[x, :, pl.ds(start, y_n)] = total[:, j * y_n:(j + 1) * y_n]


def reduce_half(basis_t, pieces, pos, side):
    groups = len(pieces)
    width, z_n, y_n = pieces[0].shape
    half = width // CORES
    x_tile = 4
    rank, order = basis_t.shape
    tiles = half // x_tile
    return pl.pallas_call(
        functools.partial(reduce_kernel, groups, side),
        grid_spec=pltpu.PrefetchScalarGridSpec(
            num_scalar_prefetch=1,
            grid=(tiles,),
            in_specs=[pl.BlockSpec((rank, order), lambda i, p: (0, 0))]
            + [pl.BlockSpec((x_tile, z_n, y_n), lambda i, p: (p[0] * tiles + i, 0, 0))] * groups,
            out_specs=pl.BlockSpec((x_tile, rank, side * y_n), lambda i, p: (i, 0, 0)),
        ),
        out_shape=jax.ShapeDtypeStruct((half, rank, side * y_n), F32),
        compiler_params=pltpu.CompilerParams(vmem_limit_bytes=24 * MIB),
        cost_estimate=pl.CostEstimate(
            flops=6 * rank * order * half * side * y_n,
            bytes_accessed=4 * groups * half * z_n * y_n, transcendentals=0),
        name="reduce_z",
    )(pos, basis_t, *pieces)


def gram_y_kernel(species, side, core_ref, *refs):
    mine, others = refs[:species], refs[species:2 * species]
    full_ref, gram_ref, sum_hh, sum_hl = refs[2 * species:]
    step = pl.program_id(0)
    core = core_ref[0]
    x_tile, rank, two = mine[0].shape
    y_n = two // side

    @pl.when(step == 0)
    def _():
        sum_hh[...] = jnp.zeros_like(sum_hh)
        sum_hl[...] = jnp.zeros_like(sum_hl)

    for s in range(species):
        for j in range(side):
            for ref, place in ((mine[s], core), (others[s], 1 - core)):
                start = pl.multiple_of((j * CORES + place) * y_n, y_n)
                full_ref[s, :, :, pl.ds(start, y_n)] = ref[:, :, j * y_n:(j + 1) * y_n]
    order = full_ref.shape[-1]
    high, low = split_bf16(full_ref[...].reshape(species * x_tile * rank, order))
    sum_hh[...] += dot_tn(high, high)
    sum_hl[...] += dot_tn(high, low)

    @pl.when(step == pl.num_programs(0) - 1)
    def _():
        cross = sum_hl[...]
        gram_ref[...] = sum_hh[...] + (cross + cross.T)


def gram_y_full(mine, others, core, side):
    species = len(mine)
    half, rank, two = mine[0].shape
    order = two * CORES
    x_tile = 4
    part = pl.BlockSpec((x_tile, rank, two), lambda i, c: (i, 0, 0))
    return pl.pallas_call(
        functools.partial(gram_y_kernel, species, side),
        grid_spec=pltpu.PrefetchScalarGridSpec(
            num_scalar_prefetch=1,
            grid=(half // x_tile,),
            in_specs=[part] * (2 * species),
            out_specs=[pl.BlockSpec((species, x_tile, rank, order), lambda i, c: (0, i, 0, 0)),
                       pl.BlockSpec((order, order), lambda i, c: (0, 0))],
            scratch_shapes=[pltpu.VMEM((order, order), F32), pltpu.VMEM((order, order), F32)],
        ),
        out_shape=[jax.ShapeDtypeStruct((species, half, rank, order), F32),
                   jax.ShapeDtypeStruct((order, order), F32)],
        compiler_params=pltpu.CompilerParams(vmem_limit_bytes=40 * MIB),
        name="gram_y",
    )(core, *mine, *others)


def core_kernel(basis_ref, full_ref, out_ref):
    species, x_tile, rank, order = full_ref.shape
    high, low = split_bf16(basis_ref[...])
    field_high, field_low = split_bf16(full_ref[...].reshape(species * x_tile * rank, order))
    first = dot_nt(field_high, jnp.concatenate([high, low], axis=0))
    second = dot_nt(field_low, high)
    total = first[:, :rank] + (first[:, rank:] + second)
    out_ref[...] = total.reshape(species, x_tile, rank, rank)


def project_core(basis_t, full):
    species, half, rank, order = full.shape
    x_tile = 4
    return pl.pallas_call(
        core_kernel,
        grid=(half // x_tile,),
        in_specs=[pl.BlockSpec((rank, order), lambda i: (0, 0)),
                  pl.BlockSpec((species, x_tile, rank, order), lambda i: (0, i, 0, 0))],
        out_specs=pl.BlockSpec((species, x_tile, rank, rank), lambda i: (0, i, 0, 0)),
        out_shape=jax.ShapeDtypeStruct((species, half, rank, rank), F32),
        compiler_params=pltpu.CompilerParams(vmem_limit_bytes=24 * MIB),
        name="core",
    )(basis_t, full)


def permute(value, mask, total):
    return lax.ppermute(value, AXES, [(i, i ^ mask) for i in range(total)])


def all_sum(value, me, total, quads):
    low = total // quads
    bits = [1 << b for b in range(low.bit_length() - 1)]
    current = value
    for bit in bits:
        half = current.shape[0] // 2
        upper = (me // bit) % 2 == 1
        first, second = current[:half], current[half:]
        current = jnp.where(upper, second, first) + permute(
            jnp.where(upper, first, second), bit, total)
    place = me // low
    parts = current.reshape(quads, -1, current.shape[1])
    pick = lambda k: lax.dynamic_index_in_dim(parts, place ^ k, 0, False)
    arrived = [permute(pick(k), low * k, total) for k in range(1, quads)]
    sums = pick(0)
    for part in arrived:
        sums = sums + part
    stack = jnp.stack([sums] + [permute(sums, low * k, total) for k in range(1, quads)])
    current = jnp.concatenate(
        [lax.dynamic_index_in_dim(stack, place ^ j, 0, False) for j in range(quads)])
    for bit in reversed(bits):
        other = permute(current, bit, total)
        upper = (me // bit) % 2 == 1
        current = jnp.concatenate(
            [jnp.where(upper, other, current), jnp.where(upper, current, other)])
    return current


def send_order(gz_n, side):
    groups = gz_n * side
    far = [k for k in range(groups // 2, groups)]
    near = [k for k in range(1, groups // 2)]
    far.sort(key=lambda k: (k % (groups // 4), k))
    order = []
    for i, k in enumerate(far):
        order.append(k)
        if i < len(near):
            order.append(near[i])
    return order


def fast_body(field):
    species, _, y_n, x_n = field.shape
    gz_n, gy_n = lax.axis_size("gz"), lax.axis_size("gy")
    total = gz_n * gy_n
    side = gy_n // CORES
    groups = gz_n * side
    grid_n = y_n * gy_n
    gz, gy = lax.axis_index("gz"), lax.axis_index("gy")
    me = gz * gy_n + gy
    core = gy % CORES
    group = (gz * side + gy // CORES).astype(jnp.int32)
    one = lambda v: jnp.reshape(v, (1,)).astype(jnp.int32)
    start_t = start_table(grid_n, RANK).T

    order = send_order(gz_n, side)
    pieces, recent = [], []
    gram = jnp.zeros((grid_n, grid_n), F32)
    source = field
    for s in range(species):
        if s:
            source = tie(source, recent[-len(order) // 2])
        sent = pack(source, one(group), s, groups)
        got = [sent[0]] + [None] * (groups - 1)
        for k in order:
            value = sent[k]
            if len(recent) >= DEPTH:
                value = tie(value, recent[-DEPTH])
            got[k] = permute(value, k * CORES, total)
            recent.append(got[k])
        pieces.append(got)
    for s in range(species):
        gram = gram_z_step(gram, pieces[s], one(group), side)
    gram = all_sum(gram, me, total, 4)
    basis_z, turned_z = leaf_basis(gram, start_t, one(gz), gz_n)

    side_pos = gy // CORES
    away = jnp.stack([1 - core, side_pos]).astype(jnp.int32)
    home = jnp.stack([core, side_pos]).astype(jnp.int32)
    leaving = [reduce_half(turned_z, pieces[s], away, side) for s in range(species)]
    others = [permute(value, 1, total) for value in leaving]
    mine = [reduce_half(turned_z, pieces[s], home, side) for s in range(species)]
    full, gram = gram_y_full(mine, others, one(core), side)
    gram = all_sum(gram, me, total, 4)
    basis_y, _ = leaf_basis(gram, start_t, one(gz), 1)
    core_tensor = project_core(basis_y, full)
    core_tensor = core_tensor.reshape(species, x_n // total, RANK * RANK)
    return core_tensor, basis_z.T, basis_y.T


def plain_basis(fibres, mode):
    highest = lax.Precision.HIGHEST
    others = tuple(d for d in range(4) if d != mode)
    gram = lax.dot_general(fibres, fibres, ((others, others), ((), ())), precision=highest)
    gram = lax.psum(gram, AXES)
    basis = start_table(gram.shape[0], RANK)
    for _ in range(ITERS):
        product = jnp.dot(gram, basis, precision=highest)
        inner = lax.dot_general(product, product, (((0,), (0,)), ((), ())), precision=highest)
        basis = lax.linalg.triangular_solve(
            jnp.linalg.cholesky(inner), product, left_side=False, lower=True, transpose_a=True)
    return basis


def plain_body(field):
    highest = lax.Precision.HIGHEST
    gz_n, gy_n = lax.axis_size("gz"), lax.axis_size("gy")
    fibres = lax.all_to_all(field, "gz", split_axis=2, concat_axis=1, tiled=True)
    basis_z = plain_basis(fibres, 1)
    reduced = jnp.einsum("szyx,zr->sryx", fibres, basis_z, precision=highest)
    mixed = lax.all_to_all(reduced, AXES, split_axis=3, concat_axis=2, tiled=True)
    shape = mixed.shape
    blocks = mixed.reshape(shape[0], shape[1], gz_n, gy_n, shape[2] // (gz_n * gy_n), shape[3])
    fibres = jnp.transpose(blocks, (0, 1, 3, 2, 4, 5)).reshape(shape)
    basis_y = plain_basis(fibres, 2)
    core_tensor = jnp.einsum("sryx,yq->sxrq", fibres, basis_y, precision=highest)
    return core_tensor.reshape(shape[0], shape[3], RANK * RANK), basis_z, basis_y


def body(field):
    gz_n, gy_n = lax.axis_size("gz"), lax.axis_size("gy")
    _, z_n, y_n, x_n = field.shape
    groups = gz_n * gy_n // CORES
    aligned = y_n % 128 == 0 and z_n % 64 == 0 and x_n % (8 * CORES * groups) == 0
    powers = gz_n % 4 == 0 and gz_n & (gz_n - 1) == 0 and gy_n >= 4 and gy_n & (gy_n - 1) == 0
    return fast_body(field) if aligned and powers else plain_body(field)


def solution(mesh):
    in_specs = (P(None, "gz", "gy", None),)
    out_specs = (P(None, AXES, None), P(), P())
    return jax.shard_map(body, mesh=mesh, in_specs=in_specs, out_specs=out_specs, check_vma=False)
```

time: 2460 us -> 1830 us (0.74)
  blocking collectives: 1650 us -> 0 us
  starting transfers between devices: 0.29 us -> 761 us
  waiting for transfers between devices: 258 us -> 729 us
  Pallas kernels: 0 us -> 225 us
  matrix products: 223 us -> 0 us
  other arithmetic: 122 us -> 7.55 us
  local copies, waits for them, and re-layouts: 187 us -> 97.6 us
    all_to_all x2 -> x0, blocking collectives: 1650 us -> none  [the longest x1 1460 us: body(): lax.all_to_all(species_field, 'gz', split_axis=2, concat_axis=1, tiled=True)]
    ppermute x0 -> x88, starting transfers between devices: none -> 761 us  [permute(): return lax.ppermute(value, AXES, [(i, i ^ mask) for i in range(total)])]
    ppermute x0 -> x88, waiting for transfers between devices: none -> 729 us  [permute(): return lax.ppermute(value, AXES, [(i, i ^ mask) for i in range(total)])]
    psum x2 -> x0, waiting for transfers between devices: 258 us -> none  [leaf_basis(): gram_total = lax.psum(mode_products(fibres, fibres, mode), ('gz', 'gy'))]
    pallas_call x0 -> x20, Pallas kernels: none -> 225 us  [the longest x4 62.9 us: pack(): pl.pallas_call(functools.partial(pack_kernel, groups, width), grid_spec=p...]
    dot_general x20 -> x0, matrix products: 221 us -> none  [the longest x2 134 us: mode_products(): lax.dot_general(left, right, ((others, others), ((), ())), precision=lax....]
    another operation x40 -> x4, other arithmetic: 97.1 us -> 0.17 us  [the longest x1 0.08 us: fast_body(): away = jnp.stack([1 - core, side_pos]).astype(jnp.int32)]
    all_to_all x2 -> x0, local copies, waits for them, and re-layouts: 44.3 us -> none  [the longest x1 43.8 us: body(): lax.all_to_all(species_field, 'gz', split_axis=2, concat_axis=1, tiled=True)]
  transfers between devices with their start and end apart: 2 -> 88, of which waited for: 2 -> 43; matrix products, arithmetic and copies ran while one was open for 0% -> 0% of each run, Pallas kernels for 0% -> 7%
where the time goes in v1:
time: 1830 us; the launch traced here: 1820 us
  starting transfers between devices  761 us (42%)
  waiting for transfers between devices  729 us (40%)
  Pallas kernels  225 us (12%)
  local copies, waits for them, and re-layouts  97.6 us (5%)
    ppermute x88, starting transfers between devices, permute(): return lax.ppermute(value, AXES, [(i, i ^ mask) for i in range(total)])  761 us
    ppermute x88, waiting for transfers between devices, permute(): return lax.ppermute(value, AXES, [(i, i ^ mask) for i in range(total)])  729 us
    unnamed x402, local copies, waits for them, and re-layouts  95.8 us
    pallas_call x4, Pallas kernels, pack(): pl.pallas_call(functools.partial(pack_kernel, groups, width), grid_spec=p...  62.9 us
    pallas_call x4, Pallas kernels, gram_z_step(): pl.pallas_call(functools.partial(gram_z_kernel, groups, side), grid_spec=...  56.7 us
    pallas_call x2, Pallas kernels, leaf_basis(): pl.pallas_call(functools.partial(basis_kernel, gz_n), in_specs=[pl.BlockS...  55.7 us
  transfers between devices with their start and end apart: 88, of which 43 were waited for; matrix products, arithmetic and copies ran while one was open for 0% of the time, Pallas kernels for 7%

profile of v1, /device:TPU:0, one launch (start us, length us, event | category | flops | bytes accessed | tf_op | source)
XLA Modules:
  0.0 1823.3 jit_solution(4919440272946208594)
XLA Ops:
  0.6 15.3 pack.4
  24.9 18.0 collective-permute-done.refs_1_
  46.1 19.8 %collective-permute-done.2.refs_3_ = f32[32,64,128]{2,1,0:T(8,128)S(1)} collective-permute-done((f32[32,64,128]{2,1,0:T(8,128)S(1)}, f32[32,64,128]{2,1,0:T(8,128)S(1)}, u32[]{:S(2)}, u32[]{:S(2)}) %collective-permute-start.2) | collective-permute-done | bytes 1048608 | tf_op jit(solution)/shard_map/ppermute | solution.py:302
  65.9 24.0 %collective-permute-start.3 = (f32[32,64,128]{2,1,0:T(8,128)S(1)}, f32[32,64,128]{2,1,0:T(8,128)S(1)}, u32[]{:S(2)}, u32[]{:S(2)}) collective-permute-start(f32[32,64,128]{2,1,0:T(8,128)S(1)} %get-tuple-element.134), channel_id=1, source_target_pairs={{0,8},{1,9},{2,10},{3,11},{4,12},{5,13},{6,14},{7,15},{8,0},{9,1},... | collective-permute-start | bytes 3145736 | tf_op jit(solution)/shard_map/ppermute | solution.py:302
  91.8 25.2 %collective-permute-start.4 = (f32[32,64,128]{2,1,0:T(8,128)S(1)}, f32[32,64,128]{2,1,0:T(8,128)S(1)}, u32[]{:S(2)}, u32[]{:S(2)}) collective-permute-start(f32[32,64,128]{2,1,0:T(8,128)S(1)} %get-tuple-element.136), channel_id=1, source_target_pairs={{0,10},{1,11},{2,8},{3,9},{4,14},{5,15},{6,12},{7,13},{8,2},{9,3},... | collective-permute-start | bytes 3145736 | tf_op jit(solution)/shard_map/ppermute | solution.py:302
  117.0 20.9 %collective-permute-done.8.refs_9_ = f32[32,64,128]{2,1,0:T(8,128)S(1)} collective-permute-done((f32[32,64,128]{2,1,0:T(8,128)S(1)}, f32[32,64,128]{2,1,0:T(8,128)S(1)}, u32[]{:S(2)}, u32[]{:S(2)}) %collective-permute-start.8) | collective-permute-done | bytes 1048608 | tf_op jit(solution)/shard_map/ppermute | solution.py:302
  138.9 65.5 %collective-permute-done.7.refs_8_ = f32[32,64,128]{2,1,0:T(8,128)S(1)} collective-permute-done((f32[32,64,128]{2,1,0:T(8,128)S(1)}, f32[32,64,128]{2,1,0:T(8,128)S(1)}, u32[]{:S(2)}, u32[]{:S(2)}) %collective-permute-start.7) | collective-permute-done | bytes 1048608 | tf_op jit(solution)/shard_map/ppermute | solution.py:302
  206.4 20.8 %collective-permute-start.11 = (f32[32,64,128]{2,1,0:T(8,128)S(1)}, f32[32,64,128]{2,1,0:T(8,128)S(1)}, u32[]{:S(2)}, u32[]{:S(2)}) collective-permute-start(f32[32,64,128]{2,1,0:T(8,128)S(1)} %get-tuple-element.148), channel_id=1, source_target_pairs={{0,26},{1,27},{2,24},{3,25},{4,30},{5,31},{6,28},{7,29},{8,18},{9,... | collective-permute-start | bytes 3145736 | tf_op jit(solution)/shard_map/ppermute | solution.py:302
  228.2 15.6 pack.5
  244.8 27.3 %collective-permute-done.4.refs_5_ = f32[32,64,128]{2,1,0:T(8,128)S(1)} collective-permute-done((f32[32,64,128]{2,1,0:T(8,128)S(1)}, f32[32,64,128]{2,1,0:T(8,128)S(1)}, u32[]{:S(2)}, u32[]{:S(2)}) %collective-permute-start.4) | collective-permute-done | bytes 1048608 | tf_op jit(solution)/shard_map/ppermute | solution.py:302
  277.4 39.5 %collective-permute-done.6.refs_7_ = f32[32,64,128]{2,1,0:T(8,128)S(1)} collective-permute-done((f32[32,64,128]{2,1,0:T(8,128)S(1)}, f32[32,64,128]{2,1,0:T(8,128)S(1)}, u32[]{:S(2)}, u32[]{:S(2)}) %collective-permute-start.6) | collective-permute-done | bytes 1048608 | tf_op jit(solution)/shard_map/ppermute | solution.py:302
  317.0 61.1 %collective-permute-start.12 = (f32[32,64,128]{2,1,0:T(8,128)S(1)}, f32[32,64,128]{2,1,0:T(8,128)S(1)}, u32[]{:S(2)}, u32[]{:S(2)}) collective-permute-start(f32[32,64,128]{2,1,0:T(8,128)S(1)} %get-tuple-element.149), channel_id=1, source_target_pairs={{0,22},{1,23},{2,20},{3,21},{4,18},{5,19},{6,16},{7,17},{8,30},{9,... | collective-permute-start | bytes 3145736 | tf_op jit(solution)/shard_map/ppermute | solution.py:302
  378.1 32.3 %collective-permute-start.23 = (f32[32,64,128]{2,1,0:T(8,128)S(1)}, f32[32,64,128]{2,1,0:T(8,128)S(1)}, u32[]{:S(2)}, u32[]{:S(2)}) collective-permute-start(f32[32,64,128]{2,1,0:T(8,128)S(1)} %get-tuple-element.173), channel_id=1, source_target_pairs={{0,18},{1,19},{2,16},{3,17},{4,22},{5,23},{6,20},{7,21},{8,26},{9,... | collective-permute-start | bytes 3145736 | tf_op jit(solution)/shard_map/ppermute | solution.py:302
  410.4 44.2 %collective-permute-done.22.refs_8_ = f32[32,64,128]{2,1,0:T(8,128)S(1)} collective-permute-done((f32[32,64,128]{2,1,0:T(8,128)S(1)}, f32[32,64,128]{2,1,0:T(8,128)S(1)}, u32[]{:S(2)}, u32[]{:S(2)}) %collective-permute-start.22) | collective-permute-done | bytes 1048608 | tf_op jit(solution)/shard_map/ppermute | solution.py:302
  454.5 7.9 collective-permute-start.25
  462.5 38.2 %collective-permute-start.26 = (f32[32,64,128]{2,1,0:T(8,128)S(1)}, f32[32,64,128]{2,1,0:T(8,128)S(1)}, u32[]{:S(2)}, u32[]{:S(2)}) collective-permute-start(f32[32,64,128]{2,1,0:T(8,128)S(1)} %get-tuple-element.180), channel_id=1, source_target_pairs={{0,26},{1,27},{2,24},{3,25},{4,30},{5,31},{6,28},{7,29},{8,18},{9,... | collective-permute-start | bytes 3145736 | tf_op jit(solution)/shard_map/ppermute | solution.py:302
  501.7 51.6 %collective-permute-done.12.refs_11_ = f32[32,64,128]{2,1,0:T(8,128)S(1)} collective-permute-done((f32[32,64,128]{2,1,0:T(8,128)S(1)}, f32[32,64,128]{2,1,0:T(8,128)S(1)}, u32[]{:S(2)}, u32[]{:S(2)}) %collective-permute-start.12) | collective-permute-done | bytes 1048608 | tf_op jit(solution)/shard_map/ppermute | solution.py:302
  553.4 14.9 collective-permute-done.23.refs_9_
  568.2 8.1 collective-permute-start.16
  576.4 21.5 %collective-permute-done.25.refs_10_ = f32[32,64,128]{2,1,0:T(8,128)S(1)} collective-permute-done((f32[32,64,128]{2,1,0:T(8,128)S(1)}, f32[32,64,128]{2,1,0:T(8,128)S(1)}, u32[]{:S(2)}, u32[]{:S(2)}) %collective-permute-start.25) | collective-permute-done | bytes 1048608 | tf_op jit(solution)/shard_map/ppermute | solution.py:302
  603.0 65.8 %collective-permute-start.27 = (f32[32,64,128]{2,1,0:T(8,128)}, f32[32,64,128]{2,1,0:T(8,128)S(1)}, u32[]{:S(2)}, u32[]{:S(2)}) collective-permute-start(f32[32,64,128]{2,1,0:T(8,128)} %get-tuple-element.181), channel_id=1, source_target_pairs={{0,22},{1,23},{2,20},{3,21},{4,18},{5,19},{6,16},{7,17},{8,30},{9,... | collective-permute-start | bytes 3145736 | tf_op jit(solution)/shard_map/ppermute | solution.py:302
  672.8 56.1 %collective-permute-start.19 = (f32[32,64,128]{2,1,0:T(8,128)}, f32[32,64,128]{2,1,0:T(8,128)}, u32[]{:S(2)}, u32[]{:S(2)}) collective-permute-start(f32[32,64,128]{2,1,0:T(8,128)} %get-tuple-element.165), channel_id=1, source_target_pairs={{0,10},{1,11},{2,8},{3,9},{4,14},{5,15},{6,12},{7,13},{8,2},{9,3},... | collective-permute-start | bytes 3145736 | tf_op jit(solution)/shard_map/ppermute | solution.py:302
  728.9 15.6 pack.6
  748.6 14.6 collective-permute-start.30
  763.1 28.1 %collective-permute-done.27.refs_11_ = f32[32,64,128]{2,1,0:T(8,128)S(1)} collective-permute-done((f32[32,64,128]{2,1,0:T(8,128)}, f32[32,64,128]{2,1,0:T(8,128)S(1)}, u32[]{:S(2)}, u32[]{:S(2)}) %collective-permute-start.27) | collective-permute-done | bytes 1048608 | tf_op jit(solution)/shard_map/ppermute | solution.py:302
  795.6 5.4 collective-permute-start.39
  801.0 12.5 collective-permute-start.38
  814.5 39.9 %collective-permute-start.37 = (f32[32,64,128]{2,1,0:T(8,128)S(1)}, f32[32,64,128]{2,1,0:T(8,128)S(1)}, u32[]{:S(2)}, u32[]{:S(2)}) collective-permute-start(f32[32,64,128]{2,1,0:T(8,128)S(1)} %get-tuple-element.203), channel_id=1, source_target_pairs={{0,16},{1,17},{2,18},{3,19},{4,20},{5,21},{6,22},{7,23},{8,24},{9,... | collective-permute-start | bytes 3145736 | tf_op jit(solution)/shard_map/ppermute | solution.py:302
  855.3 12.7 collective-permute-start.33
  870.0 21.2 %collective-permute-start.34 = (f32[32,64,128]{2,1,0:T(8,128)}, f32[32,64,128]{2,1,0:T(8,128)S(1)}, u32[]{:S(2)}, u32[]{:S(2)}) collective-permute-start(f32[32,64,128]{2,1,0:T(8,128)} %get-tuple-element.197), channel_id=1, source_target_pairs={{0,10},{1,11},{2,8},{3,9},{4,14},{5,15},{6,12},{7,13},{8,2},{9,3},... | collective-permute-start | bytes 3145736 | tf_op jit(solution)/shard_map/ppermute | solution.py:302
  891.3 21.0 %collective-permute-done.38.refs_9_ = f32[32,64,128]{2,1,0:T(8,128)S(1)} collective-permute-done((f32[32,64,128]{2,1,0:T(8,128)S(1)}, f32[32,64,128]{2,1,0:T(8,128)S(1)}, u32[]{:S(2)}, u32[]{:S(2)}) %collective-permute-start.38) | collective-permute-done | bytes 1048608 | tf_op jit(solution)/shard_map/ppermute | solution.py:302
  913.2 21.1 %collective-permute-done.37.refs_8_ = f32[32,64,128]{2,1,0:T(8,128)S(1)} collective-permute-done((f32[32,64,128]{2,1,0:T(8,128)S(1)}, f32[32,64,128]{2,1,0:T(8,128)S(1)}, u32[]{:S(2)}, u32[]{:S(2)}) %collective-permute-start.37) | collective-permute-done | bytes 1048608 | tf_op jit(solution)/shard_map/ppermute | solution.py:302
  936.7 15.5 collective-permute-done.33.refs_4_
  953.1 16.5 pack.7
  970.6 55.6 %collective-permute-done.35.refs_6_ = f32[32,64,128]{2,1,0:T(8,128)S(1)} collective-permute-done((f32[32,64,128]{2,1,0:T(8,128)}, f32[32,64,128]{2,1,0:T(8,128)S(1)}, u32[]{:S(2)}, u32[]{:S(2)}) %collective-permute-start.35) | collective-permute-done | bytes 1048608 | tf_op jit(solution)/shard_map/ppermute | solution.py:302
  1031.3 18.7 %collective-permute-done.34.refs_5_ = f32[32,64,128]{2,1,0:T(8,128)S(1)} collective-permute-done((f32[32,64,128]{2,1,0:T(8,128)}, f32[32,64,128]{2,1,0:T(8,128)S(1)}, u32[]{:S(2)}, u32[]{:S(2)}) %collective-permute-start.34) | collective-permute-done | bytes 1048608 | tf_op jit(solution)/shard_map/ppermute | solution.py:302
  1051.0 19.7 %collective-permute-start.36 = (f32[32,64,128]{2,1,0:T(8,128)S(1)}, f32[32,64,128]{2,1,0:T(8,128)S(1)}, u32[]{:S(2)}, u32[]{:S(2)}) collective-permute-start(f32[32,64,128]{2,1,0:T(8,128)S(1)} %copy-done.193), channel_id=1, source_target_pairs={{0,14},{1,15},{2,12},{3,13},{4,10},{5,11},{6,8},{7,9},{8,6},{9,7},... | collective-permute-start | bytes 3145736 | tf_op jit(solution)/shard_map/ppermute | solution.py:302
  1071.7 9.7 collective-permute-start.52
  1086.7 9.0 collective-permute-start.42
  1099.3 110.1 %collective-permute-start.55 = (f32[32,64,128]{2,1,0:T(8,128)S(1)}, f32[32,64,128]{2,1,0:T(8,128)S(1)}, u32[]{:S(2)}, u32[]{:S(2)}) collective-permute-start(f32[32,64,128]{2,1,0:T(8,128)S(1)} %get-tuple-element.241), channel_id=1, source_target_pairs={{0,20},{1,21},{2,22},{3,23},{4,16},{5,17},{6,18},{7,19},{8,28},{9,... | collective-permute-start | bytes 3145736 | tf_op jit(solution)/shard_map/ppermute | solution.py:302
  1209.5 39.4 %collective-permute-done.52.refs_8_ = f32[32,64,128]{2,1,0:T(8,128)S(1)} collective-permute-done((f32[32,64,128]{2,1,0:T(8,128)S(1)}, f32[32,64,128]{2,1,0:T(8,128)S(1)}, u32[]{:S(2)}, u32[]{:S(2)}) %collective-permute-start.52) | collective-permute-done | bytes 1048608 | tf_op jit(solution)/shard_map/ppermute | solution.py:302
  1252.5 67.6 %collective-permute-done.42.refs_11_ = f32[32,64,128]{2,1,0:T(8,128)S(1)} collective-permute-done((f32[32,64,128]{2,1,0:T(8,128)S(1)}, f32[32,64,128]{2,1,0:T(8,128)S(1)}, u32[]{:S(2)}, u32[]{:S(2)}) %collective-permute-start.42) | collective-permute-done | bytes 1048608 | tf_op jit(solution)/shard_map/ppermute | solution.py:302
  1326.0 30.7 %collective-permute-done.55.refs_10_ = f32[32,64,128]{2,1,0:T(8,128)S(1)} collective-permute-done((f32[32,64,128]{2,1,0:T(8,128)S(1)}, f32[32,64,128]{2,1,0:T(8,128)S(1)}, u32[]{:S(2)}, u32[]{:S(2)}) %collective-permute-start.55) | collective-permute-done | bytes 1048608 | tf_op jit(solution)/shard_map/ppermute | solution.py:302
  1357.8 15.9 collective-permute-done.53.refs_9_
  1394.6 13.6 gram_z.4.prev_ref
  1410.1 35.0 %collective-permute-start.57 = (f32[32,64,128]{2,1,0:T(8,128)}, f32[32,64,128]{2,1,0:T(8,128)}, u32[]{:S(2)}, u32[]{:S(2)}) collective-permute-start(f32[32,64,128]{2,1,0:T(8,128)} %get-tuple-element.245), channel_id=1, source_target_pairs={{0,22},{1,23},{2,20},{3,21},{4,18},{5,19},{6,16},{7,17},{8,30},{9,... | collective-permute-start | bytes 3145736 | tf_op jit(solution)/shard_map/ppermute | solution.py:302
  1445.2 12.4 collective-permute-start.50
  1457.6 5.2 collective-permute-start.49
  1462.8 42.6 %collective-permute-start.51 = (f32[32,64,128]{2,1,0:T(8,128)}, f32[32,64,128]{2,1,0:T(8,128)}, u32[]{:S(2)}, u32[]{:S(2)}) collective-permute-start(f32[32,64,128]{2,1,0:T(8,128)} %get-tuple-element.233), channel_id=1, source_target_pairs={{0,14},{1,15},{2,12},{3,13},{4,10},{5,11},{6,8},{7,9},{8,6},{9,7},... | collective-permute-start | bytes 3145736 | tf_op jit(solution)/shard_map/ppermute | solution.py:302
  1509.2 14.6 gram_z.5.prev_ref
  1532.3 13.5 gram_z.6.prev_ref
  1545.8 22.9 %collective-permute-done.57.refs_11_ = f32[32,64,128]{2,1,0:T(8,128)} collective-permute-done((f32[32,64,128]{2,1,0:T(8,128)}, f32[32,64,128]{2,1,0:T(8,128)}, u32[]{:S(2)}, u32[]{:S(2)}) %collective-permute-start.57) | collective-permute-done | bytes 1048608 | tf_op jit(solution)/shard_map/ppermute | solution.py:302
  1568.7 15.0 gram_z.7
  1589.0 8.4 collective-permute-done.61
  1624.6 6.4 collective-permute-done.70
  1634.2 27.8 %leaf_basis.2 = (f32[64,512]{1,0:T(8,128)}, f32[64,512]{1,0:T(8,128)S(1)}) custom-call(s32[1]{0:T(128)} %bitcast.me_ref, f32[512,512]{1,0:T(8,128)S(1)} %pad_maximum_fusion.gram_ref, f32[64,512]{1,0:T(8,128)S(1)} %multiply_cosine_fusion.start_ref), custom_call_target="tpu_custom_call" | custom-call | tf_op jit(solution)/shard_map/leaf_basis/pallas_call | solution.py:171
  1683.5 6.7 reduce_z.13
  1694.7 6.0 reduce_z.15
  1701.3 5.6 reduce_z.11.refs_3_
  1725.8 5.3 reduce_z.9.refs_1_
  1734.0 9.7 gram_y.1
  1746.3 8.0 collective-permute-done.77
  1780.3 6.0 collective-permute-done.86
  1788.6 27.9 %leaf_basis.3 = (f32[64,512]{1,0:T(8,128)}, f32[64,512]{1,0:T(8,128)}) custom-call(s32[1]{0:T(128)} %bitcast.me_ref, f32[512,512]{1,0:T(8,128)S(1)} %pad_maximum_fusion.1.gram_ref, f32[64,512]{1,0:T(8,128)S(1)} %multiply_cosine_fusion.start_ref), custom_call_target="tpu_custom_call" | custom-call | tf_op jit(solution)/shard_map/leaf_basis/pallas_call | solution.py:171
  (576 shorter events, 233.6 us)
Async XLA Ops:
  15.9 27.0 %collective-permute-start = (f32[32,64,128]{2,1,0:T(8,128)S(1)}, f32[32,64,128]{2,1,0:T(8,128)S(1)}, u32[]{:S(2)}, u32[]{:S(2)}) collective-permute-start(f32[32,64,128]{2,1,0:T(8,128)S(1)} %get-tuple-element.130), channel_id=1, source_target_pairs={{0,2},{1,3},{2,0},{3,1},{4,6},{5,7},{6,4},{7,5},{8,10},{9,11},{10,... | collective-permute-start | bytes 3145736 | tf_op jit(solution)/shard_map/ppermute | solution.py:302
  18.9 46.9 %collective-permute-start.2 = (f32[32,64,128]{2,1,0:T(8,128)S(1)}, f32[32,64,128]{2,1,0:T(8,128)S(1)}, u32[]{:S(2)}, u32[]{:S(2)}) collective-permute-start(f32[32,64,128]{2,1,0:T(8,128)S(1)} %get-tuple-element.132), channel_id=1, source_target_pairs={{0,6},{1,7},{2,4},{3,5},{4,2},{5,3},{6,0},{7,1},{8,14},{9,15},{10,... | collective-permute-start | bytes 3145736 | tf_op jit(solution)/shard_map/ppermute | solution.py:302
  20.4 69.4 %collective-permute-start.1 = (f32[32,64,128]{2,1,0:T(8,128)S(1)}, f32[32,64,128]{2,1,0:T(8,128)S(1)}, u32[]{:S(2)}, u32[]{:S(2)}) collective-permute-start(f32[32,64,128]{2,1,0:T(8,128)S(1)} %get-tuple-element.131), channel_id=1, source_target_pairs={{0,4},{1,5},{2,6},{3,7},{4,0},{5,1},{6,2},{7,3},{8,12},{9,13},{10,... | collective-permute-start | bytes 3145736 | tf_op jit(solution)/shard_map/ppermute | solution.py:302
  20.5 70.4 %collective-permute-start.9 = (f32[32,64,128]{2,1,0:T(8,128)S(1)}, f32[32,64,128]{2,1,0:T(8,128)S(1)}, u32[]{:S(2)}, u32[]{:S(2)}) collective-permute-start(f32[32,64,128]{2,1,0:T(8,128)S(1)} %get-tuple-element.144), channel_id=1, source_target_pairs={{0,24},{1,25},{2,26},{3,27},{4,28},{5,29},{6,30},{7,31},{8,16},{9,... | collective-permute-start | bytes 3145736 | tf_op jit(solution)/shard_map/ppermute | solution.py:302
  24.5 113.4 %collective-permute-start.8 = (f32[32,64,128]{2,1,0:T(8,128)S(1)}, f32[32,64,128]{2,1,0:T(8,128)S(1)}, u32[]{:S(2)}, u32[]{:S(2)}) collective-permute-start(f32[32,64,128]{2,1,0:T(8,128)S(1)} %get-tuple-element.142), channel_id=1, source_target_pairs={{0,18},{1,19},{2,16},{3,17},{4,22},{5,23},{6,20},{7,21},{8,26},{9,... | collective-permute-start | bytes 3145736 | tf_op jit(solution)/shard_map/ppermute | solution.py:302
  42.9 161.5 %collective-permute-start.7 = (f32[32,64,128]{2,1,0:T(8,128)S(1)}, f32[32,64,128]{2,1,0:T(8,128)S(1)}, u32[]{:S(2)}, u32[]{:S(2)}) collective-permute-start(f32[32,64,128]{2,1,0:T(8,128)S(1)} %get-tuple-element.141), channel_id=1, source_target_pairs={{0,16},{1,17},{2,18},{3,19},{4,20},{5,21},{6,22},{7,23},{8,24},{9,... | collective-permute-start | bytes 3145736 | tf_op jit(solution)/shard_map/ppermute | solution.py:302
  65.9 139.6 %collective-permute-start.3 = (f32[32,64,128]{2,1,0:T(8,128)S(1)}, f32[32,64,128]{2,1,0:T(8,128)S(1)}, u32[]{:S(2)}, u32[]{:S(2)}) collective-permute-start(f32[32,64,128]{2,1,0:T(8,128)S(1)} %get-tuple-element.134), channel_id=1, source_target_pairs={{0,8},{1,9},{2,10},{3,11},{4,12},{5,13},{6,14},{7,15},{8,0},{9,1},... | collective-permute-start | bytes 3145736 | tf_op jit(solution)/shard_map/ppermute | solution.py:302
  90.8 136.4 %collective-permute-start.5 = (f32[32,64,128]{2,1,0:T(8,128)S(1)}, f32[32,64,128]{2,1,0:T(8,128)S(1)}, u32[]{:S(2)}, u32[]{:S(2)}) collective-permute-start(f32[32,64,128]{2,1,0:T(8,128)S(1)} %get-tuple-element.138), channel_id=1, source_target_pairs={{0,12},{1,13},{2,14},{3,15},{4,8},{5,9},{6,10},{7,11},{8,4},{9,5},... | collective-permute-start | bytes 3145736 | tf_op jit(solution)/shard_map/ppermute | solution.py:302
  91.8 180.3 %collective-permute-start.4 = (f32[32,64,128]{2,1,0:T(8,128)S(1)}, f32[32,64,128]{2,1,0:T(8,128)S(1)}, u32[]{:S(2)}, u32[]{:S(2)}) collective-permute-start(f32[32,64,128]{2,1,0:T(8,128)S(1)} %get-tuple-element.136), channel_id=1, source_target_pairs={{0,10},{1,11},{2,8},{3,9},{4,14},{5,15},{6,12},{7,13},{8,2},{9,3},... | collective-permute-start | bytes 3145736 | tf_op jit(solution)/shard_map/ppermute | solution.py:302
  138.9 135.7 %collective-permute-start.10 = (f32[32,64,128]{2,1,0:T(8,128)S(1)}, f32[32,64,128]{2,1,0:T(8,128)S(1)}, u32[]{:S(2)}, u32[]{:S(2)}) collective-permute-start(f32[32,64,128]{2,1,0:T(8,128)S(1)} %get-tuple-element.145), channel_id=1, source_target_pairs={{0,20},{1,21},{2,22},{3,23},{4,16},{5,17},{6,18},{7,19},{8,28},{9,... | collective-permute-start | bytes 3145736 | tf_op jit(solution)/shard_map/ppermute | solution.py:302
  205.4 69.3 %collective-permute-start.13 = (f32[32,64,128]{2,1,0:T(8,128)S(1)}, f32[32,64,128]{2,1,0:T(8,128)S(1)}, u32[]{:S(2)}, u32[]{:S(2)}) collective-permute-start(f32[32,64,128]{2,1,0:T(8,128)S(1)} %get-tuple-element.151), channel_id=1, source_target_pairs={{0,28},{1,29},{2,30},{3,31},{4,24},{5,25},{6,26},{7,27},{8,20},{9,... | collective-permute-start | bytes 3145736 | tf_op jit(solution)/shard_map/ppermute | solution.py:302
  206.4 69.5 %collective-permute-start.11 = (f32[32,64,128]{2,1,0:T(8,128)S(1)}, f32[32,64,128]{2,1,0:T(8,128)S(1)}, u32[]{:S(2)}, u32[]{:S(2)}) collective-permute-start(f32[32,64,128]{2,1,0:T(8,128)S(1)} %get-tuple-element.148), channel_id=1, source_target_pairs={{0,26},{1,27},{2,24},{3,25},{4,30},{5,31},{6,28},{7,29},{8,18},{9,... | collective-permute-start | bytes 3145736 | tf_op jit(solution)/shard_map/ppermute | solution.py:302
  228.2 88.8 %collective-permute-start.6 = (f32[32,64,128]{2,1,0:T(8,128)S(1)}, f32[32,64,128]{2,1,0:T(8,128)S(1)}, u32[]{:S(2)}, u32[]{:S(2)}) collective-permute-start(f32[32,64,128]{2,1,0:T(8,128)S(1)} %get-tuple-element.140), channel_id=1, source_target_pairs={{0,14},{1,15},{2,12},{3,13},{4,10},{5,11},{6,8},{7,9},{8,6},{9,7},... | collective-permute-start | bytes 3145736 | tf_op jit(solution)/shard_map/ppermute | solution.py:302
  272.1 106.0 %collective-permute-start.24 = (f32[32,64,128]{2,1,0:T(8,128)S(1)}, f32[32,64,128]{2,1,0:T(8,128)S(1)}, u32[]{:S(2)}, u32[]{:S(2)}) collective-permute-start(f32[32,64,128]{2,1,0:T(8,128)S(1)} %get-tuple-element.176), channel_id=1, source_target_pairs={{0,24},{1,25},{2,26},{3,27},{4,28},{5,29},{6,30},{7,31},{8,16},{9,... | collective-permute-start | bytes 3145736 | tf_op jit(solution)/shard_map/ppermute | solution.py:302
  274.7 179.9 %collective-permute-start.22 = (f32[32,64,128]{2,1,0:T(8,128)S(1)}, f32[32,64,128]{2,1,0:T(8,128)S(1)}, u32[]{:S(2)}, u32[]{:S(2)}) collective-permute-start(f32[32,64,128]{2,1,0:T(8,128)S(1)} %get-tuple-element.171), channel_id=1, source_target_pairs={{0,16},{1,17},{2,18},{3,19},{4,20},{5,21},{6,22},{7,23},{8,24},{9,... | collective-permute-start | bytes 3145736 | tf_op jit(solution)/shard_map/ppermute | solution.py:302
  274.7 187.8 %collective-permute-start.14 = (f32[32,64,128]{2,1,0:T(8,128)S(1)}, f32[32,64,128]{2,1,0:T(8,128)S(1)}, u32[]{:S(2)}, u32[]{:S(2)}) collective-permute-start(f32[32,64,128]{2,1,0:T(8,128)S(1)} %get-tuple-element.153), channel_id=1, source_target_pairs={{0,30},{1,31},{2,28},{3,29},{4,26},{5,27},{6,24},{7,25},{8,22},{9,... | collective-permute-start | bytes 3145736 | tf_op jit(solution)/shard_map/ppermute | solution.py:302
  276.0 224.7 %collective-permute-start.15 = (f32[32,64,128]{2,1,0:T(8,128)S(1)}, f32[32,64,128]{2,1,0:T(8,128)S(1)}, u32[]{:S(2)}, u32[]{:S(2)}) collective-permute-start(f32[32,64,128]{2,1,0:T(8,128)S(1)} %get-tuple-element.157), channel_id=1, source_target_pairs={{0,2},{1,3},{2,0},{3,1},{4,6},{5,7},{6,4},{7,5},{8,10},{9,11},{10,... | collective-permute-start | bytes 3145736 | tf_op jit(solution)/shard_map/ppermute | solution.py:302
  317.0 236.4 %collective-permute-start.12 = (f32[32,64,128]{2,1,0:T(8,128)S(1)}, f32[32,64,128]{2,1,0:T(8,128)S(1)}, u32[]{:S(2)}, u32[]{:S(2)}) collective-permute-start(f32[32,64,128]{2,1,0:T(8,128)S(1)} %get-tuple-element.149), channel_id=1, source_target_pairs={{0,22},{1,23},{2,20},{3,21},{4,18},{5,19},{6,16},{7,17},{8,30},{9,... | collective-permute-start | bytes 3145736 | tf_op jit(solution)/shard_map/ppermute | solution.py:302
  378.1 190.1 %collective-permute-start.23 = (f32[32,64,128]{2,1,0:T(8,128)S(1)}, f32[32,64,128]{2,1,0:T(8,128)S(1)}, u32[]{:S(2)}, u32[]{:S(2)}) collective-permute-start(f32[32,64,128]{2,1,0:T(8,128)S(1)} %get-tuple-element.173), channel_id=1, source_target_pairs={{0,18},{1,19},{2,16},{3,17},{4,22},{5,23},{6,20},{7,21},{8,26},{9,... | collective-permute-start | bytes 3145736 | tf_op jit(solution)/shard_map/ppermute | solution.py:302
  454.5 143.3 %collective-permute-start.25 = (f32[32,64,128]{2,1,0:T(8,128)S(1)}, f32[32,64,128]{2,1,0:T(8,128)S(1)}, u32[]{:S(2)}, u32[]{:S(2)}) collective-permute-start(f32[32,64,128]{2,1,0:T(8,128)S(1)} %get-tuple-element.177), channel_id=1, source_target_pairs={{0,20},{1,21},{2,22},{3,23},{4,16},{5,17},{6,18},{7,19},{8,28},{9,... | collective-permute-start | bytes 3145736 | tf_op jit(solution)/shard_map/ppermute | solution.py:302
  462.5 139.0 %collective-permute-start.26 = (f32[32,64,128]{2,1,0:T(8,128)S(1)}, f32[32,64,128]{2,1,0:T(8,128)S(1)}, u32[]{:S(2)}, u32[]{:S(2)}) collective-permute-start(f32[32,64,128]{2,1,0:T(8,128)S(1)} %get-tuple-element.180), channel_id=1, source_target_pairs={{0,26},{1,27},{2,24},{3,25},{4,30},{5,31},{6,28},{7,29},{8,18},{9,... | collective-permute-start | bytes 3145736 | tf_op jit(solution)/shard_map/ppermute | solution.py:302
  500.7 102.4 %collective-permute-start.17 = (f32[32,64,128]{2,1,0:T(8,128)S(1)}, f32[32,64,128]{2,1,0:T(8,128)S(1)}, u32[]{:S(2)}, u32[]{:S(2)}) collective-permute-start(f32[32,64,128]{2,1,0:T(8,128)S(1)} %get-tuple-element.161), channel_id=1, source_target_pairs={{0,6},{1,7},{2,4},{3,5},{4,2},{5,3},{6,0},{7,1},{8,14},{9,15},{10,... | collective-permute-start | bytes 3145736 | tf_op jit(solution)/shard_map/ppermute | solution.py:302
  553.4 115.5 %collective-permute-start.18 = (f32[32,64,128]{2,1,0:T(8,128)S(1)}, f32[32,64,128]{2,1,0:T(8,128)S(1)}, u32[]{:S(2)}, u32[]{:S(2)}) collective-permute-start(f32[32,64,128]{2,1,0:T(8,128)S(1)} %get-tuple-element.163), channel_id=1, source_target_pairs={{0,8},{1,9},{2,10},{3,11},{4,12},{5,13},{6,14},{7,15},{8,0},{9,1},... | collective-permute-start | bytes 3145736 | tf_op jit(solution)/shard_map/ppermute | solution.py:302
  568.2 101.3 %collective-permute-start.16 = (f32[32,64,128]{2,1,0:T(8,128)S(1)}, f32[32,64,128]{2,1,0:T(8,128)S(1)}, u32[]{:S(2)}, u32[]{:S(2)}) collective-permute-start(f32[32,64,128]{2,1,0:T(8,128)S(1)} %get-tuple-element.159), channel_id=1, source_target_pairs={{0,4},{1,5},{2,6},{3,7},{4,0},{5,1},{6,2},{7,3},{8,12},{9,13},{10,... | collective-permute-start | bytes 3145736 | tf_op jit(solution)/shard_map/ppermute | solution.py:302
  597.9 74.9 %collective-permute-start.28 = (f32[32,64,128]{2,1,0:T(8,128)S(1)}, f32[32,64,128]{2,1,0:T(8,128)S(1)}, u32[]{:S(2)}, u32[]{:S(2)}) collective-permute-start(f32[32,64,128]{2,1,0:T(8,128)S(1)} %get-tuple-element.183), channel_id=1, source_target_pairs={{0,28},{1,29},{2,30},{3,31},{4,24},{5,25},{6,26},{7,27},{8,20},{9,... | collective-permute-start | bytes 3145736 | tf_op jit(solution)/shard_map/ppermute | solution.py:302
  601.5 147.1 %collective-permute-start.29 = (f32[32,64,128]{2,1,0:T(8,128)}, f32[32,64,128]{2,1,0:T(8,128)S(1)}, u32[]{:S(2)}, u32[]{:S(2)}) collective-permute-start(f32[32,64,128]{2,1,0:T(8,128)} %get-tuple-element.185), channel_id=1, source_target_pairs={{0,30},{1,31},{2,28},{3,29},{4,26},{5,27},{6,24},{7,25},{8,22},{9,... | collective-permute-start | bytes 3145736 | tf_op jit(solution)/shard_map/ppermute | solution.py:302
  603.0 188.2 %collective-permute-start.27 = (f32[32,64,128]{2,1,0:T(8,128)}, f32[32,64,128]{2,1,0:T(8,128)S(1)}, u32[]{:S(2)}, u32[]{:S(2)}) collective-permute-start(f32[32,64,128]{2,1,0:T(8,128)} %get-tuple-element.181), channel_id=1, source_target_pairs={{0,22},{1,23},{2,20},{3,21},{4,18},{5,19},{6,16},{7,17},{8,30},{9,... | collective-permute-start | bytes 3145736 | tf_op jit(solution)/shard_map/ppermute | solution.py:302
  668.9 122.4 %collective-permute-start.20 = (f32[32,64,128]{2,1,0:T(8,128)}, f32[32,64,128]{2,1,0:T(8,128)S(1)}, u32[]{:S(2)}, u32[]{:S(2)}) collective-permute-start(f32[32,64,128]{2,1,0:T(8,128)} %get-tuple-element.167), channel_id=1, source_target_pairs={{0,12},{1,13},{2,14},{3,15},{4,8},{5,9},{6,10},{7,11},{8,4},{9,5},... | collective-permute-start | bytes 3145736 | tf_op jit(solution)/shard_map/ppermute | solution.py:302
  669.6 126.0 %collective-permute-start.21 = (f32[32,64,128]{2,1,0:T(8,128)}, f32[32,64,128]{2,1,0:T(8,128)}, u32[]{:S(2)}, u32[]{:S(2)}) collective-permute-start(f32[32,64,128]{2,1,0:T(8,128)} %get-tuple-element.169), channel_id=1, source_target_pairs={{0,14},{1,15},{2,12},{3,13},{4,10},{5,11},{6,8},{7,9},{8,6},{9,7},... | collective-permute-start | bytes 3145736 | tf_op jit(solution)/shard_map/ppermute | solution.py:302
  672.8 128.2 %collective-permute-start.19 = (f32[32,64,128]{2,1,0:T(8,128)}, f32[32,64,128]{2,1,0:T(8,128)}, u32[]{:S(2)}, u32[]{:S(2)}) collective-permute-start(f32[32,64,128]{2,1,0:T(8,128)} %get-tuple-element.165), channel_id=1, source_target_pairs={{0,10},{1,11},{2,8},{3,9},{4,14},{5,15},{6,12},{7,13},{8,2},{9,3},... | collective-permute-start | bytes 3145736 | tf_op jit(solution)/shard_map/ppermute | solution.py:302
  748.6 64.9 %collective-permute-start.30 = (f32[32,64,128]{2,1,0:T(8,128)S(1)}, f32[32,64,128]{2,1,0:T(8,128)S(1)}, u32[]{:S(2)}, u32[]{:S(2)}) collective-permute-start(f32[32,64,128]{2,1,0:T(8,128)S(1)} %get-tuple-element.189), channel_id=1, source_target_pairs={{0,2},{1,3},{2,0},{3,1},{4,6},{5,7},{6,4},{7,5},{8,10},{9,11},{10,... | collective-permute-start | bytes 3145736 | tf_op jit(solution)/shard_map/ppermute | solution.py:302
  791.2 63.1 %collective-permute-start.32 = (f32[32,64,128]{2,1,0:T(8,128)S(1)}, f32[32,64,128]{2,1,0:T(8,128)S(1)}, u32[]{:S(2)}, u32[]{:S(2)}) collective-permute-start(f32[32,64,128]{2,1,0:T(8,128)S(1)} %get-tuple-element.193), channel_id=1, source_target_pairs={{0,6},{1,7},{2,4},{3,5},{4,2},{5,3},{6,0},{7,1},{8,14},{9,15},{10,... | collective-permute-start | bytes 3145736 | tf_op jit(solution)/shard_map/ppermute | solution.py:302
  791.3 76.7 %collective-permute-start.31 = (f32[32,64,128]{2,1,0:T(8,128)S(1)}, f32[32,64,128]{2,1,0:T(8,128)S(1)}, u32[]{:S(2)}, u32[]{:S(2)}) collective-permute-start(f32[32,64,128]{2,1,0:T(8,128)S(1)} %get-tuple-element.191), channel_id=1, source_target_pairs={{0,4},{1,5},{2,6},{3,7},{4,0},{5,1},{6,2},{7,3},{8,12},{9,13},{10,... | collective-permute-start | bytes 3145736 | tf_op jit(solution)/shard_map/ppermute | solution.py:302
  795.6 73.5 %collective-permute-start.39 = (f32[32,64,128]{2,1,0:T(8,128)S(1)}, f32[32,64,128]{2,1,0:T(8,128)S(1)}, u32[]{:S(2)}, u32[]{:S(2)}) collective-permute-start(f32[32,64,128]{2,1,0:T(8,128)S(1)} %get-tuple-element.208), channel_id=1, source_target_pairs={{0,24},{1,25},{2,26},{3,27},{4,28},{5,29},{6,30},{7,31},{8,16},{9,... | collective-permute-start | bytes 3145736 | tf_op jit(solution)/shard_map/ppermute | solution.py:302
  801.0 111.3 %collective-permute-start.38 = (f32[32,64,128]{2,1,0:T(8,128)S(1)}, f32[32,64,128]{2,1,0:T(8,128)S(1)}, u32[]{:S(2)}, u32[]{:S(2)}) collective-permute-start(f32[32,64,128]{2,1,0:T(8,128)S(1)} %get-tuple-element.205), channel_id=1, source_target_pairs={{0,18},{1,19},{2,16},{3,17},{4,22},{5,23},{6,20},{7,21},{8,26},{9,... | collective-permute-start | bytes 3145736 | tf_op jit(solution)/shard_map/ppermute | solution.py:302
  814.5 119.8 %collective-permute-start.37 = (f32[32,64,128]{2,1,0:T(8,128)S(1)}, f32[32,64,128]{2,1,0:T(8,128)S(1)}, u32[]{:S(2)}, u32[]{:S(2)}) collective-permute-start(f32[32,64,128]{2,1,0:T(8,128)S(1)} %get-tuple-element.203), channel_id=1, source_target_pairs={{0,16},{1,17},{2,18},{3,19},{4,20},{5,21},{6,22},{7,23},{8,24},{9,... | collective-permute-start | bytes 3145736 | tf_op jit(solution)/shard_map/ppermute | solution.py:302
  855.3 96.8 %collective-permute-start.33 = (f32[32,64,128]{2,1,0:T(8,128)S(1)}, f32[32,64,128]{2,1,0:T(8,128)S(1)}, u32[]{:S(2)}, u32[]{:S(2)}) collective-permute-start(f32[32,64,128]{2,1,0:T(8,128)S(1)} %get-tuple-element.195), channel_id=1, source_target_pairs={{0,8},{1,9},{2,10},{3,11},{4,12},{5,13},{6,14},{7,15},{8,0},{9,1},... | collective-permute-start | bytes 3145736 | tf_op jit(solution)/shard_map/ppermute | solution.py:302
  869.0 157.2 %collective-permute-start.35 = (f32[32,64,128]{2,1,0:T(8,128)}, f32[32,64,128]{2,1,0:T(8,128)S(1)}, u32[]{:S(2)}, u32[]{:S(2)}) collective-permute-start(f32[32,64,128]{2,1,0:T(8,128)} %get-tuple-element.199), channel_id=1, source_target_pairs={{0,12},{1,13},{2,14},{3,15},{4,8},{5,9},{6,10},{7,11},{8,4},{9,5},... | collective-permute-start | bytes 3145736 | tf_op jit(solution)/shard_map/ppermute | solution.py:302
  870.0 180.0 %collective-permute-start.34 = (f32[32,64,128]{2,1,0:T(8,128)}, f32[32,64,128]{2,1,0:T(8,128)S(1)}, u32[]{:S(2)}, u32[]{:S(2)}) collective-permute-start(f32[32,64,128]{2,1,0:T(8,128)} %get-tuple-element.197), channel_id=1, source_target_pairs={{0,10},{1,11},{2,8},{3,9},{4,14},{5,15},{6,12},{7,13},{8,2},{9,3},... | collective-permute-start | bytes 3145736 | tf_op jit(solution)/shard_map/ppermute | solution.py:302
  913.2 157.5 %collective-permute-start.40 = (f32[32,64,128]{2,1,0:T(8,128)}, f32[32,64,128]{2,1,0:T(8,128)S(1)}, u32[]{:S(2)}, u32[]{:S(2)}) collective-permute-start(f32[32,64,128]{2,1,0:T(8,128)} %get-tuple-element.209), channel_id=1, source_target_pairs={{0,20},{1,21},{2,22},{3,23},{4,16},{5,17},{6,18},{7,19},{8,28},{9,... | collective-permute-start | bytes 3145736 | tf_op jit(solution)/shard_map/ppermute | solution.py:302
  935.3 146.2 %collective-permute-start.41 = (f32[32,64,128]{2,1,0:T(8,128)}, f32[32,64,128]{2,1,0:T(8,128)S(1)}, u32[]{:S(2)}, u32[]{:S(2)}) collective-permute-start(f32[32,64,128]{2,1,0:T(8,128)} %get-tuple-element.212), channel_id=1, source_target_pairs={{0,26},{1,27},{2,24},{3,25},{4,30},{5,31},{6,28},{7,29},{8,18},{9,... | collective-permute-start | bytes 3145736 | tf_op jit(solution)/shard_map/ppermute | solution.py:302
  953.1 132.6 %collective-permute-start.43 = (f32[32,64,128]{2,1,0:T(8,128)}, f32[32,64,128]{2,1,0:T(8,128)S(1)}, u32[]{:S(2)}, u32[]{:S(2)}) collective-permute-start(f32[32,64,128]{2,1,0:T(8,128)} %get-tuple-element.215), channel_id=1, source_target_pairs={{0,28},{1,29},{2,30},{3,31},{4,24},{5,25},{6,26},{7,27},{8,20},{9,... | collective-permute-start | bytes 3145736 | tf_op jit(solution)/shard_map/ppermute | solution.py:302
  1027.2 68.5 %collective-permute-start.54 = (f32[32,64,128]{2,1,0:T(8,128)S(1)}, f32[32,64,128]{2,1,0:T(8,128)S(1)}, u32[]{:S(2)}, u32[]{:S(2)}) collective-permute-start(f32[32,64,128]{2,1,0:T(8,128)S(1)} %get-tuple-element.240), channel_id=1, source_target_pairs={{0,24},{1,25},{2,26},{3,27},{4,28},{5,29},{6,30},{7,31},{8,16},{9,... | collective-permute-start | bytes 3145736 | tf_op jit(solution)/shard_map/ppermute | solution.py:302
  1051.0 47.3 %collective-permute-start.36 = (f32[32,64,128]{2,1,0:T(8,128)S(1)}, f32[32,64,128]{2,1,0:T(8,128)S(1)}, u32[]{:S(2)}, u32[]{:S(2)}) collective-permute-start(f32[32,64,128]{2,1,0:T(8,128)S(1)} %copy-done.193), channel_id=1, source_target_pairs={{0,14},{1,15},{2,12},{3,13},{4,10},{5,11},{6,8},{7,9},{8,6},{9,7},... | collective-permute-start | bytes 3145736 | tf_op jit(solution)/shard_map/ppermute | solution.py:302
  1071.7 177.1 %collective-permute-start.52 = (f32[32,64,128]{2,1,0:T(8,128)S(1)}, f32[32,64,128]{2,1,0:T(8,128)S(1)}, u32[]{:S(2)}, u32[]{:S(2)}) collective-permute-start(f32[32,64,128]{2,1,0:T(8,128)S(1)} %get-tuple-element.235), channel_id=1, source_target_pairs={{0,16},{1,17},{2,18},{3,19},{4,20},{5,21},{6,22},{7,23},{8,24},{9,... | collective-permute-start | bytes 3145736 | tf_op jit(solution)/shard_map/ppermute | solution.py:302
  1082.5 167.5 %collective-permute-start.44 = (f32[32,64,128]{2,1,0:T(8,128)S(1)}, f32[32,64,128]{2,1,0:T(8,128)S(1)}, u32[]{:S(2)}, u32[]{:S(2)}) collective-permute-start(f32[32,64,128]{2,1,0:T(8,128)S(1)} %copy-done.191), channel_id=1, source_target_pairs={{0,30},{1,31},{2,28},{3,29},{4,26},{5,27},{6,24},{7,25},{8,22},{9,... | collective-permute-start | bytes 3145736 | tf_op jit(solution)/shard_map/ppermute | solution.py:302
  1086.7 233.3 %collective-permute-start.42 = (f32[32,64,128]{2,1,0:T(8,128)S(1)}, f32[32,64,128]{2,1,0:T(8,128)S(1)}, u32[]{:S(2)}, u32[]{:S(2)}) collective-permute-start(f32[32,64,128]{2,1,0:T(8,128)S(1)} %copy-done.189), channel_id=1, source_target_pairs={{0,22},{1,23},{2,20},{3,21},{4,18},{5,19},{6,16},{7,17},{8,30},{9,... | collective-permute-start | bytes 3145736 | tf_op jit(solution)/shard_map/ppermute | solution.py:302
  1096.7 224.4 %collective-permute-start.45 = (f32[32,64,128]{2,1,0:T(8,128)S(1)}, f32[32,64,128]{2,1,0:T(8,128)S(1)}, u32[]{:S(2)}, u32[]{:S(2)}) collective-permute-start(f32[32,64,128]{2,1,0:T(8,128)S(1)} %get-tuple-element.221), channel_id=1, source_target_pairs={{0,2},{1,3},{2,0},{3,1},{4,6},{5,7},{6,4},{7,5},{8,10},{9,11},{10,... | collective-permute-start | bytes 3145736 | tf_op jit(solution)/shard_map/ppermute | solution.py:302
  1099.3 257.4 %collective-permute-start.55 = (f32[32,64,128]{2,1,0:T(8,128)S(1)}, f32[32,64,128]{2,1,0:T(8,128)S(1)}, u32[]{:S(2)}, u32[]{:S(2)}) collective-permute-start(f32[32,64,128]{2,1,0:T(8,128)S(1)} %get-tuple-element.241), channel_id=1, source_target_pairs={{0,20},{1,21},{2,22},{3,23},{4,16},{5,17},{6,18},{7,19},{8,28},{9,... | collective-permute-start | bytes 3145736 | tf_op jit(solution)/shard_map/ppermute | solution.py:302
  1249.8 123.8 %collective-permute-start.53 = (f32[32,64,128]{2,1,0:T(8,128)S(1)}, f32[32,64,128]{2,1,0:T(8,128)S(1)}, u32[]{:S(2)}, u32[]{:S(2)}) collective-permute-start(f32[32,64,128]{2,1,0:T(8,128)S(1)} %get-tuple-element.237), channel_id=1, source_target_pairs={{0,18},{1,19},{2,16},{3,17},{4,22},{5,23},{6,20},{7,21},{8,26},{9,... | collective-permute-start | bytes 3145736 | tf_op jit(solution)/shard_map/ppermute | solution.py:302
  1250.9 158.2 %collective-permute-start.56 = (f32[32,64,128]{2,1,0:T(8,128)}, f32[32,64,128]{2,1,0:T(8,128)}, u32[]{:S(2)}, u32[]{:S(2)}) collective-permute-start(f32[32,64,128]{2,1,0:T(8,128)} %get-tuple-element.244), channel_id=1, source_target_pairs={{0,26},{1,27},{2,24},{3,25},{4,30},{5,31},{6,28},{7,29},{8,18},{9,... | collective-permute-start | bytes 3145736 | tf_op jit(solution)/shard_map/ppermute | solution.py:302
  1321.0 89.1 %collective-permute-start.47 = (f32[32,64,128]{2,1,0:T(8,128)}, f32[32,64,128]{2,1,0:T(8,128)}, u32[]{:S(2)}, u32[]{:S(2)}) collective-permute-start(f32[32,64,128]{2,1,0:T(8,128)} %get-tuple-element.225), channel_id=1, source_target_pairs={{0,6},{1,7},{2,4},{3,5},{4,2},{5,3},{6,0},{7,1},{8,14},{9,15},{10,... | collective-permute-start | bytes 3145736 | tf_op jit(solution)/shard_map/ppermute | solution.py:302
  1322.0 123.1 %collective-permute-start.46 = (f32[32,64,128]{2,1,0:T(8,128)}, f32[32,64,128]{2,1,0:T(8,128)}, u32[]{:S(2)}, u32[]{:S(2)}) collective-permute-start(f32[32,64,128]{2,1,0:T(8,128)} %get-tuple-element.223), channel_id=1, source_target_pairs={{0,4},{1,5},{2,6},{3,7},{4,0},{5,1},{6,2},{7,3},{8,12},{9,13},{10,... | collective-permute-start | bytes 3145736 | tf_op jit(solution)/shard_map/ppermute | solution.py:302
  1357.8 99.8 %collective-permute-start.48 = (f32[32,64,128]{2,1,0:T(8,128)}, f32[32,64,128]{2,1,0:T(8,128)}, u32[]{:S(2)}, u32[]{:S(2)}) collective-permute-start(f32[32,64,128]{2,1,0:T(8,128)} %get-tuple-element.227), channel_id=1, source_target_pairs={{0,8},{1,9},{2,10},{3,11},{4,12},{5,13},{6,14},{7,15},{8,0},{9,1},... | collective-permute-start | bytes 3145736 | tf_op jit(solution)/shard_map/ppermute | solution.py:302
  1374.7 88.1 %collective-permute-start.59 = (f32[32,64,128]{2,1,0:T(8,128)}, f32[32,64,128]{2,1,0:T(8,128)}, u32[]{:S(2)}, u32[]{:S(2)}) collective-permute-start(f32[32,64,128]{2,1,0:T(8,128)} %get-tuple-element.249), channel_id=1, source_target_pairs={{0,30},{1,31},{2,28},{3,29},{4,26},{5,27},{6,24},{7,25},{8,22},{9,... | collective-permute-start | bytes 3145736 | tf_op jit(solution)/shard_map/ppermute | solution.py:302
  1409.1 136.6 %collective-permute-start.58 = (f32[32,64,128]{2,1,0:T(8,128)}, f32[32,64,128]{2,1,0:T(8,128)}, u32[]{:S(2)}, u32[]{:S(2)}) collective-permute-start(f32[32,64,128]{2,1,0:T(8,128)} %get-tuple-element.247), channel_id=1, source_target_pairs={{0,28},{1,29},{2,30},{3,31},{4,24},{5,25},{6,26},{7,27},{8,20},{9,... | collective-permute-start | bytes 3145736 | tf_op jit(solution)/shard_map/ppermute | solution.py:302
  1410.1 158.5 %collective-permute-start.57 = (f32[32,64,128]{2,1,0:T(8,128)}, f32[32,64,128]{2,1,0:T(8,128)}, u32[]{:S(2)}, u32[]{:S(2)}) collective-permute-start(f32[32,64,128]{2,1,0:T(8,128)} %get-tuple-element.245), channel_id=1, source_target_pairs={{0,22},{1,23},{2,20},{3,21},{4,18},{5,19},{6,16},{7,17},{8,30},{9,... | collective-permute-start | bytes 3145736 | tf_op jit(solution)/shard_map/ppermute | solution.py:302
  1445.2 123.5 %collective-permute-start.50 = (f32[32,64,128]{2,1,0:T(8,128)}, f32[32,64,128]{2,1,0:T(8,128)}, u32[]{:S(2)}, u32[]{:S(2)}) collective-permute-start(f32[32,64,128]{2,1,0:T(8,128)} %get-tuple-element.231), channel_id=1, source_target_pairs={{0,12},{1,13},{2,14},{3,15},{4,8},{5,9},{6,10},{7,11},{8,4},{9,5},... | collective-permute-start | bytes 3145736 | tf_op jit(solution)/shard_map/ppermute | solution.py:302
  1457.6 111.1 %collective-permute-start.49 = (f32[32,64,128]{2,1,0:T(8,128)}, f32[32,64,128]{2,1,0:T(8,128)}, u32[]{:S(2)}, u32[]{:S(2)}) collective-permute-start(f32[32,64,128]{2,1,0:T(8,128)} %get-tuple-element.229), channel_id=1, source_target_pairs={{0,10},{1,11},{2,8},{3,9},{4,14},{5,15},{6,12},{7,13},{8,2},{9,3},... | collective-permute-start | bytes 3145736 | tf_op jit(solution)/shard_map/ppermute | solution.py:302
  1462.8 105.9 %collective-permute-start.51 = (f32[32,64,128]{2,1,0:T(8,128)}, f32[32,64,128]{2,1,0:T(8,128)}, u32[]{:S(2)}, u32[]{:S(2)}) collective-permute-start(f32[32,64,128]{2,1,0:T(8,128)} %get-tuple-element.233), channel_id=1, source_target_pairs={{0,14},{1,15},{2,12},{3,13},{4,10},{5,11},{6,8},{7,9},{8,6},{9,7},... | collective-permute-start | bytes 3145736 | tf_op jit(solution)/shard_map/ppermute | solution.py:302
  1681.8 52.2 %collective-permute-start.72 = (f32[16,64,256]{2,1,0:T(8,128)}, f32[16,64,256]{2,1,0:T(8,128)}, u32[]{:S(2)}, u32[]{:S(2)}) collective-permute-start(f32[16,64,256]{2,1,0:T(8,128)} %reduce_z.12), channel_id=1, source_target_pairs={{0,1},{1,0},{2,3},{3,2},{4,5},{5,4},{6,7},{7,6},{8,9},{9,8},{10,11... | collective-permute-start | bytes 3145736 | tf_op jit(solution)/shard_map/ppermute | solution.py:302
  1690.2 43.7 %collective-permute-start.73 = (f32[16,64,256]{2,1,0:T(8,128)}, f32[16,64,256]{2,1,0:T(8,128)}, u32[]{:S(2)}, u32[]{:S(2)}) collective-permute-start(f32[16,64,256]{2,1,0:T(8,128)} %reduce_z.13), channel_id=1, source_target_pairs={{0,1},{1,0},{2,3},{3,2},{4,5},{5,4},{6,7},{7,6},{8,9},{9,8},{10,11... | collective-permute-start | bytes 3145736 | tf_op jit(solution)/shard_map/ppermute | solution.py:302
  1694.3 39.7 %collective-permute-start.74 = (f32[16,64,256]{2,1,0:T(8,128)}, f32[16,64,256]{2,1,0:T(8,128)}, u32[]{:S(2)}, u32[]{:S(2)}) collective-permute-start(f32[16,64,256]{2,1,0:T(8,128)} %reduce_z.14), channel_id=1, source_target_pairs={{0,1},{1,0},{2,3},{3,2},{4,5},{5,4},{6,7},{7,6},{8,9},{9,8},{10,11... | collective-permute-start | bytes 3145736 | tf_op jit(solution)/shard_map/ppermute | solution.py:302
  1700.7 33.3 %collective-permute-start.75 = (f32[16,64,256]{2,1,0:T(8,128)}, f32[16,64,256]{2,1,0:T(8,128)}, u32[]{:S(2)}, u32[]{:S(2)}) collective-permute-start(f32[16,64,256]{2,1,0:T(8,128)} %reduce_z.15), channel_id=1, source_target_pairs={{0,1},{1,0},{2,3},{3,2},{4,5},{5,4},{6,7},{7,6},{8,9},{9,8},{10,11... | collective-permute-start | bytes 3145736 | tf_op jit(solution)/shard_map/ppermute | solution.py:302
  (225 other events, 9303.3 us)

commit v2 on v1

--- a/solution.py
+++ b/solution.py
@@ -13,7 +13,9 @@
 CORES = 2
 AXES = ("gz", "gy")
 DEPTH = 6
-MIB = 1 << 20
+PACK_AT = 9
+REDUCE_X = 4
+VMEM_LIMIT = 60 << 20
 F32 = jnp.float32
 BF16 = jnp.bfloat16
 
@@ -46,9 +48,9 @@
     return lax.dot_general(left, right, (((0,), (0,)), ((), ())), preferred_element_type=F32)
 
 
-def pack_kernel(groups, width, me_ref, field_ref, *out_refs):
-    turned = out_refs[-1]
-    me = me_ref[0]
+def pack_kernel(groups, width, me_ref, field_ref, *refs):
+    out_refs, turned = refs[:-1], refs[-1]
+    me = me_ref[0] % groups
     for z in range(field_ref.shape[1]):
         turned[...] = field_ref[0, z].T
         for k in range(groups):
@@ -56,25 +58,25 @@
             out_refs[k][:, z, :] = turned[pl.ds(start, width), :]
 
 
-def pack(field, me, species, groups):
+def pack(field, me_half, species, groups):
     _, z_n, y_n, x_n = field.shape
-    width = x_n // groups
+    width = x_n // (2 * groups)
     z_tile = 8
     return pl.pallas_call(
         functools.partial(pack_kernel, groups, width),
         grid_spec=pltpu.PrefetchScalarGridSpec(
             num_scalar_prefetch=1,
             grid=(z_n // z_tile,),
-            in_specs=[pl.BlockSpec((1, z_tile, y_n, x_n), lambda i, m: (species, i, 0, 0))],
+            in_specs=[pl.BlockSpec((1, z_tile, y_n, x_n // 2), lambda i, m: (species, i, 0, m[1]))],
             out_specs=[pl.BlockSpec((width, z_tile, y_n), lambda i, m: (0, i, 0))] * groups,
-            scratch_shapes=[pltpu.VMEM((x_n, y_n), F32)],
+            scratch_shapes=[pltpu.VMEM((x_n // 2, y_n), F32)],
         ),
         out_shape=[jax.ShapeDtypeStruct((width, z_n, y_n), F32)] * groups,
-        compiler_params=pltpu.CompilerParams(vmem_limit_bytes=24 * MIB),
+        compiler_params=pltpu.CompilerParams(vmem_limit_bytes=VMEM_LIMIT),
         cost_estimate=pl.CostEstimate(
-            flops=0, bytes_accessed=4 * 8 * z_n * y_n * x_n, transcendentals=0),
+            flops=0, bytes_accessed=4 * z_n * y_n * x_n, transcendentals=0),
         name="pack",
-    )(me, field)
+    )(me_half, field)
 
 
 def gram_z_kernel(groups, side, me_ref, prev_ref, *refs):
@@ -122,7 +124,7 @@
                             pltpu.VMEM((order, order), F32), pltpu.VMEM((order, order), F32)],
         ),
         out_shape=jax.ShapeDtypeStruct((order, order), F32),
-        compiler_params=pltpu.CompilerParams(vmem_limit_bytes=32 * MIB),
+        compiler_params=pltpu.CompilerParams(vmem_limit_bytes=VMEM_LIMIT),
         cost_estimate=pl.CostEstimate(
             flops=4 * order * order * width * side * y_n,
             bytes_accessed=4 * groups * width * z_n * y_n, transcendentals=0),
@@ -130,26 +132,59 @@
     )(me, prev, *pieces)
 
 
-def basis_kernel(gz_n, me_ref, gram_ref, start_ref, basis_ref, turned_ref):
+def split3(value):
+    first = value.astype(BF16)
+    rest = value - first.astype(F32)
+    second = rest.astype(BF16)
+    return first, second, (rest - second.astype(F32)).astype(BF16)
+
+
+def dot_split(left, right, dot):
+    rows = left[0].shape[0]
+    first = dot(jnp.concatenate(left, axis=0), right[0])
+    second = dot(jnp.concatenate(left[:2], axis=0), right[1])
+    third = dot(left[0], right[2])
+    small = first[2 * rows:] + second[rows:] + third
+    return first[:rows] + (first[rows:2 * rows] + second[:rows] + small)
+
+
+def inverse_factor(inner):
+    rank = inner.shape[0]
+    row_id = lax.broadcasted_iota(jnp.int32, (rank, 1), 0)
+    rows = lax.broadcasted_iota(jnp.int32, (rank, 2 * rank), 0)
+    lanes = lax.broadcasted_iota(jnp.int32, (rank, 2 * rank), 1)
+    eye = jnp.where(lanes[:, :rank] == rows[:, :rank], 1.0, 0.0).astype(F32)
+    work = jnp.concatenate([inner, eye], axis=1)
+    for k in range(0, rank - 2, 2):
+        col0 = jnp.broadcast_to(work[:, k:k + 1], work.shape)
+        col1 = jnp.broadcast_to(work[:, k + 1:k + 2], work.shape)
+        row0, row1 = work[k:k + 1, :], work[k + 1:k + 2, :]
+        inv0 = 1.0 / col0[k:k + 1, :]
+        share = col1[k:k + 1, :] * inv0
+        inv1 = 1.0 / (col1[k + 1:k + 2, :] - col1[k:k + 1, :] * share)
+        use1 = (row1 - share * row0) * inv1
+        use0 = row0 * inv0 - share * use1
+        below = row_id > k + 1
+        work = work - (jnp.where(below, col0, 0.0) * use0 + jnp.where(below, col1, 0.0) * use1)
+    take = lambda mask: jnp.sum(jnp.where(mask, work, 0.0), axis=1, keepdims=True)
+    above = pltpu.roll(work, 1, 0)
+    left = take(lanes == rows - 1)
+    pivot_above = jnp.sum(jnp.where(lanes == rows - 1, above, 0.0), axis=1, keepdims=True)
+    share = jnp.where(row_id % 2 == 1, left / jnp.where(row_id == 0, 1.0, pivot_above), 0.0)
+    work = work - share * above
+    return work[:, rank:] * (1.0 / jnp.sqrt(take(lanes == rows)))
+
+
+def basis_kernel(gz_n, me_ref, gram_ref, start_ref, basis_ref, turned_ref, *parts):
     rank, order = start_ref.shape
-    highest = dict(precision=lax.Precision.HIGHEST, preferred_element_type=F32)
-    row_id = lax.broadcasted_iota(jnp.int32, (rank, 1), 0)
-    lane_id = lax.broadcasted_iota(jnp.int32, (rank, rank), 1)
-    row_ids = lax.broadcasted_iota(jnp.int32, (rank, rank), 0)
-    eye = jnp.where(lane_id == row_ids, 1.0, 0.0).astype(F32)
+    for ref, part in zip(parts, split3(gram_ref[...])):
+        ref[...] = part
 
     def iterate(_, basis_t):
-        product = lax.dot_general(basis_t, gram_ref[...], (((1,), (0,)), ((), ())), **highest)
-        inner = lax.dot_general(product, product, (((1,), (1,)), ((), ())), **highest)
-        work = jnp.concatenate([inner, eye], axis=1)
-        for k in range(rank - 1):
-            row = work[k:k + 1, :]
-            scaled = row / work[k:k + 1, k:k + 1]
-            factor = jnp.where(row_id > k, work[:, k:k + 1], 0.0)
-            work = work - factor * scaled
-        pivots = jnp.sum(jnp.where(lane_id == row_ids, work[:, :rank], 0.0), axis=1, keepdims=True)
-        inverse = work[:, rank:] * (1.0 / jnp.sqrt(pivots))
-        return lax.dot_general(inverse, product, (((1,), (0,)), ((), ())), **highest)
+        product = dot_split(split3(basis_t), [ref[...] for ref in parts], dot_nn)
+        pieces = split3(product)
+        inner = dot_split(pieces, pieces, dot_nt)
+        return dot_split(split3(inverse_factor(inner)), pieces, dot_nn)
 
     basis_t = lax.fori_loop(0, ITERS, iterate, start_ref[...])
     basis_ref[...] = basis_t
@@ -173,52 +208,55 @@
         in_specs=[pl.BlockSpec(memory_space=pltpu.SMEM), vmem, vmem],
         out_specs=[vmem, vmem],
         out_shape=[jax.ShapeDtypeStruct((rank, order), F32)] * 2,
-        compiler_params=pltpu.CompilerParams(vmem_limit_bytes=24 * MIB),
+        scratch_shapes=[pltpu.VMEM((order, order), BF16)] * 3,
+        compiler_params=pltpu.CompilerParams(vmem_limit_bytes=VMEM_LIMIT),
         name="leaf_basis",
     )(me_z, gram, start_t)
 
 
-def reduce_kernel(groups, side, pos_ref, basis_ref, *refs):
-    pieces, out_ref = refs[:groups], refs[groups]
+def reduce_kernel(species, groups, side, pos_ref, basis_ref, *refs):
+    pieces, out_refs = refs[:species * groups], refs[species * groups:]
     rank = basis_ref.shape[0]
     me_x = pos_ref[1]
     x_tile, z_n, y_n = pieces[0].shape
     high, low = split_bf16(basis_ref[...])
     both = jnp.concatenate([high, low], axis=0)
-    for x in range(x_tile):
-        cols = [jnp.concatenate([pieces[k][x] for k in range(j, groups, side)], axis=0)
-                for j in range(side)]
-        field_high, field_low = split_bf16(jnp.concatenate(cols, axis=1))
-        first = dot_nn(both, field_high)
-        total = first[:rank] + (first[rank:] + dot_nn(high, field_low))
-        for j in range(side):
-            start = pl.multiple_of((me_x ^ j) * y_n, y_n)
-            out_ref[x, :, pl.ds(start, y_n)] = total[:, j * y_n:(j + 1) * y_n]
+    for s in range(species):
+        for x in range(x_tile):
+            cols = [jnp.concatenate([pieces[s * groups + k][x] for k in range(j, groups, side)], axis=0)
+                    for j in range(side)]
+            field_high, field_low = split_bf16(jnp.concatenate(cols, axis=1))
+            first = dot_nn(both, field_high)
+            total = first[:rank] + (first[rank:] + dot_nn(high, field_low))
+            for j in range(side):
+                start = pl.multiple_of((me_x ^ j) * y_n, y_n)
+                out_refs[s][x, :, pl.ds(start, y_n)] = total[:, j * y_n:(j + 1) * y_n]
 
 
 def reduce_half(basis_t, pieces, pos, side):
-    groups = len(pieces)
-    width, z_n, y_n = pieces[0].shape
+    species, groups = len(pieces), len(pieces[0])
+    width, z_n, y_n = pieces[0][0].shape
     half = width // CORES
-    x_tile = 4
+    x_tile = REDUCE_X
     rank, order = basis_t.shape
     tiles = half // x_tile
     return pl.pallas_call(
-        functools.partial(reduce_kernel, groups, side),
+        functools.partial(reduce_kernel, species, groups, side),
         grid_spec=pltpu.PrefetchScalarGridSpec(
             num_scalar_prefetch=1,
             grid=(tiles,),
             in_specs=[pl.BlockSpec((rank, order), lambda i, p: (0, 0))]
-            + [pl.BlockSpec((x_tile, z_n, y_n), lambda i, p: (p[0] * tiles + i, 0, 0))] * groups,
-            out_specs=pl.BlockSpec((x_tile, rank, side * y_n), lambda i, p: (i, 0, 0)),
+            + [pl.BlockSpec((x_tile, z_n, y_n), lambda i, p: (p[0] * tiles + i, 0, 0))]
+            * (species * groups),
+            out_specs=[pl.BlockSpec((x_tile, rank, side * y_n), lambda i, p: (i, 0, 0))] * species,
         ),
-        out_shape=jax.ShapeDtypeStruct((half, rank, side * y_n), F32),
-        compiler_params=pltpu.CompilerParams(vmem_limit_bytes=24 * MIB),
+        out_shape=[jax.ShapeDtypeStruct((half, rank, side * y_n), F32)] * species,
+        compiler_params=pltpu.CompilerParams(vmem_limit_bytes=VMEM_LIMIT),
         cost_estimate=pl.CostEstimate(
-            flops=6 * rank * order * half * side * y_n,
-            bytes_accessed=4 * groups * half * z_n * y_n, transcendentals=0),
+            flops=6 * species * rank * order * half * side * y_n,
+            bytes_accessed=4 * species * groups * half * z_n * y_n, transcendentals=0),
         name="reduce_z",
-    )(pos, basis_t, *pieces)
+    )(pos, basis_t, *[piece for row in pieces for piece in row])
 
 
 def gram_y_kernel(species, side, core_ref, *refs):
@@ -268,7 +306,7 @@
         ),
         out_shape=[jax.ShapeDtypeStruct((species, half, rank, order), F32),
                    jax.ShapeDtypeStruct((order, order), F32)],
-        compiler_params=pltpu.CompilerParams(vmem_limit_bytes=40 * MIB),
+        compiler_params=pltpu.CompilerParams(vmem_limit_bytes=VMEM_LIMIT),
         name="gram_y",
     )(core, *mine, *others)
 
@@ -293,7 +331,7 @@
                   pl.BlockSpec((species, x_tile, rank, order), lambda i: (0, i, 0, 0))],
         out_specs=pl.BlockSpec((species, x_tile, rank, rank), lambda i: (0, i, 0, 0)),
         out_shape=jax.ShapeDtypeStruct((species, half, rank, rank), F32),
-        compiler_params=pltpu.CompilerParams(vmem_limit_bytes=24 * MIB),
+        compiler_params=pltpu.CompilerParams(vmem_limit_bytes=VMEM_LIMIT),
         name="core",
     )(basis_t, full)
 
@@ -330,17 +368,35 @@
     return current
 
 
-def send_order(gz_n, side):
-    groups = gz_n * side
-    far = [k for k in range(groups // 2, groups)]
-    near = [k for k in range(1, groups // 2)]
-    far.sort(key=lambda k: (k % (groups // 4), k))
-    order = []
-    for i, k in enumerate(far):
-        order.append(k)
-        if i < len(near):
-            order.append(near[i])
-    return order
+def exchange(field, group, groups, total):
+    half = groups // 2
+    quarter = half // 2
+    upper = group // half
+    far_pos = jnp.stack([group, 1 - upper]).astype(jnp.int32)
+    near_pos = jnp.stack([group, upper]).astype(jnp.int32)
+    far_order = sorted(range(half), key=lambda k: (k % quarter, k))
+    near_order = sorted(range(1, half), key=lambda k: ((k - 1) % quarter if k < quarter else k - quarter,
+                                                       -k))
+    recent, pieces = [], []
+    source = field
+    for s in range(field.shape[0]):
+        if s:
+            source = tie(source, recent[-PACK_AT])
+        far = pack(source, far_pos, s, half)
+        near = pack(tie(source, far[0]), near_pos, s, half)
+        got = [near[0]] + [None] * (groups - 1)
+        pieces.append(got)
+        order = []
+        for i, k in enumerate(far_order):
+            order.append((half + k, far[k]))
+            if i < len(near_order):
+                order.append((near_order[i], near[near_order[i]]))
+        for k, value in order:
+            if len(recent) >= DEPTH:
+                value = tie(value, recent[-DEPTH])
+            got[k] = permute(value, k * CORES, total)
+            recent.append(got[k])
+    return pieces
 
 
 def fast_body(field):
@@ -357,22 +413,8 @@
     one = lambda v: jnp.reshape(v, (1,)).astype(jnp.int32)
     start_t = start_table(grid_n, RANK).T
 
-    order = send_order(gz_n, side)
-    pieces, recent = [], []
+    pieces = exchange(field, group, groups, total)
     gram = jnp.zeros((grid_n, grid_n), F32)
-    source = field
-    for s in range(species):
-        if s:
-            source = tie(source, recent[-len(order) // 2])
-        sent = pack(source, one(group), s, groups)
-        got = [sent[0]] + [None] * (groups - 1)
-        for k in order:
-            value = sent[k]
-            if len(recent) >= DEPTH:
-                value = tie(value, recent[-DEPTH])
-            got[k] = permute(value, k * CORES, total)
-            recent.append(got[k])
-        pieces.append(got)
     for s in range(species):
         gram = gram_z_step(gram, pieces[s], one(group), side)
     gram = all_sum(gram, me, total, 4)
@@ -381,9 +423,9 @@
     side_pos = gy // CORES
     away = jnp.stack([1 - core, side_pos]).astype(jnp.int32)
     home = jnp.stack([core, side_pos]).astype(jnp.int32)
-    leaving = [reduce_half(turned_z, pieces[s], away, side) for s in range(species)]
+    leaving = reduce_half(turned_z, pieces, away, side)
     others = [permute(value, 1, total) for value in leaving]
-    mine = [reduce_half(turned_z, pieces[s], home, side) for s in range(species)]
+    mine = reduce_half(tie(turned_z, leaving[0]), pieces, home, side)
     full, gram = gram_y_full(mine, others, one(core), side)
     gram = all_sum(gram, me, total, 4)
     basis_y, _ = leaf_basis(gram, start_t, one(gz), 1)

time: 1830 us -> 1720 us (0.940)
  waiting for transfers between devices: 729 us -> 636 us
  local copies, waits for them, and re-layouts: 97.6 us -> 5.72 us
  starting transfers between devices: 761 us -> 824 us
  Pallas kernels: 225 us -> 244 us
    unnamed x402 -> x36, local copies, waits for them, and re-layouts: 95.8 us -> 1.67 us
    ppermute x88, waiting for transfers between devices: 729 us -> 636 us  [permute(): return lax.ppermute(value, AXES, [(i, i ^ mask) for i in range(total)])]
    ppermute x88, starting transfers between devices: 761 us -> 824 us  [permute(): return lax.ppermute(value, AXES, [(i, i ^ mask) for i in range(total)])]
    pallas_call x4 -> x8, Pallas kernels: 62.9 us -> 85.8 us  [pack(): pl.pallas_call(functools.partial(pack_kernel, groups, width), grid_spec=p...]
  transfers between devices with their start and end apart: 88 -> 88, of which waited for: 43 -> 43; matrix products, arithmetic and copies ran while one was open for 0% -> 0% of each run, Pallas kernels for 7% -> 8%
where the time goes in v2:
time: 1720 us
  starting transfers between devices  824 us (48%)
  waiting for transfers between devices  636 us (37%)
  Pallas kernels  244 us (14%)
    ppermute x88, starting transfers between devices, permute(): return lax.ppermute(value, AXES, [(i, i ^ mask) for i in range(total)])  824 us
    ppermute x88, waiting for transfers between devices, permute(): return lax.ppermute(value, AXES, [(i, i ^ mask) for i in range(total)])  636 us
    pallas_call x8, Pallas kernels, pack(): pl.pallas_call(functools.partial(pack_kernel, groups, width), grid_spec=p...  85.8 us
    pallas_call x4, Pallas kernels, gram_z_step(): pl.pallas_call(functools.partial(gram_z_kernel, groups, side), grid_spec=...  67.1 us
    pallas_call x2, Pallas kernels, leaf_basis(): pl.pallas_call(functools.partial(basis_kernel, gz_n), in_specs=[pl.BlockS...  41.2 us
  transfers between devices with their start and end apart: 88, of which 43 were waited for; matrix products, arithmetic and copies ran while one was open for 0% of the time, Pallas kernels for 8%

profile of v2, /device:TPU:0, one launch (start us, length us, event | category | flops | bytes accessed | tf_op | source)
XLA Modules:
  0.0 1721.9 jit_solution(6843396953346322068)
XLA Ops:
  1.3 10.8 pack.8
  20.1 10.7 pack.9
  32.7 75.1 %collective-permute-done.7.refs_8_ = f32[32,64,128]{2,1,0:T(8,128)S(1)} collective-permute-done((f32[32,64,128]{2,1,0:T(8,128)}, f32[32,64,128]{2,1,0:T(8,128)S(1)}, u32[]{:S(2)}, u32[]{:S(2)}) %collective-permute-start.7) | collective-permute-done | bytes 1048608 | tf_op jit(solution)/shard_map/ppermute | solution.py:340
  112.1 64.4 %collective-permute-done.8.refs_9_ = f32[32,64,128]{2,1,0:T(8,128)S(1)} collective-permute-done((f32[32,64,128]{2,1,0:T(8,128)}, f32[32,64,128]{2,1,0:T(8,128)S(1)}, u32[]{:S(2)}, u32[]{:S(2)}) %collective-permute-start.8) | collective-permute-done | bytes 1048608 | tf_op jit(solution)/shard_map/ppermute | solution.py:340
  182.0 63.5 %collective-permute-start.5 = (f32[32,64,128]{2,1,0:T(8,128)}, f32[32,64,128]{2,1,0:T(8,128)}, u32[]{:S(2)}, u32[]{:S(2)}) collective-permute-start(f32[32,64,128]{2,1,0:T(8,128)} %get-tuple-element.153), channel_id=1, source_target_pairs={{0,12},{1,13},{2,14},{3,15},{4,8},{5,9},{6,10},{7,11},{8,4},{9,5},... | collective-permute-start | bytes 3145736 | tf_op jit(solution)/shard_map/ppermute | solution.py:340
  245.5 21.1 %collective-permute-done.10.refs_10_ = f32[32,64,128]{2,1,0:T(8,128)} collective-permute-done((f32[32,64,128]{2,1,0:T(8,128)}, f32[32,64,128]{2,1,0:T(8,128)}, u32[]{:S(2)}, u32[]{:S(2)}) %collective-permute-start.10) | collective-permute-done | bytes 1048608 | tf_op jit(solution)/shard_map/ppermute | solution.py:340
  267.1 10.7 pack.10
  280.8 10.7 pack.11
  291.5 59.1 %collective-permute-start.16 = (f32[32,64,128]{2,1,0:T(8,128)}, f32[32,64,128]{2,1,0:T(8,128)S(1)}, u32[]{:S(2)}, u32[]{:S(2)}) collective-permute-start(f32[32,64,128]{2,1,0:T(8,128)} %get-tuple-element.176), channel_id=1, source_target_pairs={{0,8},{1,9},{2,10},{3,11},{4,12},{5,13},{6,14},{7,15},{8,0},{9,1},... | collective-permute-start | bytes 3145736 | tf_op jit(solution)/shard_map/ppermute | solution.py:340
  352.2 7.2 collective-permute-done.12.refs_11_
  360.7 42.5 %collective-permute-done.16.refs_4_.refs_20_ = f32[32,64,128]{2,1,0:T(8,128)S(1)} collective-permute-done((f32[32,64,128]{2,1,0:T(8,128)}, f32[32,64,128]{2,1,0:T(8,128)S(1)}, u32[]{:S(2)}, u32[]{:S(2)}) %collective-permute-start.16) | collective-permute-done | bytes 1048608 | tf_op jit(solution)/shard_map/ppermute | solution.py:340
  403.2 6.2 collective-permute-start.18
  411.2 14.6 collective-permute-done.6.refs_7_
  425.8 28.1 %collective-permute-start.25 = (f32[32,64,128]{2,1,0:T(8,128)}, f32[32,64,128]{2,1,0:T(8,128)}, u32[]{:S(2)}, u32[]{:S(2)}) collective-permute-start(f32[32,64,128]{2,1,0:T(8,128)} %get-tuple-element.192), channel_id=1, source_target_pairs={{0,20},{1,21},{2,22},{3,23},{4,16},{5,17},{6,18},{7,19},{8,28},{9,... | collective-permute-start | bytes 3145736 | tf_op jit(solution)/shard_map/ppermute | solution.py:340
  454.0 42.4 %collective-permute-done.22.refs_8_.refs_24_ = f32[32,64,128]{2,1,0:T(8,128)} collective-permute-done((f32[32,64,128]{2,1,0:T(8,128)}, f32[32,64,128]{2,1,0:T(8,128)}, u32[]{:S(2)}, u32[]{:S(2)}) %collective-permute-start.22) | collective-permute-done | bytes 1048608 | tf_op jit(solution)/shard_map/ppermute | solution.py:340
  496.3 27.5 %collective-permute-start.26 = (f32[32,64,128]{2,1,0:T(8,128)}, f32[32,64,128]{2,1,0:T(8,128)}, u32[]{:S(2)}, u32[]{:S(2)}) collective-permute-start(f32[32,64,128]{2,1,0:T(8,128)} %get-tuple-element.195), channel_id=1, source_target_pairs={{0,26},{1,27},{2,24},{3,25},{4,30},{5,31},{6,28},{7,29},{8,18},{9,... | collective-permute-start | bytes 3145736 | tf_op jit(solution)/shard_map/ppermute | solution.py:340
  524.6 52.6 %collective-permute-start.21 = (f32[32,64,128]{2,1,0:T(8,128)}, f32[32,64,128]{2,1,0:T(8,128)}, u32[]{:S(2)}, u32[]{:S(2)}) collective-permute-start(f32[32,64,128]{2,1,0:T(8,128)} %get-tuple-element.185), channel_id=1, source_target_pairs={{0,14},{1,15},{2,12},{3,13},{4,10},{5,11},{6,8},{7,9},{8,6},{9,7},... | collective-permute-start | bytes 3145736 | tf_op jit(solution)/shard_map/ppermute | solution.py:340
  577.2 9.4 collective-permute-done.23.refs_9_.refs_25_
  586.6 13.5 collective-permute-start.29
  607.2 63.0 %collective-permute-start.27 = (f32[32,64,128]{2,1,0:T(8,128)}, f32[32,64,128]{2,1,0:T(8,128)}, u32[]{:S(2)}, u32[]{:S(2)}) collective-permute-start(f32[32,64,128]{2,1,0:T(8,128)} %get-tuple-element.196), channel_id=1, source_target_pairs={{0,22},{1,23},{2,20},{3,21},{4,18},{5,19},{6,16},{7,17},{8,30},{9,... | collective-permute-start | bytes 3145736 | tf_op jit(solution)/shard_map/ppermute | solution.py:340
  670.2 10.7 pack.12
  681.1 20.7 %collective-permute-start.39 = (f32[32,64,128]{2,1,0:T(8,128)}, f32[32,64,128]{2,1,0:T(8,128)S(1)}, u32[]{:S(2)}, u32[]{:S(2)}) collective-permute-start(f32[32,64,128]{2,1,0:T(8,128)} %get-tuple-element.224), channel_id=1, source_target_pairs={{0,24},{1,25},{2,26},{3,27},{4,28},{5,29},{6,30},{7,31},{8,16},{9,... | collective-permute-start | bytes 3145736 | tf_op jit(solution)/shard_map/ppermute | solution.py:340
  701.7 71.1 %collective-permute-start.38 = (f32[32,64,128]{2,1,0:T(8,128)}, f32[32,64,128]{2,1,0:T(8,128)}, u32[]{:S(2)}, u32[]{:S(2)}) collective-permute-start(f32[32,64,128]{2,1,0:T(8,128)} %get-tuple-element.221), channel_id=1, source_target_pairs={{0,18},{1,19},{2,16},{3,17},{4,22},{5,23},{6,20},{7,21},{8,26},{9,... | collective-permute-start | bytes 3145736 | tf_op jit(solution)/shard_map/ppermute | solution.py:340
  772.8 10.7 pack.13
  783.5 32.5 %collective-permute-start.33 = (f32[32,64,128]{2,1,0:T(8,128)}, f32[32,64,128]{2,1,0:T(8,128)}, u32[]{:S(2)}, u32[]{:S(2)}) collective-permute-start(f32[32,64,128]{2,1,0:T(8,128)} %get-tuple-element.213), channel_id=1, source_target_pairs={{0,10},{1,11},{2,8},{3,9},{4,14},{5,15},{6,12},{7,13},{8,2},{9,3},... | collective-permute-start | bytes 3145736 | tf_op jit(solution)/shard_map/ppermute | solution.py:340
  816.0 13.9 collective-permute-done.27.refs_11_.refs_27_
  829.9 8.4 collective-permute-start.31
  838.3 14.0 collective-permute-done.37.refs_8_.refs_40_
  854.0 11.0 collective-permute-start.41
  865.0 56.0 %collective-permute-done.38.refs_9_.refs_41_ = f32[32,64,128]{2,1,0:T(8,128)} collective-permute-done((f32[32,64,128]{2,1,0:T(8,128)}, f32[32,64,128]{2,1,0:T(8,128)}, u32[]{:S(2)}, u32[]{:S(2)}) %collective-permute-start.38) | collective-permute-done | bytes 1048608 | tf_op jit(solution)/shard_map/ppermute | solution.py:340
  921.0 33.0 %collective-permute-start.43 = (f32[32,64,128]{2,1,0:T(8,128)}, f32[32,64,128]{2,1,0:T(8,128)}, u32[]{:S(2)}, u32[]{:S(2)}) collective-permute-start(f32[32,64,128]{2,1,0:T(8,128)} %get-tuple-element.231), channel_id=1, source_target_pairs={{0,28},{1,29},{2,30},{3,31},{4,24},{5,25},{6,26},{7,27},{8,20},{9,... | collective-permute-start | bytes 3145736 | tf_op jit(solution)/shard_map/ppermute | solution.py:340
  956.2 39.1 %collective-permute-start.35 = (f32[32,64,128]{2,1,0:T(8,128)}, f32[32,64,128]{2,1,0:T(8,128)}, u32[]{:S(2)}, u32[]{:S(2)}) collective-permute-start(f32[32,64,128]{2,1,0:T(8,128)} %get-tuple-element.216), channel_id=1, source_target_pairs={{0,12},{1,13},{2,14},{3,15},{4,8},{5,9},{6,10},{7,11},{8,4},{9,5},... | collective-permute-start | bytes 3145736 | tf_op jit(solution)/shard_map/ppermute | solution.py:340
  995.3 22.0 %collective-permute-done.40.refs_10_.refs_42_ = f32[32,64,128]{2,1,0:T(8,128)} collective-permute-done((f32[32,64,128]{2,1,0:T(8,128)}, f32[32,64,128]{2,1,0:T(8,128)}, u32[]{:S(2)}, u32[]{:S(2)}) %collective-permute-start.40) | collective-permute-done | bytes 1048608 | tf_op jit(solution)/shard_map/ppermute | solution.py:340
  1017.3 8.3 collective-permute-start.44
  1025.6 10.8 pack.14
  1036.3 10.8 pack.15
  1047.2 21.8 %collective-permute-start.46 = (f32[32,64,128]{2,1,0:T(8,128)}, f32[32,64,128]{2,1,0:T(8,128)S(1)}, u32[]{:S(2)}, u32[]{:S(2)}) collective-permute-start(f32[32,64,128]{2,1,0:T(8,128)} %get-tuple-element.242), channel_id=1, source_target_pairs={{0,8},{1,9},{2,10},{3,11},{4,12},{5,13},{6,14},{7,15},{8,0},{9,1},... | collective-permute-start | bytes 3145736 | tf_op jit(solution)/shard_map/ppermute | solution.py:340
  1077.4 14.8 collective-permute-start.54
  1094.8 5.3 collective-permute-done.46.refs_4_.refs_52_
  1100.0 58.6 %collective-permute-done.42.refs_11_.refs_43_ = f32[32,64,128]{2,1,0:T(8,128)S(1)} collective-permute-done((f32[32,64,128]{2,1,0:T(8,128)S(1)}, f32[32,64,128]{2,1,0:T(8,128)S(1)}, u32[]{:S(2)}, u32[]{:S(2)}) %collective-permute-start.42) | collective-permute-done | bytes 1048608 | tf_op jit(solution)/shard_map/ppermute | solution.py:340
  1162.5 45.2 %collective-permute-start.55 = (f32[32,64,128]{2,1,0:T(8,128)}, f32[32,64,128]{2,1,0:T(8,128)}, u32[]{:S(2)}, u32[]{:S(2)}) collective-permute-start(f32[32,64,128]{2,1,0:T(8,128)} %get-tuple-element.258), channel_id=1, source_target_pairs={{0,20},{1,21},{2,22},{3,23},{4,16},{5,17},{6,18},{7,19},{8,28},{9,... | collective-permute-start | bytes 3145736 | tf_op jit(solution)/shard_map/ppermute | solution.py:340
  1207.7 40.2 %collective-permute-done.52.refs_8_.refs_56_ = f32[32,64,128]{2,1,0:T(8,128)} collective-permute-done((f32[32,64,128]{2,1,0:T(8,128)}, f32[32,64,128]{2,1,0:T(8,128)}, u32[]{:S(2)}, u32[]{:S(2)}) %collective-permute-start.52) | collective-permute-done | bytes 1048608 | tf_op jit(solution)/shard_map/ppermute | solution.py:340
  1248.5 37.2 %collective-permute-start.56 = (f32[32,64,128]{2,1,0:T(8,128)}, f32[32,64,128]{2,1,0:T(8,128)}, u32[]{:S(2)}, u32[]{:S(2)}) collective-permute-start(f32[32,64,128]{2,1,0:T(8,128)} %get-tuple-element.261), channel_id=1, source_target_pairs={{0,26},{1,27},{2,24},{3,25},{4,30},{5,31},{6,28},{7,29},{8,18},{9,... | collective-permute-start | bytes 3145736 | tf_op jit(solution)/shard_map/ppermute | solution.py:340
  1286.8 16.9 gram_z.4.prev_ref
  1306.8 23.9 %collective-permute-start.50 = (f32[32,64,128]{2,1,0:T(8,128)}, f32[32,64,128]{2,1,0:T(8,128)S(1)}, u32[]{:S(2)}, u32[]{:S(2)}) collective-permute-start(f32[32,64,128]{2,1,0:T(8,128)} %get-tuple-element.249), channel_id=1, source_target_pairs={{0,12},{1,13},{2,14},{3,15},{4,8},{5,9},{6,10},{7,11},{8,4},{9,5},... | collective-permute-start | bytes 3145736 | tf_op jit(solution)/shard_map/ppermute | solution.py:340
  1330.8 11.4 collective-permute-done.53.refs_9_.refs_57_
  1342.2 15.4 collective-permute-start.59
  1357.6 25.9 %collective-permute-done.49.refs_3_.refs_51_ = f32[32,64,128]{2,1,0:T(8,128)} collective-permute-done((f32[32,64,128]{2,1,0:T(8,128)}, f32[32,64,128]{2,1,0:T(8,128)}, u32[]{:S(2)}, u32[]{:S(2)}) %collective-permute-start.49) | collective-permute-done | bytes 1048608 | tf_op jit(solution)/shard_map/ppermute | solution.py:340
  1383.5 40.6 %collective-permute-start.57 = (f32[32,64,128]{2,1,0:T(8,128)}, f32[32,64,128]{2,1,0:T(8,128)}, u32[]{:S(2)}, u32[]{:S(2)}) collective-permute-start(f32[32,64,128]{2,1,0:T(8,128)} %get-tuple-element.262), channel_id=1, source_target_pairs={{0,22},{1,23},{2,20},{3,21},{4,18},{5,19},{6,16},{7,17},{8,30},{9,... | collective-permute-start | bytes 3145736 | tf_op jit(solution)/shard_map/ppermute | solution.py:340
  1424.1 16.7 gram_z.5.prev_ref
  1440.8 16.8 gram_z.6.prev_ref
  1457.7 38.1 %collective-permute-done.57.refs_11_.refs_59_ = f32[32,64,128]{2,1,0:T(8,128)} collective-permute-done((f32[32,64,128]{2,1,0:T(8,128)}, f32[32,64,128]{2,1,0:T(8,128)}, u32[]{:S(2)}, u32[]{:S(2)}) %collective-permute-start.57) | collective-permute-done | bytes 1048608 | tf_op jit(solution)/shard_map/ppermute | solution.py:340
  1495.8 16.8 gram_z.7
  1517.9 7.8 collective-permute-done.61
  1533.2 11.9 collective-permute-start.63
  1567.8 5.4 collective-permute-done.70
  1576.4 20.7 %leaf_basis.2 = (f32[64,512]{1,0:T(8,128)}, f32[64,512]{1,0:T(8,128)}) custom-call(s32[1]{0:T(128)} %bitcast.me_ref, f32[512,512]{1,0:T(8,128)} %pad_maximum_fusion.gram_ref, f32[64,512]{1,0:T(8,128)} %multiply_cosine_fusion.start_ref), custom_call_target="tpu_custom_call" | custom-call | tf_op jit(solution)/shard_map/leaf_basis/pallas_call | solution.py:206
  1597.2 16.3 reduce_z.2
  1614.5 16.3 reduce_z.3
  1632.5 10.8 gram_y.1
  1649.0 7.6 collective-permute-done.77
  1683.1 5.4 collective-permute-done.86
  1691.6 20.5 %leaf_basis.3 = (f32[64,512]{1,0:T(8,128)}, f32[64,512]{1,0:T(8,128)}) custom-call(s32[1]{0:T(128)} %bitcast.me_ref, f32[512,512]{1,0:T(8,128)} %pad_maximum_fusion.1.gram_ref, f32[64,512]{1,0:T(8,128)} %multiply_cosine_fusion.start_ref), custom_call_target="tpu_custom_call" | custom-call | tf_op jit(solution)/shard_map/leaf_basis/pallas_call | solution.py:206
  1712.1 6.9 core.1
  (207 shorter events, 139.6 us)
Async XLA Ops:
  12.1 95.7 %collective-permute-start.7 = (f32[32,64,128]{2,1,0:T(8,128)}, f32[32,64,128]{2,1,0:T(8,128)S(1)}, u32[]{:S(2)}, u32[]{:S(2)}) collective-permute-start(f32[32,64,128]{2,1,0:T(8,128)} %get-tuple-element.142), channel_id=1, source_target_pairs={{0,16},{1,17},{2,18},{3,19},{4,20},{5,21},{6,22},{7,23},{8,24},{9,... | collective-permute-start | bytes 3145736 | tf_op jit(solution)/shard_map/ppermute | solution.py:340
  16.1 93.5 %collective-permute-start.9 = (f32[32,64,128]{2,1,0:T(8,128)}, f32[32,64,128]{2,1,0:T(8,128)S(1)}, u32[]{:S(2)}, u32[]{:S(2)}) collective-permute-start(f32[32,64,128]{2,1,0:T(8,128)} %get-tuple-element.158), channel_id=1, source_target_pairs={{0,24},{1,25},{2,26},{3,27},{4,28},{5,29},{6,30},{7,31},{8,16},{9,... | collective-permute-start | bytes 3145736 | tf_op jit(solution)/shard_map/ppermute | solution.py:340
  17.4 159.0 %collective-permute-start.8 = (f32[32,64,128]{2,1,0:T(8,128)}, f32[32,64,128]{2,1,0:T(8,128)S(1)}, u32[]{:S(2)}, u32[]{:S(2)}) collective-permute-start(f32[32,64,128]{2,1,0:T(8,128)} %get-tuple-element.156), channel_id=1, source_target_pairs={{0,18},{1,19},{2,16},{3,17},{4,22},{5,23},{6,20},{7,21},{8,26},{9,... | collective-permute-start | bytes 3145736 | tf_op jit(solution)/shard_map/ppermute | solution.py:340
  30.7 145.8 %collective-permute-start.3 = (f32[32,64,128]{2,1,0:T(8,128)}, f32[32,64,128]{2,1,0:T(8,128)}, u32[]{:S(2)}, u32[]{:S(2)}) collective-permute-start(f32[32,64,128]{2,1,0:T(8,128)} %get-tuple-element.150), channel_id=1, source_target_pairs={{0,10},{1,11},{2,8},{3,9},{4,14},{5,15},{6,12},{7,13},{8,2},{9,3},... | collective-permute-start | bytes 3145736 | tf_op jit(solution)/shard_map/ppermute | solution.py:340
  32.1 147.9 %collective-permute-start.1 = (f32[32,64,128]{2,1,0:T(8,128)}, f32[32,64,128]{2,1,0:T(8,128)}, u32[]{:S(2)}, u32[]{:S(2)}) collective-permute-start(f32[32,64,128]{2,1,0:T(8,128)} %get-tuple-element.147), channel_id=1, source_target_pairs={{0,8},{1,9},{2,10},{3,11},{4,12},{5,13},{6,14},{7,15},{8,0},{9,1},... | collective-permute-start | bytes 3145736 | tf_op jit(solution)/shard_map/ppermute | solution.py:340
  107.8 73.2 %collective-permute-start = (f32[32,64,128]{2,1,0:T(8,128)}, f32[32,64,128]{2,1,0:T(8,128)}, u32[]{:S(2)}, u32[]{:S(2)}) collective-permute-start(f32[32,64,128]{2,1,0:T(8,128)} %get-tuple-element.145), channel_id=1, source_target_pairs={{0,2},{1,3},{2,0},{3,1},{4,6},{5,7},{6,4},{7,5},{8,10},{9,11},{10,... | collective-permute-start | bytes 3145736 | tf_op jit(solution)/shard_map/ppermute | solution.py:340
  109.6 72.4 %collective-permute-start.11 = (f32[32,64,128]{2,1,0:T(8,128)}, f32[32,64,128]{2,1,0:T(8,128)}, u32[]{:S(2)}, u32[]{:S(2)}) collective-permute-start(f32[32,64,128]{2,1,0:T(8,128)} %get-tuple-element.162), channel_id=1, source_target_pairs={{0,26},{1,27},{2,24},{3,25},{4,30},{5,31},{6,28},{7,29},{8,18},{9,... | collective-permute-start | bytes 3145736 | tf_op jit(solution)/shard_map/ppermute | solution.py:340
  176.5 90.2 %collective-permute-start.10 = (f32[32,64,128]{2,1,0:T(8,128)}, f32[32,64,128]{2,1,0:T(8,128)}, u32[]{:S(2)}, u32[]{:S(2)}) collective-permute-start(f32[32,64,128]{2,1,0:T(8,128)} %get-tuple-element.159), channel_id=1, source_target_pairs={{0,20},{1,21},{2,22},{3,23},{4,16},{5,17},{6,18},{7,19},{8,28},{9,... | collective-permute-start | bytes 3145736 | tf_op jit(solution)/shard_map/ppermute | solution.py:340
  176.5 101.3 %collective-permute-start.13 = (f32[32,64,128]{2,1,0:T(8,128)}, f32[32,64,128]{2,1,0:T(8,128)}, u32[]{:S(2)}, u32[]{:S(2)}) collective-permute-start(f32[32,64,128]{2,1,0:T(8,128)} %get-tuple-element.165), channel_id=1, source_target_pairs={{0,28},{1,29},{2,30},{3,31},{4,24},{5,25},{6,26},{7,27},{8,20},{9,... | collective-permute-start | bytes 3145736 | tf_op jit(solution)/shard_map/ppermute | solution.py:340
  180.0 111.5 %collective-permute-start.4 = (f32[32,64,128]{2,1,0:T(8,128)}, f32[32,64,128]{2,1,0:T(8,128)}, u32[]{:S(2)}, u32[]{:S(2)}) collective-permute-start(f32[32,64,128]{2,1,0:T(8,128)} %get-tuple-element.151), channel_id=1, source_target_pairs={{0,6},{1,7},{2,4},{3,5},{4,2},{5,3},{6,0},{7,1},{8,14},{9,15},{10,... | collective-permute-start | bytes 3145736 | tf_op jit(solution)/shard_map/ppermute | solution.py:340
  181.0 169.6 %collective-permute-start.2 = (f32[32,64,128]{2,1,0:T(8,128)}, f32[32,64,128]{2,1,0:T(8,128)}, u32[]{:S(2)}, u32[]{:S(2)}) collective-permute-start(f32[32,64,128]{2,1,0:T(8,128)} %get-tuple-element.148), channel_id=1, source_target_pairs={{0,4},{1,5},{2,6},{3,7},{4,0},{5,1},{6,2},{7,3},{8,12},{9,13},{10,... | collective-permute-start | bytes 3145736 | tf_op jit(solution)/shard_map/ppermute | solution.py:340
  182.0 170.2 %collective-permute-start.5 = (f32[32,64,128]{2,1,0:T(8,128)}, f32[32,64,128]{2,1,0:T(8,128)}, u32[]{:S(2)}, u32[]{:S(2)}) collective-permute-start(f32[32,64,128]{2,1,0:T(8,128)} %get-tuple-element.153), channel_id=1, source_target_pairs={{0,12},{1,13},{2,14},{3,15},{4,8},{5,9},{6,10},{7,11},{8,4},{9,5},... | collective-permute-start | bytes 3145736 | tf_op jit(solution)/shard_map/ppermute | solution.py:340
  266.7 92.8 %collective-permute-start.12 = (f32[32,64,128]{2,1,0:T(8,128)}, f32[32,64,128]{2,1,0:T(8,128)}, u32[]{:S(2)}, u32[]{:S(2)}) collective-permute-start(f32[32,64,128]{2,1,0:T(8,128)} %get-tuple-element.163), channel_id=1, source_target_pairs={{0,22},{1,23},{2,20},{3,21},{4,18},{5,19},{6,16},{7,17},{8,30},{9,... | collective-permute-start | bytes 3145736 | tf_op jit(solution)/shard_map/ppermute | solution.py:340
  277.8 81.7 %collective-permute-start.14 = (f32[32,64,128]{2,1,0:T(8,128)}, f32[32,64,128]{2,1,0:T(8,128)S(1)}, u32[]{:S(2)}, u32[]{:S(2)}) collective-permute-start(f32[32,64,128]{2,1,0:T(8,128)} %get-tuple-element.167), channel_id=1, source_target_pairs={{0,30},{1,31},{2,28},{3,29},{4,26},{5,27},{6,24},{7,25},{8,22},{9,... | collective-permute-start | bytes 3145736 | tf_op jit(solution)/shard_map/ppermute | solution.py:340
  291.5 111.7 %collective-permute-start.16 = (f32[32,64,128]{2,1,0:T(8,128)}, f32[32,64,128]{2,1,0:T(8,128)S(1)}, u32[]{:S(2)}, u32[]{:S(2)}) collective-permute-start(f32[32,64,128]{2,1,0:T(8,128)} %get-tuple-element.176), channel_id=1, source_target_pairs={{0,8},{1,9},{2,10},{3,11},{4,12},{5,13},{6,14},{7,15},{8,0},{9,1},... | collective-permute-start | bytes 3145736 | tf_op jit(solution)/shard_map/ppermute | solution.py:340
  350.6 58.8 %collective-permute-start.24 = (f32[32,64,128]{2,1,0:T(8,128)}, f32[32,64,128]{2,1,0:T(8,128)}, u32[]{:S(2)}, u32[]{:S(2)}) collective-permute-start(f32[32,64,128]{2,1,0:T(8,128)} %get-tuple-element.191), channel_id=1, source_target_pairs={{0,24},{1,25},{2,26},{3,27},{4,28},{5,29},{6,30},{7,31},{8,16},{9,... | collective-permute-start | bytes 3145736 | tf_op jit(solution)/shard_map/ppermute | solution.py:340
  352.2 73.6 %collective-permute-start.6 = (f32[32,64,128]{2,1,0:T(8,128)S(1)}, f32[32,64,128]{2,1,0:T(8,128)}, u32[]{:S(2)}, u32[]{:S(2)}) collective-permute-start(f32[32,64,128]{2,1,0:T(8,128)S(1)} %copy-done.17), channel_id=1, source_target_pairs={{0,14},{1,15},{2,12},{3,13},{4,10},{5,11},{6,8},{7,9},{8,6},{9,7},... | collective-permute-start | bytes 3145736 | tf_op jit(solution)/shard_map/ppermute | solution.py:340
  359.5 136.9 %collective-permute-start.22 = (f32[32,64,128]{2,1,0:T(8,128)}, f32[32,64,128]{2,1,0:T(8,128)}, u32[]{:S(2)}, u32[]{:S(2)}) collective-permute-start(f32[32,64,128]{2,1,0:T(8,128)} %get-tuple-element.186), channel_id=1, source_target_pairs={{0,16},{1,17},{2,18},{3,19},{4,20},{5,21},{6,22},{7,23},{8,24},{9,... | collective-permute-start | bytes 3145736 | tf_op jit(solution)/shard_map/ppermute | solution.py:340
  359.5 136.8 %collective-permute-start.15 = (f32[32,64,128]{2,1,0:T(8,128)}, f32[32,64,128]{2,1,0:T(8,128)}, u32[]{:S(2)}, u32[]{:S(2)}) collective-permute-start(f32[32,64,128]{2,1,0:T(8,128)} %get-tuple-element.173), channel_id=1, source_target_pairs={{0,2},{1,3},{2,0},{3,1},{4,6},{5,7},{6,4},{7,5},{8,10},{9,11},{10,... | collective-permute-start | bytes 3145736 | tf_op jit(solution)/shard_map/ppermute | solution.py:340
  403.2 120.7 %collective-permute-start.18 = (f32[32,64,128]{2,1,0:T(8,128)}, f32[32,64,128]{2,1,0:T(8,128)}, u32[]{:S(2)}, u32[]{:S(2)}) collective-permute-start(f32[32,64,128]{2,1,0:T(8,128)} %get-tuple-element.180), channel_id=1, source_target_pairs={{0,10},{1,11},{2,8},{3,9},{4,14},{5,15},{6,12},{7,13},{8,2},{9,3},... | collective-permute-start | bytes 3145736 | tf_op jit(solution)/shard_map/ppermute | solution.py:340
  409.4 114.8 %collective-permute-start.17 = (f32[32,64,128]{2,1,0:T(8,128)}, f32[32,64,128]{2,1,0:T(8,128)}, u32[]{:S(2)}, u32[]{:S(2)}) collective-permute-start(f32[32,64,128]{2,1,0:T(8,128)} %get-tuple-element.177), channel_id=1, source_target_pairs={{0,4},{1,5},{2,6},{3,7},{4,0},{5,1},{6,2},{7,3},{8,12},{9,13},{10,... | collective-permute-start | bytes 3145736 | tf_op jit(solution)/shard_map/ppermute | solution.py:340
  425.8 98.7 %collective-permute-start.25 = (f32[32,64,128]{2,1,0:T(8,128)}, f32[32,64,128]{2,1,0:T(8,128)}, u32[]{:S(2)}, u32[]{:S(2)}) collective-permute-start(f32[32,64,128]{2,1,0:T(8,128)} %get-tuple-element.192), channel_id=1, source_target_pairs={{0,20},{1,21},{2,22},{3,23},{4,16},{5,17},{6,18},{7,19},{8,28},{9,... | collective-permute-start | bytes 3145736 | tf_op jit(solution)/shard_map/ppermute | solution.py:340
  496.3 90.3 %collective-permute-start.23 = (f32[32,64,128]{2,1,0:T(8,128)}, f32[32,64,128]{2,1,0:T(8,128)}, u32[]{:S(2)}, u32[]{:S(2)}) collective-permute-start(f32[32,64,128]{2,1,0:T(8,128)} %get-tuple-element.188), channel_id=1, source_target_pairs={{0,18},{1,19},{2,16},{3,17},{4,22},{5,23},{6,20},{7,21},{8,26},{9,... | collective-permute-start | bytes 3145736 | tf_op jit(solution)/shard_map/ppermute | solution.py:340
  496.3 103.8 %collective-permute-start.26 = (f32[32,64,128]{2,1,0:T(8,128)}, f32[32,64,128]{2,1,0:T(8,128)}, u32[]{:S(2)}, u32[]{:S(2)}) collective-permute-start(f32[32,64,128]{2,1,0:T(8,128)} %get-tuple-element.195), channel_id=1, source_target_pairs={{0,26},{1,27},{2,24},{3,25},{4,30},{5,31},{6,28},{7,29},{8,18},{9,... | collective-permute-start | bytes 3145736 | tf_op jit(solution)/shard_map/ppermute | solution.py:340
  523.8 83.3 %collective-permute-start.20 = (f32[32,64,128]{2,1,0:T(8,128)}, f32[32,64,128]{2,1,0:T(8,128)}, u32[]{:S(2)}, u32[]{:S(2)}) collective-permute-start(f32[32,64,128]{2,1,0:T(8,128)} %get-tuple-element.183), channel_id=1, source_target_pairs={{0,12},{1,13},{2,14},{3,15},{4,8},{5,9},{6,10},{7,11},{8,4},{9,5},... | collective-permute-start | bytes 3145736 | tf_op jit(solution)/shard_map/ppermute | solution.py:340
  524.1 156.7 %collective-permute-start.19 = (f32[32,64,128]{2,1,0:T(8,128)}, f32[32,64,128]{2,1,0:T(8,128)S(1)}, u32[]{:S(2)}, u32[]{:S(2)}) collective-permute-start(f32[32,64,128]{2,1,0:T(8,128)} %get-tuple-element.181), channel_id=1, source_target_pairs={{0,6},{1,7},{2,4},{3,5},{4,2},{5,3},{6,0},{7,1},{8,14},{9,15},{10,... | collective-permute-start | bytes 3145736 | tf_op jit(solution)/shard_map/ppermute | solution.py:340
  524.6 156.5 %collective-permute-start.21 = (f32[32,64,128]{2,1,0:T(8,128)}, f32[32,64,128]{2,1,0:T(8,128)}, u32[]{:S(2)}, u32[]{:S(2)}) collective-permute-start(f32[32,64,128]{2,1,0:T(8,128)} %get-tuple-element.185), channel_id=1, source_target_pairs={{0,14},{1,15},{2,12},{3,13},{4,10},{5,11},{6,8},{7,9},{8,6},{9,7},... | collective-permute-start | bytes 3145736 | tf_op jit(solution)/shard_map/ppermute | solution.py:340
  586.6 115.1 %collective-permute-start.29 = (f32[32,64,128]{2,1,0:T(8,128)}, f32[32,64,128]{2,1,0:T(8,128)}, u32[]{:S(2)}, u32[]{:S(2)}) collective-permute-start(f32[32,64,128]{2,1,0:T(8,128)} %get-tuple-element.200), channel_id=1, source_target_pairs={{0,30},{1,31},{2,28},{3,29},{4,26},{5,27},{6,24},{7,25},{8,22},{9,... | collective-permute-start | bytes 3145736 | tf_op jit(solution)/shard_map/ppermute | solution.py:340
  600.1 183.4 %collective-permute-start.28 = (f32[32,64,128]{2,1,0:T(8,128)}, f32[32,64,128]{2,1,0:T(8,128)}, u32[]{:S(2)}, u32[]{:S(2)}) collective-permute-start(f32[32,64,128]{2,1,0:T(8,128)} %get-tuple-element.198), channel_id=1, source_target_pairs={{0,28},{1,29},{2,30},{3,31},{4,24},{5,25},{6,26},{7,27},{8,20},{9,... | collective-permute-start | bytes 3145736 | tf_op jit(solution)/shard_map/ppermute | solution.py:340
  607.2 222.7 %collective-permute-start.27 = (f32[32,64,128]{2,1,0:T(8,128)}, f32[32,64,128]{2,1,0:T(8,128)}, u32[]{:S(2)}, u32[]{:S(2)}) collective-permute-start(f32[32,64,128]{2,1,0:T(8,128)} %get-tuple-element.196), channel_id=1, source_target_pairs={{0,22},{1,23},{2,20},{3,21},{4,18},{5,19},{6,16},{7,17},{8,30},{9,... | collective-permute-start | bytes 3145736 | tf_op jit(solution)/shard_map/ppermute | solution.py:340
  680.9 171.4 %collective-permute-start.37 = (f32[32,64,128]{2,1,0:T(8,128)}, f32[32,64,128]{2,1,0:T(8,128)S(1)}, u32[]{:S(2)}, u32[]{:S(2)}) collective-permute-start(f32[32,64,128]{2,1,0:T(8,128)} %get-tuple-element.219), channel_id=1, source_target_pairs={{0,16},{1,17},{2,18},{3,19},{4,20},{5,21},{6,22},{7,23},{8,24},{9,... | collective-permute-start | bytes 3145736 | tf_op jit(solution)/shard_map/ppermute | solution.py:340
  681.1 172.9 %collective-permute-start.39 = (f32[32,64,128]{2,1,0:T(8,128)}, f32[32,64,128]{2,1,0:T(8,128)S(1)}, u32[]{:S(2)}, u32[]{:S(2)}) collective-permute-start(f32[32,64,128]{2,1,0:T(8,128)} %get-tuple-element.224), channel_id=1, source_target_pairs={{0,24},{1,25},{2,26},{3,27},{4,28},{5,29},{6,30},{7,31},{8,16},{9,... | collective-permute-start | bytes 3145736 | tf_op jit(solution)/shard_map/ppermute | solution.py:340
  701.7 219.2 %collective-permute-start.38 = (f32[32,64,128]{2,1,0:T(8,128)}, f32[32,64,128]{2,1,0:T(8,128)}, u32[]{:S(2)}, u32[]{:S(2)}) collective-permute-start(f32[32,64,128]{2,1,0:T(8,128)} %get-tuple-element.221), channel_id=1, source_target_pairs={{0,18},{1,19},{2,16},{3,17},{4,22},{5,23},{6,20},{7,21},{8,26},{9,... | collective-permute-start | bytes 3145736 | tf_op jit(solution)/shard_map/ppermute | solution.py:340
  783.5 137.5 %collective-permute-start.33 = (f32[32,64,128]{2,1,0:T(8,128)}, f32[32,64,128]{2,1,0:T(8,128)}, u32[]{:S(2)}, u32[]{:S(2)}) collective-permute-start(f32[32,64,128]{2,1,0:T(8,128)} %get-tuple-element.213), channel_id=1, source_target_pairs={{0,10},{1,11},{2,8},{3,9},{4,14},{5,15},{6,12},{7,13},{8,2},{9,3},... | collective-permute-start | bytes 3145736 | tf_op jit(solution)/shard_map/ppermute | solution.py:340
  829.9 124.1 %collective-permute-start.31 = (f32[32,64,128]{2,1,0:T(8,128)}, f32[32,64,128]{2,1,0:T(8,128)}, u32[]{:S(2)}, u32[]{:S(2)}) collective-permute-start(f32[32,64,128]{2,1,0:T(8,128)} %get-tuple-element.209), channel_id=1, source_target_pairs={{0,8},{1,9},{2,10},{3,11},{4,12},{5,13},{6,14},{7,15},{8,0},{9,1},... | collective-permute-start | bytes 3145736 | tf_op jit(solution)/shard_map/ppermute | solution.py:340
  852.3 103.6 %collective-permute-start.30 = (f32[32,64,128]{2,1,0:T(8,128)}, f32[32,64,128]{2,1,0:T(8,128)}, u32[]{:S(2)}, u32[]{:S(2)}) collective-permute-start(f32[32,64,128]{2,1,0:T(8,128)} %get-tuple-element.206), channel_id=1, source_target_pairs={{0,2},{1,3},{2,0},{3,1},{4,6},{5,7},{6,4},{7,5},{8,10},{9,11},{10,... | collective-permute-start | bytes 3145736 | tf_op jit(solution)/shard_map/ppermute | solution.py:340
  854.0 102.2 %collective-permute-start.41 = (f32[32,64,128]{2,1,0:T(8,128)}, f32[32,64,128]{2,1,0:T(8,128)}, u32[]{:S(2)}, u32[]{:S(2)}) collective-permute-start(f32[32,64,128]{2,1,0:T(8,128)} %get-tuple-element.228), channel_id=1, source_target_pairs={{0,26},{1,27},{2,24},{3,25},{4,30},{5,31},{6,28},{7,29},{8,18},{9,... | collective-permute-start | bytes 3145736 | tf_op jit(solution)/shard_map/ppermute | solution.py:340
  921.0 96.3 %collective-permute-start.40 = (f32[32,64,128]{2,1,0:T(8,128)}, f32[32,64,128]{2,1,0:T(8,128)}, u32[]{:S(2)}, u32[]{:S(2)}) collective-permute-start(f32[32,64,128]{2,1,0:T(8,128)} %get-tuple-element.225), channel_id=1, source_target_pairs={{0,20},{1,21},{2,22},{3,23},{4,16},{5,17},{6,18},{7,19},{8,28},{9,... | collective-permute-start | bytes 3145736 | tf_op jit(solution)/shard_map/ppermute | solution.py:340
  921.0 126.2 %collective-permute-start.43 = (f32[32,64,128]{2,1,0:T(8,128)}, f32[32,64,128]{2,1,0:T(8,128)}, u32[]{:S(2)}, u32[]{:S(2)}) collective-permute-start(f32[32,64,128]{2,1,0:T(8,128)} %get-tuple-element.231), channel_id=1, source_target_pairs={{0,28},{1,29},{2,30},{3,31},{4,24},{5,25},{6,26},{7,27},{8,20},{9,... | collective-permute-start | bytes 3145736 | tf_op jit(solution)/shard_map/ppermute | solution.py:340
  954.0 115.0 %collective-permute-start.34 = (f32[32,64,128]{2,1,0:T(8,128)}, f32[32,64,128]{2,1,0:T(8,128)}, u32[]{:S(2)}, u32[]{:S(2)}) collective-permute-start(f32[32,64,128]{2,1,0:T(8,128)} %get-tuple-element.214), channel_id=1, source_target_pairs={{0,6},{1,7},{2,4},{3,5},{4,2},{5,3},{6,0},{7,1},{8,14},{9,15},{10,... | collective-permute-start | bytes 3145736 | tf_op jit(solution)/shard_map/ppermute | solution.py:340
  955.9 121.5 %collective-permute-start.32 = (f32[32,64,128]{2,1,0:T(8,128)}, f32[32,64,128]{2,1,0:T(8,128)}, u32[]{:S(2)}, u32[]{:S(2)}) collective-permute-start(f32[32,64,128]{2,1,0:T(8,128)} %get-tuple-element.210), channel_id=1, source_target_pairs={{0,4},{1,5},{2,6},{3,7},{4,0},{5,1},{6,2},{7,3},{8,12},{9,13},{10,... | collective-permute-start | bytes 3145736 | tf_op jit(solution)/shard_map/ppermute | solution.py:340
  956.2 136.0 %collective-permute-start.35 = (f32[32,64,128]{2,1,0:T(8,128)}, f32[32,64,128]{2,1,0:T(8,128)}, u32[]{:S(2)}, u32[]{:S(2)}) collective-permute-start(f32[32,64,128]{2,1,0:T(8,128)} %get-tuple-element.216), channel_id=1, source_target_pairs={{0,12},{1,13},{2,14},{3,15},{4,8},{5,9},{6,10},{7,11},{8,4},{9,5},... | collective-permute-start | bytes 3145736 | tf_op jit(solution)/shard_map/ppermute | solution.py:340
  1017.3 74.9 %collective-permute-start.44 = (f32[32,64,128]{2,1,0:T(8,128)}, f32[32,64,128]{2,1,0:T(8,128)}, u32[]{:S(2)}, u32[]{:S(2)}) collective-permute-start(f32[32,64,128]{2,1,0:T(8,128)} %get-tuple-element.233), channel_id=1, source_target_pairs={{0,30},{1,31},{2,28},{3,29},{4,26},{5,27},{6,24},{7,25},{8,22},{9,... | collective-permute-start | bytes 3145736 | tf_op jit(solution)/shard_map/ppermute | solution.py:340
  1047.2 52.8 %collective-permute-start.46 = (f32[32,64,128]{2,1,0:T(8,128)}, f32[32,64,128]{2,1,0:T(8,128)S(1)}, u32[]{:S(2)}, u32[]{:S(2)}) collective-permute-start(f32[32,64,128]{2,1,0:T(8,128)} %get-tuple-element.242), channel_id=1, source_target_pairs={{0,8},{1,9},{2,10},{3,11},{4,12},{5,13},{6,14},{7,15},{8,0},{9,1},... | collective-permute-start | bytes 3145736 | tf_op jit(solution)/shard_map/ppermute | solution.py:340
  1069.0 89.7 %collective-permute-start.42 = (f32[32,64,128]{2,1,0:T(8,128)S(1)}, f32[32,64,128]{2,1,0:T(8,128)S(1)}, u32[]{:S(2)}, u32[]{:S(2)}) collective-permute-start(f32[32,64,128]{2,1,0:T(8,128)S(1)} %copy-done.16), channel_id=1, source_target_pairs={{0,22},{1,23},{2,20},{3,21},{4,18},{5,19},{6,16},{7,17},{8,30},{9,... | collective-permute-start | bytes 3145736 | tf_op jit(solution)/shard_map/ppermute | solution.py:340
  1077.4 83.1 %collective-permute-start.54 = (f32[32,64,128]{2,1,0:T(8,128)}, f32[32,64,128]{2,1,0:T(8,128)}, u32[]{:S(2)}, u32[]{:S(2)}) collective-permute-start(f32[32,64,128]{2,1,0:T(8,128)} %get-tuple-element.257), channel_id=1, source_target_pairs={{0,24},{1,25},{2,26},{3,27},{4,28},{5,29},{6,30},{7,31},{8,16},{9,... | collective-permute-start | bytes 3145736 | tf_op jit(solution)/shard_map/ppermute | solution.py:340
  1092.2 70.3 %collective-permute-start.36 = (f32[32,64,128]{2,1,0:T(8,128)}, f32[32,64,128]{2,1,0:T(8,128)}, u32[]{:S(2)}, u32[]{:S(2)}) collective-permute-start(f32[32,64,128]{2,1,0:T(8,128)} %get-tuple-element.218), channel_id=1, source_target_pairs={{0,14},{1,15},{2,12},{3,13},{4,10},{5,11},{6,8},{7,9},{8,6},{9,7},... | collective-permute-start | bytes 3145736 | tf_op jit(solution)/shard_map/ppermute | solution.py:340
  1092.2 155.8 %collective-permute-start.52 = (f32[32,64,128]{2,1,0:T(8,128)}, f32[32,64,128]{2,1,0:T(8,128)}, u32[]{:S(2)}, u32[]{:S(2)}) collective-permute-start(f32[32,64,128]{2,1,0:T(8,128)} %get-tuple-element.252), channel_id=1, source_target_pairs={{0,16},{1,17},{2,18},{3,19},{4,20},{5,21},{6,22},{7,23},{8,24},{9,... | collective-permute-start | bytes 3145736 | tf_op jit(solution)/shard_map/ppermute | solution.py:340
  1100.0 148.5 %collective-permute-start.48 = (f32[32,64,128]{2,1,0:T(8,128)}, f32[32,64,128]{2,1,0:T(8,128)}, u32[]{:S(2)}, u32[]{:S(2)}) collective-permute-start(f32[32,64,128]{2,1,0:T(8,128)} %get-tuple-element.246), channel_id=1, source_target_pairs={{0,10},{1,11},{2,8},{3,9},{4,14},{5,15},{6,12},{7,13},{8,2},{9,3},... | collective-permute-start | bytes 3145736 | tf_op jit(solution)/shard_map/ppermute | solution.py:340
  1158.7 127.1 %collective-permute-start.47 = (f32[32,64,128]{2,1,0:T(8,128)}, f32[32,64,128]{2,1,0:T(8,128)}, u32[]{:S(2)}, u32[]{:S(2)}) collective-permute-start(f32[32,64,128]{2,1,0:T(8,128)} %get-tuple-element.243), channel_id=1, source_target_pairs={{0,4},{1,5},{2,6},{3,7},{4,0},{5,1},{6,2},{7,3},{8,12},{9,13},{10,... | collective-permute-start | bytes 3145736 | tf_op jit(solution)/shard_map/ppermute | solution.py:340
  1160.5 143.3 %collective-permute-start.45 = (f32[32,64,128]{2,1,0:T(8,128)}, f32[32,64,128]{2,1,0:T(8,128)}, u32[]{:S(2)}, u32[]{:S(2)}) collective-permute-start(f32[32,64,128]{2,1,0:T(8,128)} %get-tuple-element.239), channel_id=1, source_target_pairs={{0,2},{1,3},{2,0},{3,1},{4,6},{5,7},{6,4},{7,5},{8,10},{9,11},{10,... | collective-permute-start | bytes 3145736 | tf_op jit(solution)/shard_map/ppermute | solution.py:340
  1162.5 144.3 %collective-permute-start.55 = (f32[32,64,128]{2,1,0:T(8,128)}, f32[32,64,128]{2,1,0:T(8,128)}, u32[]{:S(2)}, u32[]{:S(2)}) collective-permute-start(f32[32,64,128]{2,1,0:T(8,128)} %get-tuple-element.258), channel_id=1, source_target_pairs={{0,20},{1,21},{2,22},{3,23},{4,16},{5,17},{6,18},{7,19},{8,28},{9,... | collective-permute-start | bytes 3145736 | tf_op jit(solution)/shard_map/ppermute | solution.py:340
  1248.0 94.2 %collective-permute-start.53 = (f32[32,64,128]{2,1,0:T(8,128)}, f32[32,64,128]{2,1,0:T(8,128)}, u32[]{:S(2)}, u32[]{:S(2)}) collective-permute-start(f32[32,64,128]{2,1,0:T(8,128)} %get-tuple-element.254), channel_id=1, source_target_pairs={{0,18},{1,19},{2,16},{3,17},{4,22},{5,23},{6,20},{7,21},{8,26},{9,... | collective-permute-start | bytes 3145736 | tf_op jit(solution)/shard_map/ppermute | solution.py:340
  1248.5 109.0 %collective-permute-start.56 = (f32[32,64,128]{2,1,0:T(8,128)}, f32[32,64,128]{2,1,0:T(8,128)}, u32[]{:S(2)}, u32[]{:S(2)}) collective-permute-start(f32[32,64,128]{2,1,0:T(8,128)} %get-tuple-element.261), channel_id=1, source_target_pairs={{0,26},{1,27},{2,24},{3,25},{4,30},{5,31},{6,28},{7,29},{8,18},{9,... | collective-permute-start | bytes 3145736 | tf_op jit(solution)/shard_map/ppermute | solution.py:340
  1285.7 97.7 %collective-permute-start.49 = (f32[32,64,128]{2,1,0:T(8,128)}, f32[32,64,128]{2,1,0:T(8,128)}, u32[]{:S(2)}, u32[]{:S(2)}) collective-permute-start(f32[32,64,128]{2,1,0:T(8,128)} %get-tuple-element.247), channel_id=1, source_target_pairs={{0,6},{1,7},{2,4},{3,5},{4,2},{5,3},{6,0},{7,1},{8,14},{9,15},{10,... | collective-permute-start | bytes 3145736 | tf_op jit(solution)/shard_map/ppermute | solution.py:340
  1303.8 153.8 %collective-permute-start.51 = (f32[32,64,128]{2,1,0:T(8,128)}, f32[32,64,128]{2,1,0:T(8,128)S(1)}, u32[]{:S(2)}, u32[]{:S(2)}) collective-permute-start(f32[32,64,128]{2,1,0:T(8,128)} %get-tuple-element.251), channel_id=1, source_target_pairs={{0,14},{1,15},{2,12},{3,13},{4,10},{5,11},{6,8},{7,9},{8,6},{9,7},... | collective-permute-start | bytes 3145736 | tf_op jit(solution)/shard_map/ppermute | solution.py:340
  1306.8 150.8 %collective-permute-start.50 = (f32[32,64,128]{2,1,0:T(8,128)}, f32[32,64,128]{2,1,0:T(8,128)S(1)}, u32[]{:S(2)}, u32[]{:S(2)}) collective-permute-start(f32[32,64,128]{2,1,0:T(8,128)} %get-tuple-element.249), channel_id=1, source_target_pairs={{0,12},{1,13},{2,14},{3,15},{4,8},{5,9},{6,10},{7,11},{8,4},{9,5},... | collective-permute-start | bytes 3145736 | tf_op jit(solution)/shard_map/ppermute | solution.py:340
  1342.2 115.5 %collective-permute-start.59 = (f32[32,64,128]{2,1,0:T(8,128)}, f32[32,64,128]{2,1,0:T(8,128)S(1)}, u32[]{:S(2)}, u32[]{:S(2)}) collective-permute-start(f32[32,64,128]{2,1,0:T(8,128)} %get-tuple-element.266), channel_id=1, source_target_pairs={{0,30},{1,31},{2,28},{3,29},{4,26},{5,27},{6,24},{7,25},{8,22},{9,... | collective-permute-start | bytes 3145736 | tf_op jit(solution)/shard_map/ppermute | solution.py:340
  1357.6 100.0 %collective-permute-start.58 = (f32[32,64,128]{2,1,0:T(8,128)}, f32[32,64,128]{2,1,0:T(8,128)}, u32[]{:S(2)}, u32[]{:S(2)}) collective-permute-start(f32[32,64,128]{2,1,0:T(8,128)} %get-tuple-element.264), channel_id=1, source_target_pairs={{0,28},{1,29},{2,30},{3,31},{4,24},{5,25},{6,26},{7,27},{8,20},{9,... | collective-permute-start | bytes 3145736 | tf_op jit(solution)/shard_map/ppermute | solution.py:340
  1383.5 112.3 %collective-permute-start.57 = (f32[32,64,128]{2,1,0:T(8,128)}, f32[32,64,128]{2,1,0:T(8,128)}, u32[]{:S(2)}, u32[]{:S(2)}) collective-permute-start(f32[32,64,128]{2,1,0:T(8,128)} %get-tuple-element.262), channel_id=1, source_target_pairs={{0,22},{1,23},{2,20},{3,21},{4,18},{5,19},{6,16},{7,17},{8,30},{9,... | collective-permute-start | bytes 3145736 | tf_op jit(solution)/shard_map/ppermute | solution.py:340
  1533.2 17.2 collective-permute-start.63
  1613.5 17.4 %collective-permute-start.73 = (f32[16,64,256]{2,1,0:T(8,128)}, f32[16,64,256]{2,1,0:T(8,128)S(1)}, u32[]{:S(2)}, u32[]{:S(2)}) collective-permute-start(f32[16,64,256]{2,1,0:T(8,128)} %get-tuple-element.274), channel_id=1, source_target_pairs={{0,1},{1,0},{2,3},{3,2},{4,5},{5,4},{6,7},{7,6},{8,9},{9,8},{10,11... | collective-permute-start | bytes 3145736 | tf_op jit(solution)/shard_map/ppermute | solution.py:340
  1613.9 17.0 collective-permute-start.74
  1614.0 16.9 collective-permute-start.75
  (42 other events, 2215.9 us)

commit v3 on v2

--- a/solution.py
+++ b/solution.py
@@ -12,9 +12,12 @@
 ITERS = 4
 CORES = 2
 AXES = ("gz", "gy")
-DEPTH = 6
-PACK_AT = 9
+DEPTH = 3
+PACK_AT = 6
 REDUCE_X = 4
+GRAM_X = 4
+GRAM_Y_X = 4
+CORE_X = 8
 VMEM_LIMIT = 60 << 20
 F32 = jnp.float32
 BF16 = jnp.bfloat16
@@ -48,35 +51,37 @@
     return lax.dot_general(left, right, (((0,), (0,)), ((), ())), preferred_element_type=F32)
 
 
-def pack_kernel(groups, width, me_ref, field_ref, *refs):
+def pack_kernel(count, width, pos_ref, field_ref, *refs):
     out_refs, turned = refs[:-1], refs[-1]
-    me = me_ref[0] % groups
+    me = pos_ref[0]
     for z in range(field_ref.shape[1]):
         turned[...] = field_ref[0, z].T
-        for k in range(groups):
+        for k in range(count):
             start = pl.multiple_of((me ^ k) * width, width)
             out_refs[k][:, z, :] = turned[pl.ds(start, width), :]
 
 
-def pack(field, me_half, species, groups):
+def pack(field, group, part, species, groups, parts):
     _, z_n, y_n, x_n = field.shape
-    width = x_n // (2 * groups)
+    count, width = groups // parts, x_n // groups
+    pos = jnp.stack([group % count, (group // count) ^ part]).astype(jnp.int32)
     z_tile = 8
     return pl.pallas_call(
-        functools.partial(pack_kernel, groups, width),
+        functools.partial(pack_kernel, count, width),
         grid_spec=pltpu.PrefetchScalarGridSpec(
             num_scalar_prefetch=1,
             grid=(z_n // z_tile,),
-            in_specs=[pl.BlockSpec((1, z_tile, y_n, x_n // 2), lambda i, m: (species, i, 0, m[1]))],
-            out_specs=[pl.BlockSpec((width, z_tile, y_n), lambda i, m: (0, i, 0))] * groups,
-            scratch_shapes=[pltpu.VMEM((x_n // 2, y_n), F32)],
+            in_specs=[pl.BlockSpec((1, z_tile, y_n, x_n // parts),
+                                   lambda i, p: (species, i, 0, p[1]))],
+            out_specs=[pl.BlockSpec((width, z_tile, y_n), lambda i, p: (0, i, 0))] * count,
+            scratch_shapes=[pltpu.VMEM((x_n // parts, y_n), F32)],
         ),
-        out_shape=[jax.ShapeDtypeStruct((width, z_n, y_n), F32)] * groups,
+        out_shape=[jax.ShapeDtypeStruct((width, z_n, y_n), F32)] * count,
         compiler_params=pltpu.CompilerParams(vmem_limit_bytes=VMEM_LIMIT),
         cost_estimate=pl.CostEstimate(
-            flops=0, bytes_accessed=4 * z_n * y_n * x_n, transcendentals=0),
+            flops=0, bytes_accessed=8 * z_n * y_n * x_n // parts, transcendentals=0),
         name="pack",
-    )(me_half, field)
+    )(pos, field)
 
 
 def gram_z_kernel(groups, side, me_ref, prev_ref, *refs):
@@ -110,7 +115,7 @@
     groups = len(pieces)
     width, z_n, y_n = pieces[0].shape
     order = z_n * (groups // side)
-    x_tile = 4
+    x_tile = GRAM_X
     depth = x_tile * side * y_n
     whole = pl.BlockSpec((order, order), lambda i, m: (0, 0))
     return pl.pallas_call(
@@ -292,7 +297,7 @@
     species = len(mine)
     half, rank, two = mine[0].shape
     order = two * CORES
-    x_tile = 4
+    x_tile = GRAM_Y_X
     part = pl.BlockSpec((x_tile, rank, two), lambda i, c: (i, 0, 0))
     return pl.pallas_call(
         functools.partial(gram_y_kernel, species, side),
@@ -323,7 +328,7 @@
 
 def project_core(basis_t, full):
     species, half, rank, order = full.shape
-    x_tile = 4
+    x_tile = CORE_X
     return pl.pallas_call(
         core_kernel,
         grid=(half // x_tile,),
@@ -340,62 +345,63 @@
     return lax.ppermute(value, AXES, [(i, i ^ mask) for i in range(total)])
 
 
-def all_sum(value, me, total, quads):
-    low = total // quads
-    bits = [1 << b for b in range(low.bit_length() - 1)]
+def all_sum(value, me, total):
+    stages = [(1, 2)]
+    while stages[-1][0] * stages[-1][1] < total:
+        step = stages[-1][0] * stages[-1][1]
+        stages.append((step, min(4, total // step)))
     current = value
-    for bit in bits:
-        half = current.shape[0] // 2
-        upper = (me // bit) % 2 == 1
-        first, second = current[:half], current[half:]
-        current = jnp.where(upper, second, first) + permute(
-            jnp.where(upper, first, second), bit, total)
-    place = me // low
-    parts = current.reshape(quads, -1, current.shape[1])
-    pick = lambda k: lax.dynamic_index_in_dim(parts, place ^ k, 0, False)
-    arrived = [permute(pick(k), low * k, total) for k in range(1, quads)]
-    sums = pick(0)
-    for part in arrived:
-        sums = sums + part
-    stack = jnp.stack([sums] + [permute(sums, low * k, total) for k in range(1, quads)])
-    current = jnp.concatenate(
-        [lax.dynamic_index_in_dim(stack, place ^ j, 0, False) for j in range(quads)])
-    for bit in reversed(bits):
-        other = permute(current, bit, total)
-        upper = (me // bit) % 2 == 1
-        current = jnp.concatenate(
-            [jnp.where(upper, other, current), jnp.where(upper, current, other)])
+    for step, count in stages:
+        place = (me // step) % count
+        parts = current.reshape(count, -1, current.shape[1])
+        pick = lambda k: lax.dynamic_index_in_dim(parts, place ^ k, 0, False)
+        arrived = [permute(pick(k), step * k, total) for k in reversed(range(1, count))]
+        current = pick(0)
+        for part in reversed(arrived):
+            current = current + part
+    for step, count in reversed(stages):
+        place = (me // step) % count
+        got = [current] + [permute(current, step * k, total) for k in range(1, count)]
+        if count == 2:
+            swap = place == 1
+            got = [jnp.where(swap, got[1], got[0]), jnp.where(swap, got[0], got[1])]
+        else:
+            stack = jnp.stack(got)
+            got = [lax.dynamic_index_in_dim(stack, place ^ j, 0, False) for j in range(count)]
+        current = jnp.concatenate(got)
     return current
 
 
 def exchange(field, group, groups, total):
     half = groups // 2
     quarter = half // 2
-    upper = group // half
-    far_pos = jnp.stack([group, 1 - upper]).astype(jnp.int32)
-    near_pos = jnp.stack([group, upper]).astype(jnp.int32)
-    far_order = sorted(range(half), key=lambda k: (k % quarter, k))
     near_order = sorted(range(1, half), key=lambda k: ((k - 1) % quarter if k < quarter else k - quarter,
                                                        -k))
-    recent, pieces = [], []
+    done, pieces = [], []
     source = field
     for s in range(field.shape[0]):
         if s:
-            source = tie(source, recent[-PACK_AT])
-        far = pack(source, far_pos, s, half)
-        near = pack(tie(source, far[0]), near_pos, s, half)
+            source = tie(source, done[-PACK_AT][0])
+        if s == 0:
+            far_order = list(range(half))
+            far = pack(source, group, 2, s, groups, 4)
+            far = far + pack(tie(source, far[0]), group, 3, s, groups, 4)
+        else:
+            far_order = sorted(range(half), key=lambda k: (k % quarter, k))
+            far = pack(source, group, 1, s, groups, 2)
+        near = pack(tie(source, far[-1]), group, 0, s, groups, 2)
         got = [near[0]] + [None] * (groups - 1)
         pieces.append(got)
-        order = []
         for i, k in enumerate(far_order):
-            order.append((half + k, far[k]))
+            pair = [(half + k, far[k])]
             if i < len(near_order):
-                order.append((near_order[i], near[near_order[i]]))
-        for k, value in order:
-            if len(recent) >= DEPTH:
-                value = tie(value, recent[-DEPTH])
-            got[k] = permute(value, k * CORES, total)
-            recent.append(got[k])
+                pair.append((near_order[i], near[near_order[i]]))
+            values = [value for _, value in pair]
+            if len(done) >= DEPTH:
+                values = lax.optimization_barrier(values + done[-DEPTH])[:len(pair)]
+            for (k, _), value in zip(pair, values):
+                got[k] = permute(value, k * CORES, total)
+            done.append([got[k] for k, _ in pair])
     return pieces
 
 
@@ -417,7 +423,7 @@
     gram = jnp.zeros((grid_n, grid_n), F32)
     for s in range(species):
         gram = gram_z_step(gram, pieces[s], one(group), side)
-    gram = all_sum(gram, me, total, 4)
+    gram = all_sum(gram, me, total)
     basis_z, turned_z = leaf_basis(gram, start_t, one(gz), gz_n)
 
     side_pos = gy // CORES
@@ -427,7 +433,7 @@
     others = [permute(value, 1, total) for value in leaving]
     mine = reduce_half(tie(turned_z, leaving[0]), pieces, home, side)
     full, gram = gram_y_full(mine, others, one(core), side)
-    gram = all_sum(gram, me, total, 4)
+    gram = all_sum(gram, me, total)
     basis_y, _ = leaf_basis(gram, start_t, one(gz), 1)
     core_tensor = project_core(basis_y, full)
     core_tensor = core_tensor.reshape(species, x_n // total, RANK * RANK)

time: 1720 us -> 1680 us (0.977); the launches traced: 1720 us -> 1660 us
  starting transfers between devices: 824 us -> 721 us
  waiting for transfers between devices: 636 us -> 675 us
    ppermute x88 -> x92, starting transfers between devices: 824 us -> 721 us  [permute(): return lax.ppermute(value, AXES, [(i, i ^ mask) for i in range(total)])]
    ppermute x88 -> x92, waiting for transfers between devices: 636 us -> 675 us  [permute(): return lax.ppermute(value, AXES, [(i, i ^ mask) for i in range(total)])]
    pallas_call x8 -> x9, Pallas kernels: 85.8 us -> 91.6 us  [pack(): pl.pallas_call(functools.partial(pack_kernel, count, width), grid_spec=pl...]
  transfers between devices with their start and end apart: 88 -> 92, of which waited for: 43 -> 44; matrix products, arithmetic and copies ran while one was open for 0% -> 0% of each run, Pallas kernels for 8% -> 9%
where the time goes in v3:
time: 1680 us; the launch traced here: 1660 us
  starting transfers between devices  721 us (43%)
  waiting for transfers between devices  675 us (40%)
  Pallas kernels  249 us (15%)
    ppermute x92, starting transfers between devices, permute(): return lax.ppermute(value, AXES, [(i, i ^ mask) for i in range(total)])  721 us
    ppermute x92, waiting for transfers between devices, permute(): return lax.ppermute(value, AXES, [(i, i ^ mask) for i in range(total)])  675 us
    pallas_call x9, Pallas kernels, pack(): pl.pallas_call(functools.partial(pack_kernel, count, width), grid_spec=pl...  91.6 us
    pallas_call x4, Pallas kernels, gram_z_step(): pl.pallas_call(functools.partial(gram_z_kernel, groups, side), grid_spec=...  67.1 us
    pallas_call x2, Pallas kernels, leaf_basis(): pl.pallas_call(functools.partial(basis_kernel, gz_n), in_specs=[pl.BlockS...  41.2 us
  transfers between devices with their start and end apart: 92, of which 44 were waited for; matrix products, arithmetic and copies ran while one was open for 0% of the time, Pallas kernels for 9%

profile of v3, /device:TPU:0, one launch (start us, length us, event | category | flops | bytes accessed | tf_op | source)
XLA Modules:
  0.0 1662.1 jit_solution(14593811832964410872)
XLA Ops:
  1.3 8.3 pack.9
  9.6 4.0 collective-permute-start.1
  14.3 8.3 pack.10
  22.6 10.7 pack.11
  36.7 3.6 collective-permute-start.4
  40.2 21.0 %collective-permute-done.1.refs_8_ = f32[32,64,128]{2,1,0:T(8,128)S(1)} collective-permute-done((f32[32,64,128]{2,1,0:T(8,128)}, f32[32,64,128]{2,1,0:T(8,128)S(1)}, u32[]{:S(2)}, u32[]{:S(2)}) %collective-permute-start.1) | collective-permute-done | bytes 1048608 | tf_op jit(solution)/shard_map/ppermute | solution.py:345
  62.3 19.8 %collective-permute-done.2.refs_4_ = f32[32,64,128]{2,1,0:T(8,128)S(1)} collective-permute-done((f32[32,64,128]{2,1,0:T(8,128)}, f32[32,64,128]{2,1,0:T(8,128)S(1)}, u32[]{:S(2)}, u32[]{:S(2)}) %collective-permute-start.2) | collective-permute-done | bytes 1048608 | tf_op jit(solution)/shard_map/ppermute | solution.py:345
  82.1 4.8 collective-permute-start.3
  86.9 42.2 %collective-permute-done.7.refs_9_ = f32[32,64,128]{2,1,0:T(8,128)S(1)} collective-permute-done((f32[32,64,128]{2,1,0:T(8,128)}, f32[32,64,128]{2,1,0:T(8,128)S(1)}, u32[]{:S(2)}, u32[]{:S(2)}) %collective-permute-start.7) | collective-permute-done | bytes 1048608 | tf_op jit(solution)/shard_map/ppermute | solution.py:345
  129.7 3.3 collective-permute-start.8
  133.0 41.2 %collective-permute-done.4.refs_10_ = f32[32,64,128]{2,1,0:T(8,128)} collective-permute-done((f32[32,64,128]{2,1,0:T(8,128)}, f32[32,64,128]{2,1,0:T(8,128)}, u32[]{:S(2)}, u32[]{:S(2)}) %collective-permute-start.4) | collective-permute-done | bytes 1048608 | tf_op jit(solution)/shard_map/ppermute | solution.py:345
  179.2 63.4 %collective-permute-done.9.refs_11_ = f32[32,64,128]{2,1,0:T(8,128)} collective-permute-done((f32[32,64,128]{2,1,0:T(8,128)}, f32[32,64,128]{2,1,0:T(8,128)}, u32[]{:S(2)}, u32[]{:S(2)}) %collective-permute-start.9) | collective-permute-done | bytes 1048608 | tf_op jit(solution)/shard_map/ppermute | solution.py:345
  242.6 5.4 collective-permute-start.13
  247.9 10.7 pack.12
  258.7 10.7 pack.13
  269.4 64.7 %collective-permute-start.16 = (f32[32,64,128]{2,1,0:T(8,128)}, f32[32,64,128]{2,1,0:T(8,128)S(1)}, u32[]{:S(2)}, u32[]{:S(2)}) collective-permute-start(f32[32,64,128]{2,1,0:T(8,128)} %get-tuple-element.181), channel_id=1, source_target_pairs={{0,16},{1,17},{2,18},{3,19},{4,20},{5,21},{6,22},{7,23},{8,24},{9,... | collective-permute-start | bytes 3145736 | tf_op jit(solution)/shard_map/ppermute | solution.py:345
  338.5 86.2 %collective-permute-start.19 = (f32[32,64,128]{2,1,0:T(8,128)}, f32[32,64,128]{2,1,0:T(8,128)}, u32[]{:S(2)}, u32[]{:S(2)}) collective-permute-start(f32[32,64,128]{2,1,0:T(8,128)} %get-tuple-element.188), channel_id=1, source_target_pairs={{0,18},{1,19},{2,16},{3,17},{4,22},{5,23},{6,20},{7,21},{8,26},{9,... | collective-permute-start | bytes 3145736 | tf_op jit(solution)/shard_map/ppermute | solution.py:345
  424.8 44.0 %collective-permute-done.16.refs_8_.refs_24_ = f32[32,64,128]{2,1,0:T(8,128)S(1)} collective-permute-done((f32[32,64,128]{2,1,0:T(8,128)}, f32[32,64,128]{2,1,0:T(8,128)S(1)}, u32[]{:S(2)}, u32[]{:S(2)}) %collective-permute-start.16) | collective-permute-done | bytes 1048608 | tf_op jit(solution)/shard_map/ppermute | solution.py:345
  471.5 20.5 %collective-permute-start.23 = (f32[32,64,128]{2,1,0:T(8,128)}, f32[32,64,128]{2,1,0:T(8,128)}, u32[]{:S(2)}, u32[]{:S(2)}) collective-permute-start(f32[32,64,128]{2,1,0:T(8,128)} %get-tuple-element.194), channel_id=1, source_target_pairs={{0,12},{1,13},{2,14},{3,15},{4,8},{5,9},{6,10},{7,11},{8,4},{9,5},... | collective-permute-start | bytes 3145736 | tf_op jit(solution)/shard_map/ppermute | solution.py:345
  492.1 44.3 %collective-permute-done.19.refs_9_.refs_25_ = f32[32,64,128]{2,1,0:T(8,128)} collective-permute-done((f32[32,64,128]{2,1,0:T(8,128)}, f32[32,64,128]{2,1,0:T(8,128)}, u32[]{:S(2)}, u32[]{:S(2)}) %collective-permute-start.19) | collective-permute-done | bytes 1048608 | tf_op jit(solution)/shard_map/ppermute | solution.py:345
  536.3 4.7 collective-permute-done.20.refs_5_.refs_21_
  543.3 63.6 %collective-permute-start.25 = (f32[32,64,128]{2,1,0:T(8,128)}, f32[32,64,128]{2,1,0:T(8,128)}, u32[]{:S(2)}, u32[]{:S(2)}) collective-permute-start(f32[32,64,128]{2,1,0:T(8,128)} %get-tuple-element.198), channel_id=1, source_target_pairs={{0,14},{1,15},{2,12},{3,13},{4,10},{5,11},{6,8},{7,9},{8,6},{9,7},... | collective-permute-start | bytes 3145736 | tf_op jit(solution)/shard_map/ppermute | solution.py:345
  606.9 21.2 %collective-permute-done.23.refs_6_.refs_22_ = f32[32,64,128]{2,1,0:T(8,128)} collective-permute-done((f32[32,64,128]{2,1,0:T(8,128)}, f32[32,64,128]{2,1,0:T(8,128)}, u32[]{:S(2)}, u32[]{:S(2)}) %collective-permute-start.23) | collective-permute-done | bytes 1048608 | tf_op jit(solution)/shard_map/ppermute | solution.py:345
  632.6 10.8 pack.14
  643.4 10.7 pack.15
  654.1 42.3 %collective-permute-start.31 = (f32[32,64,128]{2,1,0:T(8,128)}, f32[32,64,128]{2,1,0:T(8,128)S(1)}, u32[]{:S(2)}, u32[]{:S(2)}) collective-permute-start(f32[32,64,128]{2,1,0:T(8,128)} %get-tuple-element.214), channel_id=1, source_target_pairs={{0,16},{1,17},{2,18},{3,19},{4,20},{5,21},{6,22},{7,23},{8,24},{9,... | collective-permute-start | bytes 3145736 | tf_op jit(solution)/shard_map/ppermute | solution.py:345
  697.2 43.0 %collective-permute-done.27.refs_11_.refs_27_ = f32[32,64,128]{2,1,0:T(8,128)} collective-permute-done((f32[32,64,128]{2,1,0:T(8,128)}, f32[32,64,128]{2,1,0:T(8,128)}, u32[]{:S(2)}, u32[]{:S(2)}) %collective-permute-start.27) | collective-permute-done | bytes 1048608 | tf_op jit(solution)/shard_map/ppermute | solution.py:345
  743.8 43.5 %collective-permute-start.34 = (f32[32,64,128]{2,1,0:T(8,128)}, f32[32,64,128]{2,1,0:T(8,128)}, u32[]{:S(2)}, u32[]{:S(2)}) collective-permute-start(f32[32,64,128]{2,1,0:T(8,128)} %get-tuple-element.221), channel_id=1, source_target_pairs={{0,18},{1,19},{2,16},{3,17},{4,22},{5,23},{6,20},{7,21},{8,26},{9,... | collective-permute-start | bytes 3145736 | tf_op jit(solution)/shard_map/ppermute | solution.py:345
  787.3 41.7 %collective-permute-done.31.refs_8_.refs_40_ = f32[32,64,128]{2,1,0:T(8,128)S(1)} collective-permute-done((f32[32,64,128]{2,1,0:T(8,128)}, f32[32,64,128]{2,1,0:T(8,128)S(1)}, u32[]{:S(2)}, u32[]{:S(2)}) %collective-permute-start.31) | collective-permute-done | bytes 1048608 | tf_op jit(solution)/shard_map/ppermute | solution.py:345
  829.0 3.1 collective-permute-start.33
  834.0 20.5 %collective-permute-start.38 = (f32[32,64,128]{2,1,0:T(8,128)}, f32[32,64,128]{2,1,0:T(8,128)}, u32[]{:S(2)}, u32[]{:S(2)}) collective-permute-start(f32[32,64,128]{2,1,0:T(8,128)} %get-tuple-element.227), channel_id=1, source_target_pairs={{0,12},{1,13},{2,14},{3,15},{4,8},{5,9},{6,10},{7,11},{8,4},{9,5},... | collective-permute-start | bytes 3145736 | tf_op jit(solution)/shard_map/ppermute | solution.py:345
  854.6 43.7 %collective-permute-done.34.refs_9_.refs_41_ = f32[32,64,128]{2,1,0:T(8,128)} collective-permute-done((f32[32,64,128]{2,1,0:T(8,128)}, f32[32,64,128]{2,1,0:T(8,128)}, u32[]{:S(2)}, u32[]{:S(2)}) %collective-permute-start.34) | collective-permute-done | bytes 1048608 | tf_op jit(solution)/shard_map/ppermute | solution.py:345
  900.9 4.3 collective-permute-start.43
  905.2 63.5 %collective-permute-start.40 = (f32[32,64,128]{2,1,0:T(8,128)}, f32[32,64,128]{2,1,0:T(8,128)}, u32[]{:S(2)}, u32[]{:S(2)}) collective-permute-start(f32[32,64,128]{2,1,0:T(8,128)} %get-tuple-element.231), channel_id=1, source_target_pairs={{0,14},{1,15},{2,12},{3,13},{4,10},{5,11},{6,8},{7,9},{8,6},{9,7},... | collective-permute-start | bytes 3145736 | tf_op jit(solution)/shard_map/ppermute | solution.py:345
  968.7 20.5 %collective-permute-done.38.refs_6_.refs_38_ = f32[32,64,128]{2,1,0:T(8,128)} collective-permute-done((f32[32,64,128]{2,1,0:T(8,128)}, f32[32,64,128]{2,1,0:T(8,128)}, u32[]{:S(2)}, u32[]{:S(2)}) %collective-permute-start.38) | collective-permute-done | bytes 1048608 | tf_op jit(solution)/shard_map/ppermute | solution.py:345
  989.2 3.0 collective-permute-start.42
  994.7 10.8 pack.16
  1005.5 10.7 pack.17
  1016.2 40.1 %collective-permute-start.46 = (f32[32,64,128]{2,1,0:T(8,128)}, f32[32,64,128]{2,1,0:T(8,128)S(1)}, u32[]{:S(2)}, u32[]{:S(2)}) collective-permute-start(f32[32,64,128]{2,1,0:T(8,128)} %get-tuple-element.247), channel_id=1, source_target_pairs={{0,16},{1,17},{2,18},{3,19},{4,20},{5,21},{6,22},{7,23},{8,24},{9,... | collective-permute-start | bytes 3145736 | tf_op jit(solution)/shard_map/ppermute | solution.py:345
  1059.2 42.7 %collective-permute-done.42.refs_11_.refs_43_ = f32[32,64,128]{2,1,0:T(8,128)} collective-permute-done((f32[32,64,128]{2,1,0:T(8,128)}, f32[32,64,128]{2,1,0:T(8,128)}, u32[]{:S(2)}, u32[]{:S(2)}) %collective-permute-start.42) | collective-permute-done | bytes 1048608 | tf_op jit(solution)/shard_map/ppermute | solution.py:345
  1101.8 3.2 collective-permute-start.45
  1105.0 43.0 %collective-permute-start.49 = (f32[32,64,128]{2,1,0:T(8,128)}, f32[32,64,128]{2,1,0:T(8,128)}, u32[]{:S(2)}, u32[]{:S(2)}) collective-permute-start(f32[32,64,128]{2,1,0:T(8,128)} %get-tuple-element.254), channel_id=1, source_target_pairs={{0,18},{1,19},{2,16},{3,17},{4,22},{5,23},{6,20},{7,21},{8,26},{9,... | collective-permute-start | bytes 3145736 | tf_op jit(solution)/shard_map/ppermute | solution.py:345
  1148.0 42.7 %collective-permute-done.46.refs_8_.refs_56_ = f32[32,64,128]{2,1,0:T(8,128)S(1)} collective-permute-done((f32[32,64,128]{2,1,0:T(8,128)}, f32[32,64,128]{2,1,0:T(8,128)S(1)}, u32[]{:S(2)}, u32[]{:S(2)}) %collective-permute-start.46) | collective-permute-done | bytes 1048608 | tf_op jit(solution)/shard_map/ppermute | solution.py:345
  1190.7 3.3 collective-permute-start.48
  1196.0 41.8 %collective-permute-start.53 = (f32[32,64,128]{2,1,0:T(8,128)}, f32[32,64,128]{2,1,0:T(8,128)}, u32[]{:S(2)}, u32[]{:S(2)}) collective-permute-start(f32[32,64,128]{2,1,0:T(8,128)} %get-tuple-element.260), channel_id=1, source_target_pairs={{0,12},{1,13},{2,14},{3,15},{4,8},{5,9},{6,10},{7,11},{8,4},{9,5},... | collective-permute-start | bytes 3145736 | tf_op jit(solution)/shard_map/ppermute | solution.py:345
  1237.8 23.1 %collective-permute-done.49.refs_9_.refs_57_ = f32[32,64,128]{2,1,0:T(8,128)} collective-permute-done((f32[32,64,128]{2,1,0:T(8,128)}, f32[32,64,128]{2,1,0:T(8,128)}, u32[]{:S(2)}, u32[]{:S(2)}) %collective-permute-start.49) | collective-permute-done | bytes 1048608 | tf_op jit(solution)/shard_map/ppermute | solution.py:345
  1261.9 16.9 %gram_z.4.prev_ref = f32[512,512]{1,0:T(8,128)} custom-call(s32[1]{0:T(128)} %bitcast.3.me_ref, f32[512,512]{1,0:T(8,128)} %broadcast_in_dim.2.prev_ref, f32[32,64,128]{2,1,0:T(8,128)} %get-tuple-element.147.refs_0_, f32[32,64,128]{2,1,0:T(8,128)} %collective-permute-done.refs_1_, f32[32,64,128]{2,1,0:T(8,128)} %collective-permute-done.3.refs_2_, ...), custom_call_target="tpu_custom_call" | custom-call | flops 8589934592 | bytes 16777216 | tf_op jit(solution)/shard_map/gram_z/pallas_call | solution.py:121
  1282.1 47.7 %collective-permute-start.55 = (f32[32,64,128]{2,1,0:T(8,128)}, f32[32,64,128]{2,1,0:T(8,128)S(1)}, u32[]{:S(2)}, u32[]{:S(2)}) collective-permute-start(f32[32,64,128]{2,1,0:T(8,128)} %get-tuple-element.264), channel_id=1, source_target_pairs={{0,14},{1,15},{2,12},{3,13},{4,10},{5,11},{6,8},{7,9},{8,6},{9,7},... | collective-permute-start | bytes 3145736 | tf_op jit(solution)/shard_map/ppermute | solution.py:345
  1329.8 21.5 %collective-permute-done.56.refs_10_.refs_58_ = f32[32,64,128]{2,1,0:T(8,128)} collective-permute-done((f32[32,64,128]{2,1,0:T(8,128)}, f32[32,64,128]{2,1,0:T(8,128)}, u32[]{:S(2)}, u32[]{:S(2)}) %collective-permute-start.56) | collective-permute-done | bytes 1048608 | tf_op jit(solution)/shard_map/ppermute | solution.py:345
  1351.3 9.5 collective-permute-start.59
  1360.8 16.7 %gram_z.5.prev_ref = f32[512,512]{1,0:T(8,128)} custom-call(s32[1]{0:T(128)} %bitcast.3.me_ref, f32[512,512]{1,0:T(8,128)} %gram_z.4.prev_ref, f32[32,64,128]{2,1,0:T(8,128)} %get-tuple-element.173.refs_0_.refs_16_, f32[32,64,128]{2,1,0:T(8,128)} %copy-done.5, f32[32,64,128]{2,1,0:T(8,128)} %collective-permute-done.18.refs_2_.refs_18_, ...), custom_call_target="tpu_custom_call" | custom-call | flops 8589934592 | bytes 16777216 | tf_op jit(solution)/shard_map/gram_z/pallas_call | solution.py:121
  1377.5 16.7 %gram_z.6.prev_ref = f32[512,512]{1,0:T(8,128)} custom-call(s32[1]{0:T(128)} %bitcast.3.me_ref, f32[512,512]{1,0:T(8,128)} %gram_z.5.prev_ref, f32[32,64,128]{2,1,0:T(8,128)} %get-tuple-element.206.refs_0_.refs_32_, f32[32,64,128]{2,1,0:T(8,128)} %copy-done.8, f32[32,64,128]{2,1,0:T(8,128)} %collective-permute-done.33.refs_2_.refs_34_, ...), custom_call_target="tpu_custom_call" | custom-call | flops 8589934592 | bytes 16777216 | tf_op jit(solution)/shard_map/gram_z/pallas_call | solution.py:121
  1394.3 50.5 %collective-permute-done.57.refs_11_.refs_59_ = f32[32,64,128]{2,1,0:T(8,128)} collective-permute-done((f32[32,64,128]{2,1,0:T(8,128)}, f32[32,64,128]{2,1,0:T(8,128)}, u32[]{:S(2)}, u32[]{:S(2)}) %collective-permute-start.57) | collective-permute-done | bytes 1048608 | tf_op jit(solution)/shard_map/ppermute | solution.py:345
  1444.8 16.7 %gram_z.7 = f32[512,512]{1,0:T(8,128)} custom-call(s32[1]{0:T(128)} %bitcast.3.me_ref, f32[512,512]{1,0:T(8,128)} %gram_z.6.prev_ref, f32[32,64,128]{2,1,0:T(8,128)} %get-tuple-element.239.refs_0_.refs_48_, f32[32,64,128]{2,1,0:T(8,128)} %copy-done.11, f32[32,64,128]{2,1,0:T(8,128)} %collective-permute-done.48.refs_2_.refs_50_, f32[32,64,128]{2,1,0:T(8,128)} %copy-done.12, ...), custom_call_target="tpu_custom_call" | custom-call | flops 8589934592 | bytes 16777216 | tf_op jit(solution)/shard_map/gram_z/pallas_call | solution.py:121
  1475.4 22.3 %collective-permute-start.64 = (f32[16,512]{1,0:T(8,128)S(1)}, f32[16,512]{1,0:T(8,128)S(1)}, u32[]{:S(2)}, u32[]{:S(2)}) collective-permute-start(f32[16,512]{1,0:T(8,128)S(1)} %get-tuple-element.316), channel_id=1, source_target_pairs={{0,8},{1,9},{2,10},{3,11},{4,12},{5,13},{6,14},{7,15},{8,0},{9,1},... | collective-permute-start | bytes 98312 | tf_op jit(solution)/shard_map/ppermute | solution.py:345
  1497.7 3.4 collective-permute-start.66
  1506.9 3.5 collective-permute-start.67
  1524.3 20.7 %leaf_basis.2 = (f32[64,512]{1,0:T(8,128)}, f32[64,512]{1,0:T(8,128)}) custom-call(s32[1]{0:T(128)} %bitcast.me_ref, f32[512,512]{1,0:T(8,128)} %pad_maximum_fusion.gram_ref, f32[64,512]{1,0:T(8,128)} %multiply_cosine_fusion.start_ref), custom_call_target="tpu_custom_call" | custom-call | tf_op jit(solution)/shard_map/leaf_basis/pallas_call | solution.py:211
  1545.1 16.3 reduce_z.2
  1562.5 16.3 reduce_z.3
  1580.5 10.8 gram_y.1
  1609.5 3.5 collective-permute-done.84
  1632.5 20.5 %leaf_basis.3 = (f32[64,512]{1,0:T(8,128)}, f32[64,512]{1,0:T(8,128)}) custom-call(s32[1]{0:T(128)} %bitcast.me_ref, f32[512,512]{1,0:T(8,128)} %pad_maximum_fusion.1.gram_ref, f32[64,512]{1,0:T(8,128)} %multiply_cosine_fusion.start_ref), custom_call_target="tpu_custom_call" | custom-call | tf_op jit(solution)/shard_map/leaf_basis/pallas_call | solution.py:211
  1652.9 5.9 core.1
  (211 shorter events, 122.7 us)
Async XLA Ops:
  9.6 51.6 %collective-permute-start.1 = (f32[32,64,128]{2,1,0:T(8,128)}, f32[32,64,128]{2,1,0:T(8,128)S(1)}, u32[]{:S(2)}, u32[]{:S(2)}) collective-permute-start(f32[32,64,128]{2,1,0:T(8,128)} %get-tuple-element.143), channel_id=1, source_target_pairs={{0,16},{1,17},{2,18},{3,19},{4,20},{5,21},{6,22},{7,23},{8,24},{9,... | collective-permute-start | bytes 3145736 | tf_op jit(solution)/shard_map/ppermute | solution.py:345
  33.3 48.8 %collective-permute-start.2 = (f32[32,64,128]{2,1,0:T(8,128)}, f32[32,64,128]{2,1,0:T(8,128)S(1)}, u32[]{:S(2)}, u32[]{:S(2)}) collective-permute-start(f32[32,64,128]{2,1,0:T(8,128)} %get-tuple-element.151), channel_id=1, source_target_pairs={{0,8},{1,9},{2,10},{3,11},{4,12},{5,13},{6,14},{7,15},{8,0},{9,1},... | collective-permute-start | bytes 3145736 | tf_op jit(solution)/shard_map/ppermute | solution.py:345
  34.9 94.2 %collective-permute-start.7 = (f32[32,64,128]{2,1,0:T(8,128)}, f32[32,64,128]{2,1,0:T(8,128)S(1)}, u32[]{:S(2)}, u32[]{:S(2)}) collective-permute-start(f32[32,64,128]{2,1,0:T(8,128)} %get-tuple-element.160), channel_id=1, source_target_pairs={{0,18},{1,19},{2,16},{3,17},{4,22},{5,23},{6,20},{7,21},{8,26},{9,... | collective-permute-start | bytes 3145736 | tf_op jit(solution)/shard_map/ppermute | solution.py:345
  36.1 93.6 %collective-permute-start = (f32[32,64,128]{2,1,0:T(8,128)}, f32[32,64,128]{2,1,0:T(8,128)}, u32[]{:S(2)}, u32[]{:S(2)}) collective-permute-start(f32[32,64,128]{2,1,0:T(8,128)} %get-tuple-element.148), channel_id=1, source_target_pairs={{0,2},{1,3},{2,0},{3,1},{4,6},{5,7},{6,4},{7,5},{8,10},{9,11},{10,... | collective-permute-start | bytes 3145736 | tf_op jit(solution)/shard_map/ppermute | solution.py:345
  36.7 137.5 %collective-permute-start.4 = (f32[32,64,128]{2,1,0:T(8,128)}, f32[32,64,128]{2,1,0:T(8,128)}, u32[]{:S(2)}, u32[]{:S(2)}) collective-permute-start(f32[32,64,128]{2,1,0:T(8,128)} %get-tuple-element.155), channel_id=1, source_target_pairs={{0,20},{1,21},{2,22},{3,23},{4,16},{5,17},{6,18},{7,19},{8,28},{9,... | collective-permute-start | bytes 3145736 | tf_op jit(solution)/shard_map/ppermute | solution.py:345
  61.2 115.4 %collective-permute-start.5 = (f32[32,64,128]{2,1,0:T(8,128)}, f32[32,64,128]{2,1,0:T(8,128)}, u32[]{:S(2)}, u32[]{:S(2)}) collective-permute-start(f32[32,64,128]{2,1,0:T(8,128)} %get-tuple-element.156), channel_id=1, source_target_pairs={{0,10},{1,11},{2,8},{3,9},{4,14},{5,15},{6,12},{7,13},{8,2},{9,3},... | collective-permute-start | bytes 3145736 | tf_op jit(solution)/shard_map/ppermute | solution.py:345
  82.1 96.0 %collective-permute-start.3 = (f32[32,64,128]{2,1,0:T(8,128)}, f32[32,64,128]{2,1,0:T(8,128)}, u32[]{:S(2)}, u32[]{:S(2)}) collective-permute-start(f32[32,64,128]{2,1,0:T(8,128)} %get-tuple-element.152), channel_id=1, source_target_pairs={{0,4},{1,5},{2,6},{3,7},{4,0},{5,1},{6,2},{7,3},{8,12},{9,13},{10,... | collective-permute-start | bytes 3145736 | tf_op jit(solution)/shard_map/ppermute | solution.py:345
  129.1 113.5 %collective-permute-start.9 = (f32[32,64,128]{2,1,0:T(8,128)}, f32[32,64,128]{2,1,0:T(8,128)}, u32[]{:S(2)}, u32[]{:S(2)}) collective-permute-start(f32[32,64,128]{2,1,0:T(8,128)} %get-tuple-element.164), channel_id=1, source_target_pairs={{0,22},{1,23},{2,20},{3,21},{4,18},{5,19},{6,16},{7,17},{8,30},{9,... | collective-permute-start | bytes 3145736 | tf_op jit(solution)/shard_map/ppermute | solution.py:345
  129.7 112.9 %collective-permute-start.8 = (f32[32,64,128]{2,1,0:T(8,128)}, f32[32,64,128]{2,1,0:T(8,128)}, u32[]{:S(2)}, u32[]{:S(2)}) collective-permute-start(f32[32,64,128]{2,1,0:T(8,128)} %get-tuple-element.161), channel_id=1, source_target_pairs={{0,12},{1,13},{2,14},{3,15},{4,8},{5,9},{6,10},{7,11},{8,4},{9,5},... | collective-permute-start | bytes 3145736 | tf_op jit(solution)/shard_map/ppermute | solution.py:345
  174.2 73.8 %collective-permute-start.11 = (f32[32,64,128]{2,1,0:T(8,128)}, f32[32,64,128]{2,1,0:T(8,128)}, u32[]{:S(2)}, u32[]{:S(2)}) collective-permute-start(f32[32,64,128]{2,1,0:T(8,128)} %get-tuple-element.166), channel_id=1, source_target_pairs={{0,24},{1,25},{2,26},{3,27},{4,28},{5,29},{6,30},{7,31},{8,16},{9,... | collective-permute-start | bytes 3145736 | tf_op jit(solution)/shard_map/ppermute | solution.py:345
  176.6 92.8 %collective-permute-start.6 = (f32[32,64,128]{2,1,0:T(8,128)}, f32[32,64,128]{2,1,0:T(8,128)}, u32[]{:S(2)}, u32[]{:S(2)}) collective-permute-start(f32[32,64,128]{2,1,0:T(8,128)} %get-tuple-element.157), channel_id=1, source_target_pairs={{0,6},{1,7},{2,4},{3,5},{4,2},{5,3},{6,0},{7,1},{8,14},{9,15},{10,... | collective-permute-start | bytes 3145736 | tf_op jit(solution)/shard_map/ppermute | solution.py:345
  178.1 91.3 %collective-permute-start.12 = (f32[32,64,128]{2,1,0:T(8,128)}, f32[32,64,128]{2,1,0:T(8,128)}, u32[]{:S(2)}, u32[]{:S(2)}) collective-permute-start(f32[32,64,128]{2,1,0:T(8,128)} %get-tuple-element.167), channel_id=1, source_target_pairs={{0,26},{1,27},{2,24},{3,25},{4,30},{5,31},{6,28},{7,29},{8,18},{9,... | collective-permute-start | bytes 3145736 | tf_op jit(solution)/shard_map/ppermute | solution.py:345
  242.6 92.1 %collective-permute-start.10 = (f32[32,64,128]{2,1,0:T(8,128)}, f32[32,64,128]{2,1,0:T(8,128)}, u32[]{:S(2)}, u32[]{:S(2)}) collective-permute-start(f32[32,64,128]{2,1,0:T(8,128)} %get-tuple-element.165), channel_id=1, source_target_pairs={{0,14},{1,15},{2,12},{3,13},{4,10},{5,11},{6,8},{7,9},{8,6},{9,7},... | collective-permute-start | bytes 3145736 | tf_op jit(solution)/shard_map/ppermute | solution.py:345
  242.6 92.1 %collective-permute-start.13 = (f32[32,64,128]{2,1,0:T(8,128)}, f32[32,64,128]{2,1,0:T(8,128)}, u32[]{:S(2)}, u32[]{:S(2)}) collective-permute-start(f32[32,64,128]{2,1,0:T(8,128)} %get-tuple-element.168), channel_id=1, source_target_pairs={{0,28},{1,29},{2,30},{3,31},{4,24},{5,25},{6,26},{7,27},{8,20},{9,... | collective-permute-start | bytes 3145736 | tf_op jit(solution)/shard_map/ppermute | solution.py:345
  247.9 90.6 %collective-permute-start.14 = (f32[32,64,128]{2,1,0:T(8,128)}, f32[32,64,128]{2,1,0:T(8,128)}, u32[]{:S(2)}, u32[]{:S(2)}) collective-permute-start(f32[32,64,128]{2,1,0:T(8,128)} %get-tuple-element.169), channel_id=1, source_target_pairs={{0,30},{1,31},{2,28},{3,29},{4,26},{5,27},{6,24},{7,25},{8,22},{9,... | collective-permute-start | bytes 3145736 | tf_op jit(solution)/shard_map/ppermute | solution.py:345
  269.4 199.5 %collective-permute-start.16 = (f32[32,64,128]{2,1,0:T(8,128)}, f32[32,64,128]{2,1,0:T(8,128)S(1)}, u32[]{:S(2)}, u32[]{:S(2)}) collective-permute-start(f32[32,64,128]{2,1,0:T(8,128)} %get-tuple-element.181), channel_id=1, source_target_pairs={{0,16},{1,17},{2,18},{3,19},{4,20},{5,21},{6,22},{7,23},{8,24},{9,... | collective-permute-start | bytes 3145736 | tf_op jit(solution)/shard_map/ppermute | solution.py:345
  334.0 134.8 %collective-permute-start.17 = (f32[32,64,128]{2,1,0:T(8,128)}, f32[32,64,128]{2,1,0:T(8,128)S(1)}, u32[]{:S(2)}, u32[]{:S(2)}) collective-permute-start(f32[32,64,128]{2,1,0:T(8,128)} %get-tuple-element.182), channel_id=1, source_target_pairs={{0,8},{1,9},{2,10},{3,11},{4,12},{5,13},{6,14},{7,15},{8,0},{9,1},... | collective-permute-start | bytes 3145736 | tf_op jit(solution)/shard_map/ppermute | solution.py:345
  334.6 134.9 %collective-permute-start.15 = (f32[32,64,128]{2,1,0:T(8,128)}, f32[32,64,128]{2,1,0:T(8,128)S(1)}, u32[]{:S(2)}, u32[]{:S(2)}) collective-permute-start(f32[32,64,128]{2,1,0:T(8,128)} %get-tuple-element.176), channel_id=1, source_target_pairs={{0,2},{1,3},{2,0},{3,1},{4,6},{5,7},{6,4},{7,5},{8,10},{9,11},{10,... | collective-permute-start | bytes 3145736 | tf_op jit(solution)/shard_map/ppermute | solution.py:345
  336.1 135.4 %collective-permute-start.22 = (f32[32,64,128]{2,1,0:T(8,128)}, f32[32,64,128]{2,1,0:T(8,128)}, u32[]{:S(2)}, u32[]{:S(2)}) collective-permute-start(f32[32,64,128]{2,1,0:T(8,128)} %get-tuple-element.193), channel_id=1, source_target_pairs={{0,24},{1,25},{2,26},{3,27},{4,28},{5,29},{6,30},{7,31},{8,16},{9,... | collective-permute-start | bytes 3145736 | tf_op jit(solution)/shard_map/ppermute | solution.py:345
  338.5 197.8 %collective-permute-start.19 = (f32[32,64,128]{2,1,0:T(8,128)}, f32[32,64,128]{2,1,0:T(8,128)}, u32[]{:S(2)}, u32[]{:S(2)}) collective-permute-start(f32[32,64,128]{2,1,0:T(8,128)} %get-tuple-element.188), channel_id=1, source_target_pairs={{0,18},{1,19},{2,16},{3,17},{4,22},{5,23},{6,20},{7,21},{8,26},{9,... | collective-permute-start | bytes 3145736 | tf_op jit(solution)/shard_map/ppermute | solution.py:345
  468.8 72.3 %collective-permute-start.20 = (f32[32,64,128]{2,1,0:T(8,128)}, f32[32,64,128]{2,1,0:T(8,128)}, u32[]{:S(2)}, u32[]{:S(2)}) collective-permute-start(f32[32,64,128]{2,1,0:T(8,128)} %get-tuple-element.189), channel_id=1, source_target_pairs={{0,10},{1,11},{2,8},{3,9},{4,14},{5,15},{6,12},{7,13},{8,2},{9,3},... | collective-permute-start | bytes 3145736 | tf_op jit(solution)/shard_map/ppermute | solution.py:345
  468.9 72.2 %collective-permute-start.18 = (f32[32,64,128]{2,1,0:T(8,128)}, f32[32,64,128]{2,1,0:T(8,128)}, u32[]{:S(2)}, u32[]{:S(2)}) collective-permute-start(f32[32,64,128]{2,1,0:T(8,128)} %get-tuple-element.183), channel_id=1, source_target_pairs={{0,4},{1,5},{2,6},{3,7},{4,0},{5,1},{6,2},{7,3},{8,12},{9,13},{10,... | collective-permute-start | bytes 3145736 | tf_op jit(solution)/shard_map/ppermute | solution.py:345
  469.6 73.8 %collective-permute-start.24 = (f32[32,64,128]{2,1,0:T(8,128)}, f32[32,64,128]{2,1,0:T(8,128)}, u32[]{:S(2)}, u32[]{:S(2)}) collective-permute-start(f32[32,64,128]{2,1,0:T(8,128)} %get-tuple-element.197), channel_id=1, source_target_pairs={{0,26},{1,27},{2,24},{3,25},{4,30},{5,31},{6,28},{7,29},{8,18},{9,... | collective-permute-start | bytes 3145736 | tf_op jit(solution)/shard_map/ppermute | solution.py:345
  471.5 156.6 %collective-permute-start.23 = (f32[32,64,128]{2,1,0:T(8,128)}, f32[32,64,128]{2,1,0:T(8,128)}, u32[]{:S(2)}, u32[]{:S(2)}) collective-permute-start(f32[32,64,128]{2,1,0:T(8,128)} %get-tuple-element.194), channel_id=1, source_target_pairs={{0,12},{1,13},{2,14},{3,15},{4,8},{5,9},{6,10},{7,11},{8,4},{9,5},... | collective-permute-start | bytes 3145736 | tf_op jit(solution)/shard_map/ppermute | solution.py:345
  536.3 93.4 %collective-permute-start.26 = (f32[32,64,128]{2,1,0:T(8,128)}, f32[32,64,128]{2,1,0:T(8,128)}, u32[]{:S(2)}, u32[]{:S(2)}) collective-permute-start(f32[32,64,128]{2,1,0:T(8,128)} %get-tuple-element.199), channel_id=1, source_target_pairs={{0,20},{1,21},{2,22},{3,23},{4,16},{5,17},{6,18},{7,19},{8,28},{9,... | collective-permute-start | bytes 3145736 | tf_op jit(solution)/shard_map/ppermute | solution.py:345
  541.1 113.0 %collective-permute-start.21 = (f32[32,64,128]{2,1,0:T(8,128)}, f32[32,64,128]{2,1,0:T(8,128)}, u32[]{:S(2)}, u32[]{:S(2)}) collective-permute-start(f32[32,64,128]{2,1,0:T(8,128)} %get-tuple-element.190), channel_id=1, source_target_pairs={{0,6},{1,7},{2,4},{3,5},{4,2},{5,3},{6,0},{7,1},{8,14},{9,15},{10,... | collective-permute-start | bytes 3145736 | tf_op jit(solution)/shard_map/ppermute | solution.py:345
  541.1 113.0 %collective-permute-start.28 = (f32[32,64,128]{2,1,0:T(8,128)}, f32[32,64,128]{2,1,0:T(8,128)}, u32[]{:S(2)}, u32[]{:S(2)}) collective-permute-start(f32[32,64,128]{2,1,0:T(8,128)} %get-tuple-element.201), channel_id=1, source_target_pairs={{0,28},{1,29},{2,30},{3,31},{4,24},{5,25},{6,26},{7,27},{8,20},{9,... | collective-permute-start | bytes 3145736 | tf_op jit(solution)/shard_map/ppermute | solution.py:345
  543.3 153.9 %collective-permute-start.25 = (f32[32,64,128]{2,1,0:T(8,128)}, f32[32,64,128]{2,1,0:T(8,128)}, u32[]{:S(2)}, u32[]{:S(2)}) collective-permute-start(f32[32,64,128]{2,1,0:T(8,128)} %get-tuple-element.198), channel_id=1, source_target_pairs={{0,14},{1,15},{2,12},{3,13},{4,10},{5,11},{6,8},{7,9},{8,6},{9,7},... | collective-permute-start | bytes 3145736 | tf_op jit(solution)/shard_map/ppermute | solution.py:345
  628.2 112.0 %collective-permute-start.27 = (f32[32,64,128]{2,1,0:T(8,128)}, f32[32,64,128]{2,1,0:T(8,128)}, u32[]{:S(2)}, u32[]{:S(2)}) collective-permute-start(f32[32,64,128]{2,1,0:T(8,128)} %get-tuple-element.200), channel_id=1, source_target_pairs={{0,22},{1,23},{2,20},{3,21},{4,18},{5,19},{6,16},{7,17},{8,30},{9,... | collective-permute-start | bytes 3145736 | tf_op jit(solution)/shard_map/ppermute | solution.py:345
  629.7 114.0 %collective-permute-start.29 = (f32[32,64,128]{2,1,0:T(8,128)}, f32[32,64,128]{2,1,0:T(8,128)}, u32[]{:S(2)}, u32[]{:S(2)}) collective-permute-start(f32[32,64,128]{2,1,0:T(8,128)} %get-tuple-element.202), channel_id=1, source_target_pairs={{0,30},{1,31},{2,28},{3,29},{4,26},{5,27},{6,24},{7,25},{8,22},{9,... | collective-permute-start | bytes 3145736 | tf_op jit(solution)/shard_map/ppermute | solution.py:345
  654.1 174.9 %collective-permute-start.31 = (f32[32,64,128]{2,1,0:T(8,128)}, f32[32,64,128]{2,1,0:T(8,128)S(1)}, u32[]{:S(2)}, u32[]{:S(2)}) collective-permute-start(f32[32,64,128]{2,1,0:T(8,128)} %get-tuple-element.214), channel_id=1, source_target_pairs={{0,16},{1,17},{2,18},{3,19},{4,20},{5,21},{6,22},{7,23},{8,24},{9,... | collective-permute-start | bytes 3145736 | tf_op jit(solution)/shard_map/ppermute | solution.py:345
  696.4 132.6 %collective-permute-start.32 = (f32[32,64,128]{2,1,0:T(8,128)}, f32[32,64,128]{2,1,0:T(8,128)S(1)}, u32[]{:S(2)}, u32[]{:S(2)}) collective-permute-start(f32[32,64,128]{2,1,0:T(8,128)} %get-tuple-element.215), channel_id=1, source_target_pairs={{0,8},{1,9},{2,10},{3,11},{4,12},{5,13},{6,14},{7,15},{8,0},{9,1},... | collective-permute-start | bytes 3145736 | tf_op jit(solution)/shard_map/ppermute | solution.py:345
  740.2 91.9 %collective-permute-start.30 = (f32[32,64,128]{2,1,0:T(8,128)}, f32[32,64,128]{2,1,0:T(8,128)S(1)}, u32[]{:S(2)}, u32[]{:S(2)}) collective-permute-start(f32[32,64,128]{2,1,0:T(8,128)} %get-tuple-element.209), channel_id=1, source_target_pairs={{0,2},{1,3},{2,0},{3,1},{4,6},{5,7},{6,4},{7,5},{8,10},{9,11},{10,... | collective-permute-start | bytes 3145736 | tf_op jit(solution)/shard_map/ppermute | solution.py:345
  743.1 91.0 %collective-permute-start.37 = (f32[32,64,128]{2,1,0:T(8,128)}, f32[32,64,128]{2,1,0:T(8,128)}, u32[]{:S(2)}, u32[]{:S(2)}) collective-permute-start(f32[32,64,128]{2,1,0:T(8,128)} %get-tuple-element.226), channel_id=1, source_target_pairs={{0,24},{1,25},{2,26},{3,27},{4,28},{5,29},{6,30},{7,31},{8,16},{9,... | collective-permute-start | bytes 3145736 | tf_op jit(solution)/shard_map/ppermute | solution.py:345
  743.8 154.5 %collective-permute-start.34 = (f32[32,64,128]{2,1,0:T(8,128)}, f32[32,64,128]{2,1,0:T(8,128)}, u32[]{:S(2)}, u32[]{:S(2)}) collective-permute-start(f32[32,64,128]{2,1,0:T(8,128)} %get-tuple-element.221), channel_id=1, source_target_pairs={{0,18},{1,19},{2,16},{3,17},{4,22},{5,23},{6,20},{7,21},{8,26},{9,... | collective-permute-start | bytes 3145736 | tf_op jit(solution)/shard_map/ppermute | solution.py:345
  829.0 71.4 %collective-permute-start.35 = (f32[32,64,128]{2,1,0:T(8,128)}, f32[32,64,128]{2,1,0:T(8,128)}, u32[]{:S(2)}, u32[]{:S(2)}) collective-permute-start(f32[32,64,128]{2,1,0:T(8,128)} %get-tuple-element.222), channel_id=1, source_target_pairs={{0,10},{1,11},{2,8},{3,9},{4,14},{5,15},{6,12},{7,13},{8,2},{9,3},... | collective-permute-start | bytes 3145736 | tf_op jit(solution)/shard_map/ppermute | solution.py:345
  829.0 71.9 %collective-permute-start.33 = (f32[32,64,128]{2,1,0:T(8,128)}, f32[32,64,128]{2,1,0:T(8,128)}, u32[]{:S(2)}, u32[]{:S(2)}) collective-permute-start(f32[32,64,128]{2,1,0:T(8,128)} %get-tuple-element.216), channel_id=1, source_target_pairs={{0,4},{1,5},{2,6},{3,7},{4,0},{5,1},{6,2},{7,3},{8,12},{9,13},{10,... | collective-permute-start | bytes 3145736 | tf_op jit(solution)/shard_map/ppermute | solution.py:345
  832.1 73.1 %collective-permute-start.39 = (f32[32,64,128]{2,1,0:T(8,128)}, f32[32,64,128]{2,1,0:T(8,128)}, u32[]{:S(2)}, u32[]{:S(2)}) collective-permute-start(f32[32,64,128]{2,1,0:T(8,128)} %get-tuple-element.230), channel_id=1, source_target_pairs={{0,26},{1,27},{2,24},{3,25},{4,30},{5,31},{6,28},{7,29},{8,18},{9,... | collective-permute-start | bytes 3145736 | tf_op jit(solution)/shard_map/ppermute | solution.py:345
  834.0 155.2 %collective-permute-start.38 = (f32[32,64,128]{2,1,0:T(8,128)}, f32[32,64,128]{2,1,0:T(8,128)}, u32[]{:S(2)}, u32[]{:S(2)}) collective-permute-start(f32[32,64,128]{2,1,0:T(8,128)} %get-tuple-element.227), channel_id=1, source_target_pairs={{0,12},{1,13},{2,14},{3,15},{4,8},{5,9},{6,10},{7,11},{8,4},{9,5},... | collective-permute-start | bytes 3145736 | tf_op jit(solution)/shard_map/ppermute | solution.py:345
  898.3 94.0 %collective-permute-start.41 = (f32[32,64,128]{2,1,0:T(8,128)}, f32[32,64,128]{2,1,0:T(8,128)}, u32[]{:S(2)}, u32[]{:S(2)}) collective-permute-start(f32[32,64,128]{2,1,0:T(8,128)} %get-tuple-element.232), channel_id=1, source_target_pairs={{0,20},{1,21},{2,22},{3,23},{4,16},{5,17},{6,18},{7,19},{8,28},{9,... | collective-permute-start | bytes 3145736 | tf_op jit(solution)/shard_map/ppermute | solution.py:345
  900.4 115.8 %collective-permute-start.36 = (f32[32,64,128]{2,1,0:T(8,128)}, f32[32,64,128]{2,1,0:T(8,128)}, u32[]{:S(2)}, u32[]{:S(2)}) collective-permute-start(f32[32,64,128]{2,1,0:T(8,128)} %get-tuple-element.223), channel_id=1, source_target_pairs={{0,6},{1,7},{2,4},{3,5},{4,2},{5,3},{6,0},{7,1},{8,14},{9,15},{10,... | collective-permute-start | bytes 3145736 | tf_op jit(solution)/shard_map/ppermute | solution.py:345
  900.9 115.3 %collective-permute-start.43 = (f32[32,64,128]{2,1,0:T(8,128)}, f32[32,64,128]{2,1,0:T(8,128)}, u32[]{:S(2)}, u32[]{:S(2)}) collective-permute-start(f32[32,64,128]{2,1,0:T(8,128)} %get-tuple-element.234), channel_id=1, source_target_pairs={{0,28},{1,29},{2,30},{3,31},{4,24},{5,25},{6,26},{7,27},{8,20},{9,... | collective-permute-start | bytes 3145736 | tf_op jit(solution)/shard_map/ppermute | solution.py:345
  905.2 153.9 %collective-permute-start.40 = (f32[32,64,128]{2,1,0:T(8,128)}, f32[32,64,128]{2,1,0:T(8,128)}, u32[]{:S(2)}, u32[]{:S(2)}) collective-permute-start(f32[32,64,128]{2,1,0:T(8,128)} %get-tuple-element.231), channel_id=1, source_target_pairs={{0,14},{1,15},{2,12},{3,13},{4,10},{5,11},{6,8},{7,9},{8,6},{9,7},... | collective-permute-start | bytes 3145736 | tf_op jit(solution)/shard_map/ppermute | solution.py:345
  989.2 112.6 %collective-permute-start.42 = (f32[32,64,128]{2,1,0:T(8,128)}, f32[32,64,128]{2,1,0:T(8,128)}, u32[]{:S(2)}, u32[]{:S(2)}) collective-permute-start(f32[32,64,128]{2,1,0:T(8,128)} %get-tuple-element.233), channel_id=1, source_target_pairs={{0,22},{1,23},{2,20},{3,21},{4,18},{5,19},{6,16},{7,17},{8,30},{9,... | collective-permute-start | bytes 3145736 | tf_op jit(solution)/shard_map/ppermute | solution.py:345
  992.2 112.8 %collective-permute-start.44 = (f32[32,64,128]{2,1,0:T(8,128)}, f32[32,64,128]{2,1,0:T(8,128)}, u32[]{:S(2)}, u32[]{:S(2)}) collective-permute-start(f32[32,64,128]{2,1,0:T(8,128)} %get-tuple-element.235), channel_id=1, source_target_pairs={{0,30},{1,31},{2,28},{3,29},{4,26},{5,27},{6,24},{7,25},{8,22},{9,... | collective-permute-start | bytes 3145736 | tf_op jit(solution)/shard_map/ppermute | solution.py:345
  1016.2 174.5 %collective-permute-start.46 = (f32[32,64,128]{2,1,0:T(8,128)}, f32[32,64,128]{2,1,0:T(8,128)S(1)}, u32[]{:S(2)}, u32[]{:S(2)}) collective-permute-start(f32[32,64,128]{2,1,0:T(8,128)} %get-tuple-element.247), channel_id=1, source_target_pairs={{0,16},{1,17},{2,18},{3,19},{4,20},{5,21},{6,22},{7,23},{8,24},{9,... | collective-permute-start | bytes 3145736 | tf_op jit(solution)/shard_map/ppermute | solution.py:345
  1056.3 134.4 %collective-permute-start.47 = (f32[32,64,128]{2,1,0:T(8,128)}, f32[32,64,128]{2,1,0:T(8,128)S(1)}, u32[]{:S(2)}, u32[]{:S(2)}) collective-permute-start(f32[32,64,128]{2,1,0:T(8,128)} %get-tuple-element.248), channel_id=1, source_target_pairs={{0,8},{1,9},{2,10},{3,11},{4,12},{5,13},{6,14},{7,15},{8,0},{9,1},... | collective-permute-start | bytes 3145736 | tf_op jit(solution)/shard_map/ppermute | solution.py:345
  1101.8 92.2 %collective-permute-start.45 = (f32[32,64,128]{2,1,0:T(8,128)}, f32[32,64,128]{2,1,0:T(8,128)S(1)}, u32[]{:S(2)}, u32[]{:S(2)}) collective-permute-start(f32[32,64,128]{2,1,0:T(8,128)} %get-tuple-element.242), channel_id=1, source_target_pairs={{0,2},{1,3},{2,0},{3,1},{4,6},{5,7},{6,4},{7,5},{8,10},{9,11},{10,... | collective-permute-start | bytes 3145736 | tf_op jit(solution)/shard_map/ppermute | solution.py:345
  1105.0 91.0 %collective-permute-start.52 = (f32[32,64,128]{2,1,0:T(8,128)}, f32[32,64,128]{2,1,0:T(8,128)}, u32[]{:S(2)}, u32[]{:S(2)}) collective-permute-start(f32[32,64,128]{2,1,0:T(8,128)} %get-tuple-element.259), channel_id=1, source_target_pairs={{0,24},{1,25},{2,26},{3,27},{4,28},{5,29},{6,30},{7,31},{8,16},{9,... | collective-permute-start | bytes 3145736 | tf_op jit(solution)/shard_map/ppermute | solution.py:345
  1105.0 155.8 %collective-permute-start.49 = (f32[32,64,128]{2,1,0:T(8,128)}, f32[32,64,128]{2,1,0:T(8,128)}, u32[]{:S(2)}, u32[]{:S(2)}) collective-permute-start(f32[32,64,128]{2,1,0:T(8,128)} %get-tuple-element.254), channel_id=1, source_target_pairs={{0,18},{1,19},{2,16},{3,17},{4,22},{5,23},{6,20},{7,21},{8,26},{9,... | collective-permute-start | bytes 3145736 | tf_op jit(solution)/shard_map/ppermute | solution.py:345
  1190.7 88.2 %collective-permute-start.50 = (f32[32,64,128]{2,1,0:T(8,128)}, f32[32,64,128]{2,1,0:T(8,128)}, u32[]{:S(2)}, u32[]{:S(2)}) collective-permute-start(f32[32,64,128]{2,1,0:T(8,128)} %get-tuple-element.255), channel_id=1, source_target_pairs={{0,10},{1,11},{2,8},{3,9},{4,14},{5,15},{6,12},{7,13},{8,2},{9,3},... | collective-permute-start | bytes 3145736 | tf_op jit(solution)/shard_map/ppermute | solution.py:345
  1190.7 89.8 %collective-permute-start.48 = (f32[32,64,128]{2,1,0:T(8,128)}, f32[32,64,128]{2,1,0:T(8,128)}, u32[]{:S(2)}, u32[]{:S(2)}) collective-permute-start(f32[32,64,128]{2,1,0:T(8,128)} %get-tuple-element.249), channel_id=1, source_target_pairs={{0,4},{1,5},{2,6},{3,7},{4,0},{5,1},{6,2},{7,3},{8,12},{9,13},{10,... | collective-permute-start | bytes 3145736 | tf_op jit(solution)/shard_map/ppermute | solution.py:345
  1194.1 88.1 %collective-permute-start.54 = (f32[32,64,128]{2,1,0:T(8,128)}, f32[32,64,128]{2,1,0:T(8,128)}, u32[]{:S(2)}, u32[]{:S(2)}) collective-permute-start(f32[32,64,128]{2,1,0:T(8,128)} %get-tuple-element.263), channel_id=1, source_target_pairs={{0,26},{1,27},{2,24},{3,25},{4,30},{5,31},{6,28},{7,29},{8,18},{9,... | collective-permute-start | bytes 3145736 | tf_op jit(solution)/shard_map/ppermute | solution.py:345
  1196.0 133.8 %collective-permute-start.53 = (f32[32,64,128]{2,1,0:T(8,128)}, f32[32,64,128]{2,1,0:T(8,128)}, u32[]{:S(2)}, u32[]{:S(2)}) collective-permute-start(f32[32,64,128]{2,1,0:T(8,128)} %get-tuple-element.260), channel_id=1, source_target_pairs={{0,12},{1,13},{2,14},{3,15},{4,8},{5,9},{6,10},{7,11},{8,4},{9,5},... | collective-permute-start | bytes 3145736 | tf_op jit(solution)/shard_map/ppermute | solution.py:345
  1260.8 90.5 %collective-permute-start.56 = (f32[32,64,128]{2,1,0:T(8,128)}, f32[32,64,128]{2,1,0:T(8,128)}, u32[]{:S(2)}, u32[]{:S(2)}) collective-permute-start(f32[32,64,128]{2,1,0:T(8,128)} %get-tuple-element.265), channel_id=1, source_target_pairs={{0,20},{1,21},{2,22},{3,23},{4,16},{5,17},{6,18},{7,19},{8,28},{9,... | collective-permute-start | bytes 3145736 | tf_op jit(solution)/shard_map/ppermute | solution.py:345
  1278.9 115.3 %collective-permute-start.51 = (f32[32,64,128]{2,1,0:T(8,128)}, f32[32,64,128]{2,1,0:T(8,128)S(1)}, u32[]{:S(2)}, u32[]{:S(2)}) collective-permute-start(f32[32,64,128]{2,1,0:T(8,128)} %get-tuple-element.256), channel_id=1, source_target_pairs={{0,6},{1,7},{2,4},{3,5},{4,2},{5,3},{6,0},{7,1},{8,14},{9,15},{10,... | collective-permute-start | bytes 3145736 | tf_op jit(solution)/shard_map/ppermute | solution.py:345
  1280.5 113.7 %collective-permute-start.58 = (f32[32,64,128]{2,1,0:T(8,128)}, f32[32,64,128]{2,1,0:T(8,128)S(1)}, u32[]{:S(2)}, u32[]{:S(2)}) collective-permute-start(f32[32,64,128]{2,1,0:T(8,128)} %get-tuple-element.267), channel_id=1, source_target_pairs={{0,28},{1,29},{2,30},{3,31},{4,24},{5,25},{6,26},{7,27},{8,20},{9,... | collective-permute-start | bytes 3145736 | tf_op jit(solution)/shard_map/ppermute | solution.py:345
  1282.1 112.1 %collective-permute-start.55 = (f32[32,64,128]{2,1,0:T(8,128)}, f32[32,64,128]{2,1,0:T(8,128)S(1)}, u32[]{:S(2)}, u32[]{:S(2)}) collective-permute-start(f32[32,64,128]{2,1,0:T(8,128)} %get-tuple-element.264), channel_id=1, source_target_pairs={{0,14},{1,15},{2,12},{3,13},{4,10},{5,11},{6,8},{7,9},{8,6},{9,7},... | collective-permute-start | bytes 3145736 | tf_op jit(solution)/shard_map/ppermute | solution.py:345
  1329.8 115.0 %collective-permute-start.57 = (f32[32,64,128]{2,1,0:T(8,128)}, f32[32,64,128]{2,1,0:T(8,128)}, u32[]{:S(2)}, u32[]{:S(2)}) collective-permute-start(f32[32,64,128]{2,1,0:T(8,128)} %get-tuple-element.266), channel_id=1, source_target_pairs={{0,22},{1,23},{2,20},{3,21},{4,18},{5,19},{6,16},{7,17},{8,30},{9,... | collective-permute-start | bytes 3145736 | tf_op jit(solution)/shard_map/ppermute | solution.py:345
  1351.3 93.5 %collective-permute-start.59 = (f32[32,64,128]{2,1,0:T(8,128)}, f32[32,64,128]{2,1,0:T(8,128)}, u32[]{:S(2)}, u32[]{:S(2)}) collective-permute-start(f32[32,64,128]{2,1,0:T(8,128)} %get-tuple-element.268), channel_id=1, source_target_pairs={{0,30},{1,31},{2,28},{3,29},{4,26},{5,27},{6,24},{7,25},{8,22},{9,... | collective-permute-start | bytes 3145736 | tf_op jit(solution)/shard_map/ppermute | solution.py:345
  1475.4 25.7 %collective-permute-start.64 = (f32[16,512]{1,0:T(8,128)S(1)}, f32[16,512]{1,0:T(8,128)S(1)}, u32[]{:S(2)}, u32[]{:S(2)}) collective-permute-start(f32[16,512]{1,0:T(8,128)S(1)} %get-tuple-element.316), channel_id=1, source_target_pairs={{0,8},{1,9},{2,10},{3,11},{4,12},{5,13},{6,14},{7,15},{8,0},{9,1},... | collective-permute-start | bytes 98312 | tf_op jit(solution)/shard_map/ppermute | solution.py:345
  1561.4 17.4 %collective-permute-start.75 = (f32[16,64,256]{2,1,0:T(8,128)}, f32[16,64,256]{2,1,0:T(8,128)S(1)}, u32[]{:S(2)}, u32[]{:S(2)}) collective-permute-start(f32[16,64,256]{2,1,0:T(8,128)} %get-tuple-element.276), channel_id=1, source_target_pairs={{0,1},{1,0},{2,3},{3,2},{4,5},{5,4},{6,7},{7,6},{8,9},{9,8},{10,11... | collective-permute-start | bytes 3145736 | tf_op jit(solution)/shard_map/ppermute | solution.py:345
  1561.9 16.9 %collective-permute-start.76 = (f32[16,64,256]{2,1,0:T(8,128)}, f32[16,64,256]{2,1,0:T(8,128)S(1)}, u32[]{:S(2)}, u32[]{:S(2)}) collective-permute-start(f32[16,64,256]{2,1,0:T(8,128)} %get-tuple-element.277), channel_id=1, source_target_pairs={{0,1},{1,0},{2,3},{3,2},{4,5},{5,4},{6,7},{7,6},{8,9},{9,8},{10,11... | collective-permute-start | bytes 3145736 | tf_op jit(solution)/shard_map/ppermute | solution.py:345
  1562.0 16.8 %collective-permute-start.77 = (f32[16,64,256]{2,1,0:T(8,128)}, f32[16,64,256]{2,1,0:T(8,128)S(1)}, u32[]{:S(2)}, u32[]{:S(2)}) collective-permute-start(f32[16,64,256]{2,1,0:T(8,128)} %get-tuple-element.278), channel_id=1, source_target_pairs={{0,1},{1,0},{2,3},{3,2},{4,5},{5,4},{6,7},{7,6},{8,9},{9,8},{10,11... | collective-permute-start | bytes 3145736 | tf_op jit(solution)/shard_map/ppermute | solution.py:345
  (46 other events, 2128.3 us)

commit v4 on v3

--- a/solution.py
+++ b/solution.py
@@ -18,6 +18,7 @@
 GRAM_X = 4
 GRAM_Y_X = 4
 CORE_X = 8
+BLOCK = 8
 VMEM_LIMIT = 60 << 20
 F32 = jnp.float32
 BF16 = jnp.bfloat16
@@ -155,29 +156,36 @@
 
 def inverse_factor(inner):
     rank = inner.shape[0]
-    row_id = lax.broadcasted_iota(jnp.int32, (rank, 1), 0)
-    rows = lax.broadcasted_iota(jnp.int32, (rank, 2 * rank), 0)
-    lanes = lax.broadcasted_iota(jnp.int32, (rank, 2 * rank), 1)
-    eye = jnp.where(lanes[:, :rank] == rows[:, :rank], 1.0, 0.0).astype(F32)
+    rows = lax.broadcasted_iota(jnp.int32, (rank, rank), 0)
+    lanes = lax.broadcasted_iota(jnp.int32, (rank, rank), 1)
+    eye = jnp.where(lanes == rows, 1.0, 0.0).astype(F32)
     work = jnp.concatenate([inner, eye], axis=1)
-    for k in range(0, rank - 2, 2):
-        col0 = jnp.broadcast_to(work[:, k:k + 1], work.shape)
-        col1 = jnp.broadcast_to(work[:, k + 1:k + 2], work.shape)
-        row0, row1 = work[k:k + 1, :], work[k + 1:k + 2, :]
-        inv0 = 1.0 / col0[k:k + 1, :]
-        share = col1[k:k + 1, :] * inv0
-        inv1 = 1.0 / (col1[k + 1:k + 2, :] - col1[k:k + 1, :] * share)
-        use1 = (row1 - share * row0) * inv1
-        use0 = row0 * inv0 - share * use1
-        below = row_id > k + 1
-        work = work - (jnp.where(below, col0, 0.0) * use0 + jnp.where(below, col1, 0.0) * use1)
-    take = lambda mask: jnp.sum(jnp.where(mask, work, 0.0), axis=1, keepdims=True)
-    above = pltpu.roll(work, 1, 0)
-    left = take(lanes == rows - 1)
-    pivot_above = jnp.sum(jnp.where(lanes == rows - 1, above, 0.0), axis=1, keepdims=True)
-    share = jnp.where(row_id % 2 == 1, left / jnp.where(row_id == 0, 1.0, pivot_above), 0.0)
-    work = work - share * above
-    return work[:, rank:] * (1.0 / jnp.sqrt(take(lanes == rows)))
+    finished = []
+    for start in range(0, rank, BLOCK):
+        cols = [jnp.broadcast_to(work[:, start + j:start + j + 1], work.shape) for j in range(BLOCK)]
+        entry = {(i, j): cols[j][i:i + 1, :] for i in range(BLOCK) for j in range(i + 1)}
+        row = [work[i:i + 1, :] for i in range(BLOCK)]
+        scale, factor = [], {}
+        for j in range(BLOCK):
+            scale.append(1.0 / entry[j, j])
+            finished.append((row[j] * (1.0 / jnp.sqrt(entry[j, j])))[:, rank:])
+            for i in range(j + 1, BLOCK):
+                factor[i, j] = entry[i, j] * scale[j]
+            for i in range(j + 1, BLOCK):
+                for t in range(j + 1, i + 1):
+                    entry[i, t] = entry[i, t] - factor[i, j] * entry[t, j]
+                row[i] = row[i] - factor[i, j] * row[j]
+        if start + BLOCK == rank:
+            break
+        use = [row[j] * scale[j] for j in range(BLOCK)]
+        for i in reversed(range(BLOCK)):
+            for j in range(i):
+                use[j] = use[j] - factor[i, j] * use[i]
+        total = cols[0][BLOCK:] * use[0]
+        for j in range(1, BLOCK):
+            total = total + cols[j][BLOCK:] * use[j]
+        work = work[BLOCK:] - total
+    return jnp.concatenate(finished, axis=0)
 
 
 def basis_kernel(gz_n, me_ref, gram_ref, start_ref, basis_ref, turned_ref, *parts):

time: 1680 us -> 1660 us (0.988)
  no operation moved by 1% of the time
where the time goes in v4:
time: 1660 us; the launch traced here: 1650 us
  starting transfers between devices  721 us (43%)
  waiting for transfers between devices  675 us (41%)
  Pallas kernels  237 us (14%)
    ppermute x92, starting transfers between devices, permute(): return lax.ppermute(value, AXES, [(i, i ^ mask) for i in range(total)])  721 us
    ppermute x92, waiting for transfers between devices, permute(): return lax.ppermute(value, AXES, [(i, i ^ mask) for i in range(total)])  675 us
    pallas_call x9, Pallas kernels, pack(): pl.pallas_call(functools.partial(pack_kernel, count, width), grid_spec=pl...  91.6 us
    pallas_call x4, Pallas kernels, gram_z_step(): pl.pallas_call(functools.partial(gram_z_kernel, groups, side), grid_spec=...  67.1 us
  transfers between devices with their start and end apart: 92, of which 44 were waited for; matrix products, arithmetic and copies ran while one was open for 0% of the time, Pallas kernels for 9%

profile of v4, /device:TPU:0, one launch (start us, length us, event | category | flops | bytes accessed | tf_op | source)
XLA Modules:
  0.0 1649.9 jit_solution(5100657845502109590)
XLA Ops:
  1.3 8.3 pack.9
  9.6 4.0 collective-permute-start.1
  14.3 8.3 pack.10
  22.6 10.7 pack.11
  36.7 3.6 collective-permute-start.4
  40.2 21.0 %collective-permute-done.1.refs_8_ = f32[32,64,128]{2,1,0:T(8,128)S(1)} collective-permute-done((f32[32,64,128]{2,1,0:T(8,128)}, f32[32,64,128]{2,1,0:T(8,128)S(1)}, u32[]{:S(2)}, u32[]{:S(2)}) %collective-permute-start.1) | collective-permute-done | bytes 1048608 | tf_op jit(solution)/shard_map/ppermute | solution.py:353
  62.3 19.8 %collective-permute-done.2.refs_4_ = f32[32,64,128]{2,1,0:T(8,128)S(1)} collective-permute-done((f32[32,64,128]{2,1,0:T(8,128)}, f32[32,64,128]{2,1,0:T(8,128)S(1)}, u32[]{:S(2)}, u32[]{:S(2)}) %collective-permute-start.2) | collective-permute-done | bytes 1048608 | tf_op jit(solution)/shard_map/ppermute | solution.py:353
  82.1 4.8 collective-permute-start.3
  86.9 42.2 %collective-permute-done.7.refs_9_ = f32[32,64,128]{2,1,0:T(8,128)S(1)} collective-permute-done((f32[32,64,128]{2,1,0:T(8,128)}, f32[32,64,128]{2,1,0:T(8,128)S(1)}, u32[]{:S(2)}, u32[]{:S(2)}) %collective-permute-start.7) | collective-permute-done | bytes 1048608 | tf_op jit(solution)/shard_map/ppermute | solution.py:353
  129.7 3.3 collective-permute-start.8
  133.0 41.2 %collective-permute-done.4.refs_10_ = f32[32,64,128]{2,1,0:T(8,128)} collective-permute-done((f32[32,64,128]{2,1,0:T(8,128)}, f32[32,64,128]{2,1,0:T(8,128)}, u32[]{:S(2)}, u32[]{:S(2)}) %collective-permute-start.4) | collective-permute-done | bytes 1048608 | tf_op jit(solution)/shard_map/ppermute | solution.py:353
  179.2 63.4 %collective-permute-done.9.refs_11_ = f32[32,64,128]{2,1,0:T(8,128)} collective-permute-done((f32[32,64,128]{2,1,0:T(8,128)}, f32[32,64,128]{2,1,0:T(8,128)}, u32[]{:S(2)}, u32[]{:S(2)}) %collective-permute-start.9) | collective-permute-done | bytes 1048608 | tf_op jit(solution)/shard_map/ppermute | solution.py:353
  242.6 5.4 collective-permute-start.13
  247.9 10.7 pack.12
  258.7 10.7 pack.13
  269.4 64.7 %collective-permute-start.16 = (f32[32,64,128]{2,1,0:T(8,128)}, f32[32,64,128]{2,1,0:T(8,128)S(1)}, u32[]{:S(2)}, u32[]{:S(2)}) collective-permute-start(f32[32,64,128]{2,1,0:T(8,128)} %get-tuple-element.181), channel_id=1, source_target_pairs={{0,16},{1,17},{2,18},{3,19},{4,20},{5,21},{6,22},{7,23},{8,24},{9,... | collective-permute-start | bytes 3145736 | tf_op jit(solution)/shard_map/ppermute | solution.py:353
  338.5 86.2 %collective-permute-start.19 = (f32[32,64,128]{2,1,0:T(8,128)}, f32[32,64,128]{2,1,0:T(8,128)}, u32[]{:S(2)}, u32[]{:S(2)}) collective-permute-start(f32[32,64,128]{2,1,0:T(8,128)} %get-tuple-element.188), channel_id=1, source_target_pairs={{0,18},{1,19},{2,16},{3,17},{4,22},{5,23},{6,20},{7,21},{8,26},{9,... | collective-permute-start | bytes 3145736 | tf_op jit(solution)/shard_map/ppermute | solution.py:353
  424.8 44.0 %collective-permute-done.16.refs_8_.refs_24_ = f32[32,64,128]{2,1,0:T(8,128)S(1)} collective-permute-done((f32[32,64,128]{2,1,0:T(8,128)}, f32[32,64,128]{2,1,0:T(8,128)S(1)}, u32[]{:S(2)}, u32[]{:S(2)}) %collective-permute-start.16) | collective-permute-done | bytes 1048608 | tf_op jit(solution)/shard_map/ppermute | solution.py:353
  471.5 20.5 %collective-permute-start.23 = (f32[32,64,128]{2,1,0:T(8,128)}, f32[32,64,128]{2,1,0:T(8,128)}, u32[]{:S(2)}, u32[]{:S(2)}) collective-permute-start(f32[32,64,128]{2,1,0:T(8,128)} %get-tuple-element.194), channel_id=1, source_target_pairs={{0,12},{1,13},{2,14},{3,15},{4,8},{5,9},{6,10},{7,11},{8,4},{9,5},... | collective-permute-start | bytes 3145736 | tf_op jit(solution)/shard_map/ppermute | solution.py:353
  492.1 44.3 %collective-permute-done.19.refs_9_.refs_25_ = f32[32,64,128]{2,1,0:T(8,128)} collective-permute-done((f32[32,64,128]{2,1,0:T(8,128)}, f32[32,64,128]{2,1,0:T(8,128)}, u32[]{:S(2)}, u32[]{:S(2)}) %collective-permute-start.19) | collective-permute-done | bytes 1048608 | tf_op jit(solution)/shard_map/ppermute | solution.py:353
  536.3 4.7 collective-permute-done.20.refs_5_.refs_21_
  543.3 63.6 %collective-permute-start.25 = (f32[32,64,128]{2,1,0:T(8,128)}, f32[32,64,128]{2,1,0:T(8,128)}, u32[]{:S(2)}, u32[]{:S(2)}) collective-permute-start(f32[32,64,128]{2,1,0:T(8,128)} %get-tuple-element.198), channel_id=1, source_target_pairs={{0,14},{1,15},{2,12},{3,13},{4,10},{5,11},{6,8},{7,9},{8,6},{9,7},... | collective-permute-start | bytes 3145736 | tf_op jit(solution)/shard_map/ppermute | solution.py:353
  606.9 21.2 %collective-permute-done.23.refs_6_.refs_22_ = f32[32,64,128]{2,1,0:T(8,128)} collective-permute-done((f32[32,64,128]{2,1,0:T(8,128)}, f32[32,64,128]{2,1,0:T(8,128)}, u32[]{:S(2)}, u32[]{:S(2)}) %collective-permute-start.23) | collective-permute-done | bytes 1048608 | tf_op jit(solution)/shard_map/ppermute | solution.py:353
  632.6 10.8 pack.14
  643.4 10.7 pack.15
  654.1 42.3 %collective-permute-start.31 = (f32[32,64,128]{2,1,0:T(8,128)}, f32[32,64,128]{2,1,0:T(8,128)S(1)}, u32[]{:S(2)}, u32[]{:S(2)}) collective-permute-start(f32[32,64,128]{2,1,0:T(8,128)} %get-tuple-element.214), channel_id=1, source_target_pairs={{0,16},{1,17},{2,18},{3,19},{4,20},{5,21},{6,22},{7,23},{8,24},{9,... | collective-permute-start | bytes 3145736 | tf_op jit(solution)/shard_map/ppermute | solution.py:353
  697.2 43.0 %collective-permute-done.27.refs_11_.refs_27_ = f32[32,64,128]{2,1,0:T(8,128)} collective-permute-done((f32[32,64,128]{2,1,0:T(8,128)}, f32[32,64,128]{2,1,0:T(8,128)}, u32[]{:S(2)}, u32[]{:S(2)}) %collective-permute-start.27) | collective-permute-done | bytes 1048608 | tf_op jit(solution)/shard_map/ppermute | solution.py:353
  743.8 43.5 %collective-permute-start.34 = (f32[32,64,128]{2,1,0:T(8,128)}, f32[32,64,128]{2,1,0:T(8,128)}, u32[]{:S(2)}, u32[]{:S(2)}) collective-permute-start(f32[32,64,128]{2,1,0:T(8,128)} %get-tuple-element.221), channel_id=1, source_target_pairs={{0,18},{1,19},{2,16},{3,17},{4,22},{5,23},{6,20},{7,21},{8,26},{9,... | collective-permute-start | bytes 3145736 | tf_op jit(solution)/shard_map/ppermute | solution.py:353
  787.3 41.7 %collective-permute-done.31.refs_8_.refs_40_ = f32[32,64,128]{2,1,0:T(8,128)S(1)} collective-permute-done((f32[32,64,128]{2,1,0:T(8,128)}, f32[32,64,128]{2,1,0:T(8,128)S(1)}, u32[]{:S(2)}, u32[]{:S(2)}) %collective-permute-start.31) | collective-permute-done | bytes 1048608 | tf_op jit(solution)/shard_map/ppermute | solution.py:353
  829.0 3.1 collective-permute-start.33
  834.0 20.5 %collective-permute-start.38 = (f32[32,64,128]{2,1,0:T(8,128)}, f32[32,64,128]{2,1,0:T(8,128)}, u32[]{:S(2)}, u32[]{:S(2)}) collective-permute-start(f32[32,64,128]{2,1,0:T(8,128)} %get-tuple-element.227), channel_id=1, source_target_pairs={{0,12},{1,13},{2,14},{3,15},{4,8},{5,9},{6,10},{7,11},{8,4},{9,5},... | collective-permute-start | bytes 3145736 | tf_op jit(solution)/shard_map/ppermute | solution.py:353
  854.6 43.7 %collective-permute-done.34.refs_9_.refs_41_ = f32[32,64,128]{2,1,0:T(8,128)} collective-permute-done((f32[32,64,128]{2,1,0:T(8,128)}, f32[32,64,128]{2,1,0:T(8,128)}, u32[]{:S(2)}, u32[]{:S(2)}) %collective-permute-start.34) | collective-permute-done | bytes 1048608 | tf_op jit(solution)/shard_map/ppermute | solution.py:353
  900.9 4.3 collective-permute-start.43
  905.2 63.5 %collective-permute-start.40 = (f32[32,64,128]{2,1,0:T(8,128)}, f32[32,64,128]{2,1,0:T(8,128)}, u32[]{:S(2)}, u32[]{:S(2)}) collective-permute-start(f32[32,64,128]{2,1,0:T(8,128)} %get-tuple-element.231), channel_id=1, source_target_pairs={{0,14},{1,15},{2,12},{3,13},{4,10},{5,11},{6,8},{7,9},{8,6},{9,7},... | collective-permute-start | bytes 3145736 | tf_op jit(solution)/shard_map/ppermute | solution.py:353
  968.7 20.5 %collective-permute-done.38.refs_6_.refs_38_ = f32[32,64,128]{2,1,0:T(8,128)} collective-permute-done((f32[32,64,128]{2,1,0:T(8,128)}, f32[32,64,128]{2,1,0:T(8,128)}, u32[]{:S(2)}, u32[]{:S(2)}) %collective-permute-start.38) | collective-permute-done | bytes 1048608 | tf_op jit(solution)/shard_map/ppermute | solution.py:353
  989.2 3.0 collective-permute-start.42
  994.7 10.8 pack.16
  1005.5 10.7 pack.17
  1016.2 40.1 %collective-permute-start.46 = (f32[32,64,128]{2,1,0:T(8,128)}, f32[32,64,128]{2,1,0:T(8,128)S(1)}, u32[]{:S(2)}, u32[]{:S(2)}) collective-permute-start(f32[32,64,128]{2,1,0:T(8,128)} %get-tuple-element.247), channel_id=1, source_target_pairs={{0,16},{1,17},{2,18},{3,19},{4,20},{5,21},{6,22},{7,23},{8,24},{9,... | collective-permute-start | bytes 3145736 | tf_op jit(solution)/shard_map/ppermute | solution.py:353
  1059.2 42.7 %collective-permute-done.42.refs_11_.refs_43_ = f32[32,64,128]{2,1,0:T(8,128)} collective-permute-done((f32[32,64,128]{2,1,0:T(8,128)}, f32[32,64,128]{2,1,0:T(8,128)}, u32[]{:S(2)}, u32[]{:S(2)}) %collective-permute-start.42) | collective-permute-done | bytes 1048608 | tf_op jit(solution)/shard_map/ppermute | solution.py:353
  1101.8 3.2 collective-permute-start.45
  1105.0 43.0 %collective-permute-start.49 = (f32[32,64,128]{2,1,0:T(8,128)}, f32[32,64,128]{2,1,0:T(8,128)}, u32[]{:S(2)}, u32[]{:S(2)}) collective-permute-start(f32[32,64,128]{2,1,0:T(8,128)} %get-tuple-element.254), channel_id=1, source_target_pairs={{0,18},{1,19},{2,16},{3,17},{4,22},{5,23},{6,20},{7,21},{8,26},{9,... | collective-permute-start | bytes 3145736 | tf_op jit(solution)/shard_map/ppermute | solution.py:353
  1148.0 42.7 %collective-permute-done.46.refs_8_.refs_56_ = f32[32,64,128]{2,1,0:T(8,128)S(1)} collective-permute-done((f32[32,64,128]{2,1,0:T(8,128)}, f32[32,64,128]{2,1,0:T(8,128)S(1)}, u32[]{:S(2)}, u32[]{:S(2)}) %collective-permute-start.46) | collective-permute-done | bytes 1048608 | tf_op jit(solution)/shard_map/ppermute | solution.py:353
  1190.7 3.3 collective-permute-start.48
  1196.0 41.8 %collective-permute-start.53 = (f32[32,64,128]{2,1,0:T(8,128)}, f32[32,64,128]{2,1,0:T(8,128)}, u32[]{:S(2)}, u32[]{:S(2)}) collective-permute-start(f32[32,64,128]{2,1,0:T(8,128)} %get-tuple-element.260), channel_id=1, source_target_pairs={{0,12},{1,13},{2,14},{3,15},{4,8},{5,9},{6,10},{7,11},{8,4},{9,5},... | collective-permute-start | bytes 3145736 | tf_op jit(solution)/shard_map/ppermute | solution.py:353
  1237.8 23.1 %collective-permute-done.49.refs_9_.refs_57_ = f32[32,64,128]{2,1,0:T(8,128)} collective-permute-done((f32[32,64,128]{2,1,0:T(8,128)}, f32[32,64,128]{2,1,0:T(8,128)}, u32[]{:S(2)}, u32[]{:S(2)}) %collective-permute-start.49) | collective-permute-done | bytes 1048608 | tf_op jit(solution)/shard_map/ppermute | solution.py:353
  1261.9 16.9 %gram_z.4.prev_ref = f32[512,512]{1,0:T(8,128)} custom-call(s32[1]{0:T(128)} %bitcast.3.me_ref, f32[512,512]{1,0:T(8,128)} %broadcast_in_dim.2.prev_ref, f32[32,64,128]{2,1,0:T(8,128)} %get-tuple-element.147.refs_0_, f32[32,64,128]{2,1,0:T(8,128)} %collective-permute-done.refs_1_, f32[32,64,128]{2,1,0:T(8,128)} %collective-permute-done.3.refs_2_, ...), custom_call_target="tpu_custom_call" | custom-call | flops 8589934592 | bytes 16777216 | tf_op jit(solution)/shard_map/gram_z/pallas_call | solution.py:122
  1282.1 47.7 %collective-permute-start.55 = (f32[32,64,128]{2,1,0:T(8,128)}, f32[32,64,128]{2,1,0:T(8,128)S(1)}, u32[]{:S(2)}, u32[]{:S(2)}) collective-permute-start(f32[32,64,128]{2,1,0:T(8,128)} %get-tuple-element.264), channel_id=1, source_target_pairs={{0,14},{1,15},{2,12},{3,13},{4,10},{5,11},{6,8},{7,9},{8,6},{9,7},... | collective-permute-start | bytes 3145736 | tf_op jit(solution)/shard_map/ppermute | solution.py:353
  1329.8 21.5 %collective-permute-done.56.refs_10_.refs_58_ = f32[32,64,128]{2,1,0:T(8,128)} collective-permute-done((f32[32,64,128]{2,1,0:T(8,128)}, f32[32,64,128]{2,1,0:T(8,128)}, u32[]{:S(2)}, u32[]{:S(2)}) %collective-permute-start.56) | collective-permute-done | bytes 1048608 | tf_op jit(solution)/shard_map/ppermute | solution.py:353
  1351.3 9.5 collective-permute-start.59
  1360.8 16.7 %gram_z.5.prev_ref = f32[512,512]{1,0:T(8,128)} custom-call(s32[1]{0:T(128)} %bitcast.3.me_ref, f32[512,512]{1,0:T(8,128)} %gram_z.4.prev_ref, f32[32,64,128]{2,1,0:T(8,128)} %get-tuple-element.173.refs_0_.refs_16_, f32[32,64,128]{2,1,0:T(8,128)} %copy-done.5, f32[32,64,128]{2,1,0:T(8,128)} %collective-permute-done.18.refs_2_.refs_18_, ...), custom_call_target="tpu_custom_call" | custom-call | flops 8589934592 | bytes 16777216 | tf_op jit(solution)/shard_map/gram_z/pallas_call | solution.py:122
  1377.5 16.7 %gram_z.6.prev_ref = f32[512,512]{1,0:T(8,128)} custom-call(s32[1]{0:T(128)} %bitcast.3.me_ref, f32[512,512]{1,0:T(8,128)} %gram_z.5.prev_ref, f32[32,64,128]{2,1,0:T(8,128)} %get-tuple-element.206.refs_0_.refs_32_, f32[32,64,128]{2,1,0:T(8,128)} %copy-done.8, f32[32,64,128]{2,1,0:T(8,128)} %collective-permute-done.33.refs_2_.refs_34_, ...), custom_call_target="tpu_custom_call" | custom-call | flops 8589934592 | bytes 16777216 | tf_op jit(solution)/shard_map/gram_z/pallas_call | solution.py:122
  1394.3 50.5 %collective-permute-done.57.refs_11_.refs_59_ = f32[32,64,128]{2,1,0:T(8,128)} collective-permute-done((f32[32,64,128]{2,1,0:T(8,128)}, f32[32,64,128]{2,1,0:T(8,128)}, u32[]{:S(2)}, u32[]{:S(2)}) %collective-permute-start.57) | collective-permute-done | bytes 1048608 | tf_op jit(solution)/shard_map/ppermute | solution.py:353
  1444.8 16.8 %gram_z.7 = f32[512,512]{1,0:T(8,128)} custom-call(s32[1]{0:T(128)} %bitcast.3.me_ref, f32[512,512]{1,0:T(8,128)} %gram_z.6.prev_ref, f32[32,64,128]{2,1,0:T(8,128)} %get-tuple-element.239.refs_0_.refs_48_, f32[32,64,128]{2,1,0:T(8,128)} %copy-done.11, f32[32,64,128]{2,1,0:T(8,128)} %collective-permute-done.48.refs_2_.refs_50_, f32[32,64,128]{2,1,0:T(8,128)} %copy-done.12, ...), custom_call_target="tpu_custom_call" | custom-call | flops 8589934592 | bytes 16777216 | tf_op jit(solution)/shard_map/gram_z/pallas_call | solution.py:122
  1475.5 22.2 %collective-permute-start.64 = (f32[16,512]{1,0:T(8,128)S(1)}, f32[16,512]{1,0:T(8,128)S(1)}, u32[]{:S(2)}, u32[]{:S(2)}) collective-permute-start(f32[16,512]{1,0:T(8,128)S(1)} %get-tuple-element.316), channel_id=1, source_target_pairs={{0,8},{1,9},{2,10},{3,11},{4,12},{5,13},{6,14},{7,15},{8,0},{9,1},... | collective-permute-start | bytes 98312 | tf_op jit(solution)/shard_map/ppermute | solution.py:353
  1497.7 3.4 collective-permute-start.66
  1506.9 3.5 collective-permute-start.67
  1524.3 14.5 leaf_basis.2
  1538.8 16.3 reduce_z.2
  1556.2 16.3 reduce_z.3
  1574.2 10.8 gram_y.1
  1603.2 3.5 collective-permute-done.84
  1626.2 14.5 leaf_basis.3
  1640.6 5.9 core.1
  (211 shorter events, 122.7 us)
Async XLA Ops:
  9.6 51.6 %collective-permute-start.1 = (f32[32,64,128]{2,1,0:T(8,128)}, f32[32,64,128]{2,1,0:T(8,128)S(1)}, u32[]{:S(2)}, u32[]{:S(2)}) collective-permute-start(f32[32,64,128]{2,1,0:T(8,128)} %get-tuple-element.143), channel_id=1, source_target_pairs={{0,16},{1,17},{2,18},{3,19},{4,20},{5,21},{6,22},{7,23},{8,24},{9,... | collective-permute-start | bytes 3145736 | tf_op jit(solution)/shard_map/ppermute | solution.py:353
  33.3 48.8 %collective-permute-start.2 = (f32[32,64,128]{2,1,0:T(8,128)}, f32[32,64,128]{2,1,0:T(8,128)S(1)}, u32[]{:S(2)}, u32[]{:S(2)}) collective-permute-start(f32[32,64,128]{2,1,0:T(8,128)} %get-tuple-element.151), channel_id=1, source_target_pairs={{0,8},{1,9},{2,10},{3,11},{4,12},{5,13},{6,14},{7,15},{8,0},{9,1},... | collective-permute-start | bytes 3145736 | tf_op jit(solution)/shard_map/ppermute | solution.py:353
  34.9 94.2 %collective-permute-start.7 = (f32[32,64,128]{2,1,0:T(8,128)}, f32[32,64,128]{2,1,0:T(8,128)S(1)}, u32[]{:S(2)}, u32[]{:S(2)}) collective-permute-start(f32[32,64,128]{2,1,0:T(8,128)} %get-tuple-element.160), channel_id=1, source_target_pairs={{0,18},{1,19},{2,16},{3,17},{4,22},{5,23},{6,20},{7,21},{8,26},{9,... | collective-permute-start | bytes 3145736 | tf_op jit(solution)/shard_map/ppermute | solution.py:353
  36.1 93.6 %collective-permute-start = (f32[32,64,128]{2,1,0:T(8,128)}, f32[32,64,128]{2,1,0:T(8,128)}, u32[]{:S(2)}, u32[]{:S(2)}) collective-permute-start(f32[32,64,128]{2,1,0:T(8,128)} %get-tuple-element.148), channel_id=1, source_target_pairs={{0,2},{1,3},{2,0},{3,1},{4,6},{5,7},{6,4},{7,5},{8,10},{9,11},{10,... | collective-permute-start | bytes 3145736 | tf_op jit(solution)/shard_map/ppermute | solution.py:353
  36.7 137.5 %collective-permute-start.4 = (f32[32,64,128]{2,1,0:T(8,128)}, f32[32,64,128]{2,1,0:T(8,128)}, u32[]{:S(2)}, u32[]{:S(2)}) collective-permute-start(f32[32,64,128]{2,1,0:T(8,128)} %get-tuple-element.155), channel_id=1, source_target_pairs={{0,20},{1,21},{2,22},{3,23},{4,16},{5,17},{6,18},{7,19},{8,28},{9,... | collective-permute-start | bytes 3145736 | tf_op jit(solution)/shard_map/ppermute | solution.py:353
  61.2 115.4 %collective-permute-start.5 = (f32[32,64,128]{2,1,0:T(8,128)}, f32[32,64,128]{2,1,0:T(8,128)}, u32[]{:S(2)}, u32[]{:S(2)}) collective-permute-start(f32[32,64,128]{2,1,0:T(8,128)} %get-tuple-element.156), channel_id=1, source_target_pairs={{0,10},{1,11},{2,8},{3,9},{4,14},{5,15},{6,12},{7,13},{8,2},{9,3},... | collective-permute-start | bytes 3145736 | tf_op jit(solution)/shard_map/ppermute | solution.py:353
  82.1 96.0 %collective-permute-start.3 = (f32[32,64,128]{2,1,0:T(8,128)}, f32[32,64,128]{2,1,0:T(8,128)}, u32[]{:S(2)}, u32[]{:S(2)}) collective-permute-start(f32[32,64,128]{2,1,0:T(8,128)} %get-tuple-element.152), channel_id=1, source_target_pairs={{0,4},{1,5},{2,6},{3,7},{4,0},{5,1},{6,2},{7,3},{8,12},{9,13},{10,... | collective-permute-start | bytes 3145736 | tf_op jit(solution)/shard_map/ppermute | solution.py:353
  129.1 113.5 %collective-permute-start.9 = (f32[32,64,128]{2,1,0:T(8,128)}, f32[32,64,128]{2,1,0:T(8,128)}, u32[]{:S(2)}, u32[]{:S(2)}) collective-permute-start(f32[32,64,128]{2,1,0:T(8,128)} %get-tuple-element.164), channel_id=1, source_target_pairs={{0,22},{1,23},{2,20},{3,21},{4,18},{5,19},{6,16},{7,17},{8,30},{9,... | collective-permute-start | bytes 3145736 | tf_op jit(solution)/shard_map/ppermute | solution.py:353
  129.7 112.9 %collective-permute-start.8 = (f32[32,64,128]{2,1,0:T(8,128)}, f32[32,64,128]{2,1,0:T(8,128)}, u32[]{:S(2)}, u32[]{:S(2)}) collective-permute-start(f32[32,64,128]{2,1,0:T(8,128)} %get-tuple-element.161), channel_id=1, source_target_pairs={{0,12},{1,13},{2,14},{3,15},{4,8},{5,9},{6,10},{7,11},{8,4},{9,5},... | collective-permute-start | bytes 3145736 | tf_op jit(solution)/shard_map/ppermute | solution.py:353
  174.2 73.8 %collective-permute-start.11 = (f32[32,64,128]{2,1,0:T(8,128)}, f32[32,64,128]{2,1,0:T(8,128)}, u32[]{:S(2)}, u32[]{:S(2)}) collective-permute-start(f32[32,64,128]{2,1,0:T(8,128)} %get-tuple-element.166), channel_id=1, source_target_pairs={{0,24},{1,25},{2,26},{3,27},{4,28},{5,29},{6,30},{7,31},{8,16},{9,... | collective-permute-start | bytes 3145736 | tf_op jit(solution)/shard_map/ppermute | solution.py:353
  176.6 92.8 %collective-permute-start.6 = (f32[32,64,128]{2,1,0:T(8,128)}, f32[32,64,128]{2,1,0:T(8,128)}, u32[]{:S(2)}, u32[]{:S(2)}) collective-permute-start(f32[32,64,128]{2,1,0:T(8,128)} %get-tuple-element.157), channel_id=1, source_target_pairs={{0,6},{1,7},{2,4},{3,5},{4,2},{5,3},{6,0},{7,1},{8,14},{9,15},{10,... | collective-permute-start | bytes 3145736 | tf_op jit(solution)/shard_map/ppermute | solution.py:353
  178.1 91.3 %collective-permute-start.12 = (f32[32,64,128]{2,1,0:T(8,128)}, f32[32,64,128]{2,1,0:T(8,128)}, u32[]{:S(2)}, u32[]{:S(2)}) collective-permute-start(f32[32,64,128]{2,1,0:T(8,128)} %get-tuple-element.167), channel_id=1, source_target_pairs={{0,26},{1,27},{2,24},{3,25},{4,30},{5,31},{6,28},{7,29},{8,18},{9,... | collective-permute-start | bytes 3145736 | tf_op jit(solution)/shard_map/ppermute | solution.py:353
  242.6 92.1 %collective-permute-start.10 = (f32[32,64,128]{2,1,0:T(8,128)}, f32[32,64,128]{2,1,0:T(8,128)}, u32[]{:S(2)}, u32[]{:S(2)}) collective-permute-start(f32[32,64,128]{2,1,0:T(8,128)} %get-tuple-element.165), channel_id=1, source_target_pairs={{0,14},{1,15},{2,12},{3,13},{4,10},{5,11},{6,8},{7,9},{8,6},{9,7},... | collective-permute-start | bytes 3145736 | tf_op jit(solution)/shard_map/ppermute | solution.py:353
  242.6 92.1 %collective-permute-start.13 = (f32[32,64,128]{2,1,0:T(8,128)}, f32[32,64,128]{2,1,0:T(8,128)}, u32[]{:S(2)}, u32[]{:S(2)}) collective-permute-start(f32[32,64,128]{2,1,0:T(8,128)} %get-tuple-element.168), channel_id=1, source_target_pairs={{0,28},{1,29},{2,30},{3,31},{4,24},{5,25},{6,26},{7,27},{8,20},{9,... | collective-permute-start | bytes 3145736 | tf_op jit(solution)/shard_map/ppermute | solution.py:353
  247.9 90.6 %collective-permute-start.14 = (f32[32,64,128]{2,1,0:T(8,128)}, f32[32,64,128]{2,1,0:T(8,128)}, u32[]{:S(2)}, u32[]{:S(2)}) collective-permute-start(f32[32,64,128]{2,1,0:T(8,128)} %get-tuple-element.169), channel_id=1, source_target_pairs={{0,30},{1,31},{2,28},{3,29},{4,26},{5,27},{6,24},{7,25},{8,22},{9,... | collective-permute-start | bytes 3145736 | tf_op jit(solution)/shard_map/ppermute | solution.py:353
  269.4 199.5 %collective-permute-start.16 = (f32[32,64,128]{2,1,0:T(8,128)}, f32[32,64,128]{2,1,0:T(8,128)S(1)}, u32[]{:S(2)}, u32[]{:S(2)}) collective-permute-start(f32[32,64,128]{2,1,0:T(8,128)} %get-tuple-element.181), channel_id=1, source_target_pairs={{0,16},{1,17},{2,18},{3,19},{4,20},{5,21},{6,22},{7,23},{8,24},{9,... | collective-permute-start | bytes 3145736 | tf_op jit(solution)/shard_map/ppermute | solution.py:353
  334.0 134.8 %collective-permute-start.17 = (f32[32,64,128]{2,1,0:T(8,128)}, f32[32,64,128]{2,1,0:T(8,128)S(1)}, u32[]{:S(2)}, u32[]{:S(2)}) collective-permute-start(f32[32,64,128]{2,1,0:T(8,128)} %get-tuple-element.182), channel_id=1, source_target_pairs={{0,8},{1,9},{2,10},{3,11},{4,12},{5,13},{6,14},{7,15},{8,0},{9,1},... | collective-permute-start | bytes 3145736 | tf_op jit(solution)/shard_map/ppermute | solution.py:353
  334.6 134.9 %collective-permute-start.15 = (f32[32,64,128]{2,1,0:T(8,128)}, f32[32,64,128]{2,1,0:T(8,128)S(1)}, u32[]{:S(2)}, u32[]{:S(2)}) collective-permute-start(f32[32,64,128]{2,1,0:T(8,128)} %get-tuple-element.176), channel_id=1, source_target_pairs={{0,2},{1,3},{2,0},{3,1},{4,6},{5,7},{6,4},{7,5},{8,10},{9,11},{10,... | collective-permute-start | bytes 3145736 | tf_op jit(solution)/shard_map/ppermute | solution.py:353
  336.1 135.4 %collective-permute-start.22 = (f32[32,64,128]{2,1,0:T(8,128)}, f32[32,64,128]{2,1,0:T(8,128)}, u32[]{:S(2)}, u32[]{:S(2)}) collective-permute-start(f32[32,64,128]{2,1,0:T(8,128)} %get-tuple-element.193), channel_id=1, source_target_pairs={{0,24},{1,25},{2,26},{3,27},{4,28},{5,29},{6,30},{7,31},{8,16},{9,... | collective-permute-start | bytes 3145736 | tf_op jit(solution)/shard_map/ppermute | solution.py:353
  338.5 197.8 %collective-permute-start.19 = (f32[32,64,128]{2,1,0:T(8,128)}, f32[32,64,128]{2,1,0:T(8,128)}, u32[]{:S(2)}, u32[]{:S(2)}) collective-permute-start(f32[32,64,128]{2,1,0:T(8,128)} %get-tuple-element.188), channel_id=1, source_target_pairs={{0,18},{1,19},{2,16},{3,17},{4,22},{5,23},{6,20},{7,21},{8,26},{9,... | collective-permute-start | bytes 3145736 | tf_op jit(solution)/shard_map/ppermute | solution.py:353
  468.8 72.3 %collective-permute-start.20 = (f32[32,64,128]{2,1,0:T(8,128)}, f32[32,64,128]{2,1,0:T(8,128)}, u32[]{:S(2)}, u32[]{:S(2)}) collective-permute-start(f32[32,64,128]{2,1,0:T(8,128)} %get-tuple-element.189), channel_id=1, source_target_pairs={{0,10},{1,11},{2,8},{3,9},{4,14},{5,15},{6,12},{7,13},{8,2},{9,3},... | collective-permute-start | bytes 3145736 | tf_op jit(solution)/shard_map/ppermute | solution.py:353
  468.9 72.2 %collective-permute-start.18 = (f32[32,64,128]{2,1,0:T(8,128)}, f32[32,64,128]{2,1,0:T(8,128)}, u32[]{:S(2)}, u32[]{:S(2)}) collective-permute-start(f32[32,64,128]{2,1,0:T(8,128)} %get-tuple-element.183), channel_id=1, source_target_pairs={{0,4},{1,5},{2,6},{3,7},{4,0},{5,1},{6,2},{7,3},{8,12},{9,13},{10,... | collective-permute-start | bytes 3145736 | tf_op jit(solution)/shard_map/ppermute | solution.py:353
  469.6 73.8 %collective-permute-start.24 = (f32[32,64,128]{2,1,0:T(8,128)}, f32[32,64,128]{2,1,0:T(8,128)}, u32[]{:S(2)}, u32[]{:S(2)}) collective-permute-start(f32[32,64,128]{2,1,0:T(8,128)} %get-tuple-element.197), channel_id=1, source_target_pairs={{0,26},{1,27},{2,24},{3,25},{4,30},{5,31},{6,28},{7,29},{8,18},{9,... | collective-permute-start | bytes 3145736 | tf_op jit(solution)/shard_map/ppermute | solution.py:353
  471.5 156.6 %collective-permute-start.23 = (f32[32,64,128]{2,1,0:T(8,128)}, f32[32,64,128]{2,1,0:T(8,128)}, u32[]{:S(2)}, u32[]{:S(2)}) collective-permute-start(f32[32,64,128]{2,1,0:T(8,128)} %get-tuple-element.194), channel_id=1, source_target_pairs={{0,12},{1,13},{2,14},{3,15},{4,8},{5,9},{6,10},{7,11},{8,4},{9,5},... | collective-permute-start | bytes 3145736 | tf_op jit(solution)/shard_map/ppermute | solution.py:353
  536.3 93.4 %collective-permute-start.26 = (f32[32,64,128]{2,1,0:T(8,128)}, f32[32,64,128]{2,1,0:T(8,128)}, u32[]{:S(2)}, u32[]{:S(2)}) collective-permute-start(f32[32,64,128]{2,1,0:T(8,128)} %get-tuple-element.199), channel_id=1, source_target_pairs={{0,20},{1,21},{2,22},{3,23},{4,16},{5,17},{6,18},{7,19},{8,28},{9,... | collective-permute-start | bytes 3145736 | tf_op jit(solution)/shard_map/ppermute | solution.py:353
  541.1 113.0 %collective-permute-start.21 = (f32[32,64,128]{2,1,0:T(8,128)}, f32[32,64,128]{2,1,0:T(8,128)}, u32[]{:S(2)}, u32[]{:S(2)}) collective-permute-start(f32[32,64,128]{2,1,0:T(8,128)} %get-tuple-element.190), channel_id=1, source_target_pairs={{0,6},{1,7},{2,4},{3,5},{4,2},{5,3},{6,0},{7,1},{8,14},{9,15},{10,... | collective-permute-start | bytes 3145736 | tf_op jit(solution)/shard_map/ppermute | solution.py:353
  541.1 113.0 %collective-permute-start.28 = (f32[32,64,128]{2,1,0:T(8,128)}, f32[32,64,128]{2,1,0:T(8,128)}, u32[]{:S(2)}, u32[]{:S(2)}) collective-permute-start(f32[32,64,128]{2,1,0:T(8,128)} %get-tuple-element.201), channel_id=1, source_target_pairs={{0,28},{1,29},{2,30},{3,31},{4,24},{5,25},{6,26},{7,27},{8,20},{9,... | collective-permute-start | bytes 3145736 | tf_op jit(solution)/shard_map/ppermute | solution.py:353
  543.3 153.9 %collective-permute-start.25 = (f32[32,64,128]{2,1,0:T(8,128)}, f32[32,64,128]{2,1,0:T(8,128)}, u32[]{:S(2)}, u32[]{:S(2)}) collective-permute-start(f32[32,64,128]{2,1,0:T(8,128)} %get-tuple-element.198), channel_id=1, source_target_pairs={{0,14},{1,15},{2,12},{3,13},{4,10},{5,11},{6,8},{7,9},{8,6},{9,7},... | collective-permute-start | bytes 3145736 | tf_op jit(solution)/shard_map/ppermute | solution.py:353
  628.2 112.0 %collective-permute-start.27 = (f32[32,64,128]{2,1,0:T(8,128)}, f32[32,64,128]{2,1,0:T(8,128)}, u32[]{:S(2)}, u32[]{:S(2)}) collective-permute-start(f32[32,64,128]{2,1,0:T(8,128)} %get-tuple-element.200), channel_id=1, source_target_pairs={{0,22},{1,23},{2,20},{3,21},{4,18},{5,19},{6,16},{7,17},{8,30},{9,... | collective-permute-start | bytes 3145736 | tf_op jit(solution)/shard_map/ppermute | solution.py:353
  629.7 114.0 %collective-permute-start.29 = (f32[32,64,128]{2,1,0:T(8,128)}, f32[32,64,128]{2,1,0:T(8,128)}, u32[]{:S(2)}, u32[]{:S(2)}) collective-permute-start(f32[32,64,128]{2,1,0:T(8,128)} %get-tuple-element.202), channel_id=1, source_target_pairs={{0,30},{1,31},{2,28},{3,29},{4,26},{5,27},{6,24},{7,25},{8,22},{9,... | collective-permute-start | bytes 3145736 | tf_op jit(solution)/shard_map/ppermute | solution.py:353
  654.1 174.9 %collective-permute-start.31 = (f32[32,64,128]{2,1,0:T(8,128)}, f32[32,64,128]{2,1,0:T(8,128)S(1)}, u32[]{:S(2)}, u32[]{:S(2)}) collective-permute-start(f32[32,64,128]{2,1,0:T(8,128)} %get-tuple-element.214), channel_id=1, source_target_pairs={{0,16},{1,17},{2,18},{3,19},{4,20},{5,21},{6,22},{7,23},{8,24},{9,... | collective-permute-start | bytes 3145736 | tf_op jit(solution)/shard_map/ppermute | solution.py:353
  696.4 132.6 %collective-permute-start.32 = (f32[32,64,128]{2,1,0:T(8,128)}, f32[32,64,128]{2,1,0:T(8,128)S(1)}, u32[]{:S(2)}, u32[]{:S(2)}) collective-permute-start(f32[32,64,128]{2,1,0:T(8,128)} %get-tuple-element.215), channel_id=1, source_target_pairs={{0,8},{1,9},{2,10},{3,11},{4,12},{5,13},{6,14},{7,15},{8,0},{9,1},... | collective-permute-start | bytes 3145736 | tf_op jit(solution)/shard_map/ppermute | solution.py:353
  740.2 91.9 %collective-permute-start.30 = (f32[32,64,128]{2,1,0:T(8,128)}, f32[32,64,128]{2,1,0:T(8,128)S(1)}, u32[]{:S(2)}, u32[]{:S(2)}) collective-permute-start(f32[32,64,128]{2,1,0:T(8,128)} %get-tuple-element.209), channel_id=1, source_target_pairs={{0,2},{1,3},{2,0},{3,1},{4,6},{5,7},{6,4},{7,5},{8,10},{9,11},{10,... | collective-permute-start | bytes 3145736 | tf_op jit(solution)/shard_map/ppermute | solution.py:353
  743.1 91.0 %collective-permute-start.37 = (f32[32,64,128]{2,1,0:T(8,128)}, f32[32,64,128]{2,1,0:T(8,128)}, u32[]{:S(2)}, u32[]{:S(2)}) collective-permute-start(f32[32,64,128]{2,1,0:T(8,128)} %get-tuple-element.226), channel_id=1, source_target_pairs={{0,24},{1,25},{2,26},{3,27},{4,28},{5,29},{6,30},{7,31},{8,16},{9,... | collective-permute-start | bytes 3145736 | tf_op jit(solution)/shard_map/ppermute | solution.py:353
  743.8 154.5 %collective-permute-start.34 = (f32[32,64,128]{2,1,0:T(8,128)}, f32[32,64,128]{2,1,0:T(8,128)}, u32[]{:S(2)}, u32[]{:S(2)}) collective-permute-start(f32[32,64,128]{2,1,0:T(8,128)} %get-tuple-element.221), channel_id=1, source_target_pairs={{0,18},{1,19},{2,16},{3,17},{4,22},{5,23},{6,20},{7,21},{8,26},{9,... | collective-permute-start | bytes 3145736 | tf_op jit(solution)/shard_map/ppermute | solution.py:353
  829.0 71.4 %collective-permute-start.35 = (f32[32,64,128]{2,1,0:T(8,128)}, f32[32,64,128]{2,1,0:T(8,128)}, u32[]{:S(2)}, u32[]{:S(2)}) collective-permute-start(f32[32,64,128]{2,1,0:T(8,128)} %get-tuple-element.222), channel_id=1, source_target_pairs={{0,10},{1,11},{2,8},{3,9},{4,14},{5,15},{6,12},{7,13},{8,2},{9,3},... | collective-permute-start | bytes 3145736 | tf_op jit(solution)/shard_map/ppermute | solution.py:353
  829.0 71.9 %collective-permute-start.33 = (f32[32,64,128]{2,1,0:T(8,128)}, f32[32,64,128]{2,1,0:T(8,128)}, u32[]{:S(2)}, u32[]{:S(2)}) collective-permute-start(f32[32,64,128]{2,1,0:T(8,128)} %get-tuple-element.216), channel_id=1, source_target_pairs={{0,4},{1,5},{2,6},{3,7},{4,0},{5,1},{6,2},{7,3},{8,12},{9,13},{10,... | collective-permute-start | bytes 3145736 | tf_op jit(solution)/shard_map/ppermute | solution.py:353
  832.1 73.1 %collective-permute-start.39 = (f32[32,64,128]{2,1,0:T(8,128)}, f32[32,64,128]{2,1,0:T(8,128)}, u32[]{:S(2)}, u32[]{:S(2)}) collective-permute-start(f32[32,64,128]{2,1,0:T(8,128)} %get-tuple-element.230), channel_id=1, source_target_pairs={{0,26},{1,27},{2,24},{3,25},{4,30},{5,31},{6,28},{7,29},{8,18},{9,... | collective-permute-start | bytes 3145736 | tf_op jit(solution)/shard_map/ppermute | solution.py:353
  834.0 155.2 %collective-permute-start.38 = (f32[32,64,128]{2,1,0:T(8,128)}, f32[32,64,128]{2,1,0:T(8,128)}, u32[]{:S(2)}, u32[]{:S(2)}) collective-permute-start(f32[32,64,128]{2,1,0:T(8,128)} %get-tuple-element.227), channel_id=1, source_target_pairs={{0,12},{1,13},{2,14},{3,15},{4,8},{5,9},{6,10},{7,11},{8,4},{9,5},... | collective-permute-start | bytes 3145736 | tf_op jit(solution)/shard_map/ppermute | solution.py:353
  898.3 94.0 %collective-permute-start.41 = (f32[32,64,128]{2,1,0:T(8,128)}, f32[32,64,128]{2,1,0:T(8,128)}, u32[]{:S(2)}, u32[]{:S(2)}) collective-permute-start(f32[32,64,128]{2,1,0:T(8,128)} %get-tuple-element.232), channel_id=1, source_target_pairs={{0,20},{1,21},{2,22},{3,23},{4,16},{5,17},{6,18},{7,19},{8,28},{9,... | collective-permute-start | bytes 3145736 | tf_op jit(solution)/shard_map/ppermute | solution.py:353
  900.4 115.8 %collective-permute-start.36 = (f32[32,64,128]{2,1,0:T(8,128)}, f32[32,64,128]{2,1,0:T(8,128)}, u32[]{:S(2)}, u32[]{:S(2)}) collective-permute-start(f32[32,64,128]{2,1,0:T(8,128)} %get-tuple-element.223), channel_id=1, source_target_pairs={{0,6},{1,7},{2,4},{3,5},{4,2},{5,3},{6,0},{7,1},{8,14},{9,15},{10,... | collective-permute-start | bytes 3145736 | tf_op jit(solution)/shard_map/ppermute | solution.py:353
  900.9 115.3 %collective-permute-start.43 = (f32[32,64,128]{2,1,0:T(8,128)}, f32[32,64,128]{2,1,0:T(8,128)}, u32[]{:S(2)}, u32[]{:S(2)}) collective-permute-start(f32[32,64,128]{2,1,0:T(8,128)} %get-tuple-element.234), channel_id=1, source_target_pairs={{0,28},{1,29},{2,30},{3,31},{4,24},{5,25},{6,26},{7,27},{8,20},{9,... | collective-permute-start | bytes 3145736 | tf_op jit(solution)/shard_map/ppermute | solution.py:353
  905.2 153.9 %collective-permute-start.40 = (f32[32,64,128]{2,1,0:T(8,128)}, f32[32,64,128]{2,1,0:T(8,128)}, u32[]{:S(2)}, u32[]{:S(2)}) collective-permute-start(f32[32,64,128]{2,1,0:T(8,128)} %get-tuple-element.231), channel_id=1, source_target_pairs={{0,14},{1,15},{2,12},{3,13},{4,10},{5,11},{6,8},{7,9},{8,6},{9,7},... | collective-permute-start | bytes 3145736 | tf_op jit(solution)/shard_map/ppermute | solution.py:353
  989.2 112.6 %collective-permute-start.42 = (f32[32,64,128]{2,1,0:T(8,128)}, f32[32,64,128]{2,1,0:T(8,128)}, u32[]{:S(2)}, u32[]{:S(2)}) collective-permute-start(f32[32,64,128]{2,1,0:T(8,128)} %get-tuple-element.233), channel_id=1, source_target_pairs={{0,22},{1,23},{2,20},{3,21},{4,18},{5,19},{6,16},{7,17},{8,30},{9,... | collective-permute-start | bytes 3145736 | tf_op jit(solution)/shard_map/ppermute | solution.py:353
  992.2 112.8 %collective-permute-start.44 = (f32[32,64,128]{2,1,0:T(8,128)}, f32[32,64,128]{2,1,0:T(8,128)}, u32[]{:S(2)}, u32[]{:S(2)}) collective-permute-start(f32[32,64,128]{2,1,0:T(8,128)} %get-tuple-element.235), channel_id=1, source_target_pairs={{0,30},{1,31},{2,28},{3,29},{4,26},{5,27},{6,24},{7,25},{8,22},{9,... | collective-permute-start | bytes 3145736 | tf_op jit(solution)/shard_map/ppermute | solution.py:353
  1016.2 174.5 %collective-permute-start.46 = (f32[32,64,128]{2,1,0:T(8,128)}, f32[32,64,128]{2,1,0:T(8,128)S(1)}, u32[]{:S(2)}, u32[]{:S(2)}) collective-permute-start(f32[32,64,128]{2,1,0:T(8,128)} %get-tuple-element.247), channel_id=1, source_target_pairs={{0,16},{1,17},{2,18},{3,19},{4,20},{5,21},{6,22},{7,23},{8,24},{9,... | collective-permute-start | bytes 3145736 | tf_op jit(solution)/shard_map/ppermute | solution.py:353
  1056.3 134.4 %collective-permute-start.47 = (f32[32,64,128]{2,1,0:T(8,128)}, f32[32,64,128]{2,1,0:T(8,128)S(1)}, u32[]{:S(2)}, u32[]{:S(2)}) collective-permute-start(f32[32,64,128]{2,1,0:T(8,128)} %get-tuple-element.248), channel_id=1, source_target_pairs={{0,8},{1,9},{2,10},{3,11},{4,12},{5,13},{6,14},{7,15},{8,0},{9,1},... | collective-permute-start | bytes 3145736 | tf_op jit(solution)/shard_map/ppermute | solution.py:353
  1101.8 92.2 %collective-permute-start.45 = (f32[32,64,128]{2,1,0:T(8,128)}, f32[32,64,128]{2,1,0:T(8,128)S(1)}, u32[]{:S(2)}, u32[]{:S(2)}) collective-permute-start(f32[32,64,128]{2,1,0:T(8,128)} %get-tuple-element.242), channel_id=1, source_target_pairs={{0,2},{1,3},{2,0},{3,1},{4,6},{5,7},{6,4},{7,5},{8,10},{9,11},{10,... | collective-permute-start | bytes 3145736 | tf_op jit(solution)/shard_map/ppermute | solution.py:353
  1105.0 91.0 %collective-permute-start.52 = (f32[32,64,128]{2,1,0:T(8,128)}, f32[32,64,128]{2,1,0:T(8,128)}, u32[]{:S(2)}, u32[]{:S(2)}) collective-permute-start(f32[32,64,128]{2,1,0:T(8,128)} %get-tuple-element.259), channel_id=1, source_target_pairs={{0,24},{1,25},{2,26},{3,27},{4,28},{5,29},{6,30},{7,31},{8,16},{9,... | collective-permute-start | bytes 3145736 | tf_op jit(solution)/shard_map/ppermute | solution.py:353
  1105.0 155.8 %collective-permute-start.49 = (f32[32,64,128]{2,1,0:T(8,128)}, f32[32,64,128]{2,1,0:T(8,128)}, u32[]{:S(2)}, u32[]{:S(2)}) collective-permute-start(f32[32,64,128]{2,1,0:T(8,128)} %get-tuple-element.254), channel_id=1, source_target_pairs={{0,18},{1,19},{2,16},{3,17},{4,22},{5,23},{6,20},{7,21},{8,26},{9,... | collective-permute-start | bytes 3145736 | tf_op jit(solution)/shard_map/ppermute | solution.py:353
  1190.7 88.2 %collective-permute-start.50 = (f32[32,64,128]{2,1,0:T(8,128)}, f32[32,64,128]{2,1,0:T(8,128)}, u32[]{:S(2)}, u32[]{:S(2)}) collective-permute-start(f32[32,64,128]{2,1,0:T(8,128)} %get-tuple-element.255), channel_id=1, source_target_pairs={{0,10},{1,11},{2,8},{3,9},{4,14},{5,15},{6,12},{7,13},{8,2},{9,3},... | collective-permute-start | bytes 3145736 | tf_op jit(solution)/shard_map/ppermute | solution.py:353
  1190.7 89.8 %collective-permute-start.48 = (f32[32,64,128]{2,1,0:T(8,128)}, f32[32,64,128]{2,1,0:T(8,128)}, u32[]{:S(2)}, u32[]{:S(2)}) collective-permute-start(f32[32,64,128]{2,1,0:T(8,128)} %get-tuple-element.249), channel_id=1, source_target_pairs={{0,4},{1,5},{2,6},{3,7},{4,0},{5,1},{6,2},{7,3},{8,12},{9,13},{10,... | collective-permute-start | bytes 3145736 | tf_op jit(solution)/shard_map/ppermute | solution.py:353
  1194.1 88.1 %collective-permute-start.54 = (f32[32,64,128]{2,1,0:T(8,128)}, f32[32,64,128]{2,1,0:T(8,128)}, u32[]{:S(2)}, u32[]{:S(2)}) collective-permute-start(f32[32,64,128]{2,1,0:T(8,128)} %get-tuple-element.263), channel_id=1, source_target_pairs={{0,26},{1,27},{2,24},{3,25},{4,30},{5,31},{6,28},{7,29},{8,18},{9,... | collective-permute-start | bytes 3145736 | tf_op jit(solution)/shard_map/ppermute | solution.py:353
  1196.0 133.8 %collective-permute-start.53 = (f32[32,64,128]{2,1,0:T(8,128)}, f32[32,64,128]{2,1,0:T(8,128)}, u32[]{:S(2)}, u32[]{:S(2)}) collective-permute-start(f32[32,64,128]{2,1,0:T(8,128)} %get-tuple-element.260), channel_id=1, source_target_pairs={{0,12},{1,13},{2,14},{3,15},{4,8},{5,9},{6,10},{7,11},{8,4},{9,5},... | collective-permute-start | bytes 3145736 | tf_op jit(solution)/shard_map/ppermute | solution.py:353
  1260.8 90.5 %collective-permute-start.56 = (f32[32,64,128]{2,1,0:T(8,128)}, f32[32,64,128]{2,1,0:T(8,128)}, u32[]{:S(2)}, u32[]{:S(2)}) collective-permute-start(f32[32,64,128]{2,1,0:T(8,128)} %get-tuple-element.265), channel_id=1, source_target_pairs={{0,20},{1,21},{2,22},{3,23},{4,16},{5,17},{6,18},{7,19},{8,28},{9,... | collective-permute-start | bytes 3145736 | tf_op jit(solution)/shard_map/ppermute | solution.py:353
  1278.9 115.3 %collective-permute-start.51 = (f32[32,64,128]{2,1,0:T(8,128)}, f32[32,64,128]{2,1,0:T(8,128)S(1)}, u32[]{:S(2)}, u32[]{:S(2)}) collective-permute-start(f32[32,64,128]{2,1,0:T(8,128)} %get-tuple-element.256), channel_id=1, source_target_pairs={{0,6},{1,7},{2,4},{3,5},{4,2},{5,3},{6,0},{7,1},{8,14},{9,15},{10,... | collective-permute-start | bytes 3145736 | tf_op jit(solution)/shard_map/ppermute | solution.py:353
  1280.5 113.7 %collective-permute-start.58 = (f32[32,64,128]{2,1,0:T(8,128)}, f32[32,64,128]{2,1,0:T(8,128)S(1)}, u32[]{:S(2)}, u32[]{:S(2)}) collective-permute-start(f32[32,64,128]{2,1,0:T(8,128)} %get-tuple-element.267), channel_id=1, source_target_pairs={{0,28},{1,29},{2,30},{3,31},{4,24},{5,25},{6,26},{7,27},{8,20},{9,... | collective-permute-start | bytes 3145736 | tf_op jit(solution)/shard_map/ppermute | solution.py:353
  1282.1 112.1 %collective-permute-start.55 = (f32[32,64,128]{2,1,0:T(8,128)}, f32[32,64,128]{2,1,0:T(8,128)S(1)}, u32[]{:S(2)}, u32[]{:S(2)}) collective-permute-start(f32[32,64,128]{2,1,0:T(8,128)} %get-tuple-element.264), channel_id=1, source_target_pairs={{0,14},{1,15},{2,12},{3,13},{4,10},{5,11},{6,8},{7,9},{8,6},{9,7},... | collective-permute-start | bytes 3145736 | tf_op jit(solution)/shard_map/ppermute | solution.py:353
  1329.8 115.0 %collective-permute-start.57 = (f32[32,64,128]{2,1,0:T(8,128)}, f32[32,64,128]{2,1,0:T(8,128)}, u32[]{:S(2)}, u32[]{:S(2)}) collective-permute-start(f32[32,64,128]{2,1,0:T(8,128)} %get-tuple-element.266), channel_id=1, source_target_pairs={{0,22},{1,23},{2,20},{3,21},{4,18},{5,19},{6,16},{7,17},{8,30},{9,... | collective-permute-start | bytes 3145736 | tf_op jit(solution)/shard_map/ppermute | solution.py:353
  1351.3 93.5 %collective-permute-start.59 = (f32[32,64,128]{2,1,0:T(8,128)}, f32[32,64,128]{2,1,0:T(8,128)}, u32[]{:S(2)}, u32[]{:S(2)}) collective-permute-start(f32[32,64,128]{2,1,0:T(8,128)} %get-tuple-element.268), channel_id=1, source_target_pairs={{0,30},{1,31},{2,28},{3,29},{4,26},{5,27},{6,24},{7,25},{8,22},{9,... | collective-permute-start | bytes 3145736 | tf_op jit(solution)/shard_map/ppermute | solution.py:353
  1475.5 25.6 %collective-permute-start.64 = (f32[16,512]{1,0:T(8,128)S(1)}, f32[16,512]{1,0:T(8,128)S(1)}, u32[]{:S(2)}, u32[]{:S(2)}) collective-permute-start(f32[16,512]{1,0:T(8,128)S(1)} %get-tuple-element.316), channel_id=1, source_target_pairs={{0,8},{1,9},{2,10},{3,11},{4,12},{5,13},{6,14},{7,15},{8,0},{9,1},... | collective-permute-start | bytes 98312 | tf_op jit(solution)/shard_map/ppermute | solution.py:353
  1555.1 17.4 %collective-permute-start.75 = (f32[16,64,256]{2,1,0:T(8,128)}, f32[16,64,256]{2,1,0:T(8,128)S(1)}, u32[]{:S(2)}, u32[]{:S(2)}) collective-permute-start(f32[16,64,256]{2,1,0:T(8,128)} %get-tuple-element.276), channel_id=1, source_target_pairs={{0,1},{1,0},{2,3},{3,2},{4,5},{5,4},{6,7},{7,6},{8,9},{9,8},{10,11... | collective-permute-start | bytes 3145736 | tf_op jit(solution)/shard_map/ppermute | solution.py:353
  1555.6 16.9 %collective-permute-start.76 = (f32[16,64,256]{2,1,0:T(8,128)}, f32[16,64,256]{2,1,0:T(8,128)S(1)}, u32[]{:S(2)}, u32[]{:S(2)}) collective-permute-start(f32[16,64,256]{2,1,0:T(8,128)} %get-tuple-element.277), channel_id=1, source_target_pairs={{0,1},{1,0},{2,3},{3,2},{4,5},{5,4},{6,7},{7,6},{8,9},{9,8},{10,11... | collective-permute-start | bytes 3145736 | tf_op jit(solution)/shard_map/ppermute | solution.py:353
  1555.7 16.8 %collective-permute-start.77 = (f32[16,64,256]{2,1,0:T(8,128)}, f32[16,64,256]{2,1,0:T(8,128)S(1)}, u32[]{:S(2)}, u32[]{:S(2)}) collective-permute-start(f32[16,64,256]{2,1,0:T(8,128)} %get-tuple-element.278), channel_id=1, source_target_pairs={{0,1},{1,0},{2,3},{3,2},{4,5},{5,4},{6,7},{7,6},{8,9},{9,8},{10,11... | collective-permute-start | bytes 3145736 | tf_op jit(solution)/shard_map/ppermute | solution.py:353
  (46 other events, 2128.3 us)

commit v5 on v4

--- a/solution.py
+++ b/solution.py
@@ -86,7 +86,7 @@
 
 
 def gram_z_kernel(groups, side, me_ref, prev_ref, *refs):
-    pieces, out_ref, (high, low, sum_hh, sum_hl) = refs[:groups], refs[groups], refs[groups + 1:]
+    pieces, out_refs, (high, low, sum_hh, sum_hl) = refs[:groups], refs[groups:-4], refs[-4:]
     step = pl.program_id(0)
     me_z = me_ref[0] // side
     x_tile, z_n, y_n = pieces[0].shape
@@ -109,10 +109,18 @@
     @pl.when(step == pl.num_programs(0) - 1)
     def _():
         cross = sum_hl[...]
-        out_ref[...] = prev_ref[...] + (sum_hh[...] + (cross + cross.T))
-
-
-def gram_z_step(prev, pieces, me, side):
+        sum_hh[...] = prev_ref[...] + (sum_hh[...] + (cross + cross.T))
+        store_halves(out_refs, sum_hh, me_ref[1])
+
+
+def store_halves(out_refs, full, core):
+    rows = out_refs[0].shape[0]
+    for i, ref in enumerate(out_refs):
+        place = 0 if len(out_refs) == 1 else (core if i == 0 else 1 - core)
+        ref[...] = full[pl.ds(pl.multiple_of(place * rows, rows), rows), :]
+
+
+def gram_z_step(prev, pieces, me, side, halves):
     groups = len(pieces)
     width, z_n, y_n = pieces[0].shape
     order = z_n * (groups // side)
@@ -125,11 +133,11 @@
             num_scalar_prefetch=1,
             grid=(width // x_tile,),
             in_specs=[whole] + [pl.BlockSpec((x_tile, z_n, y_n), lambda i, m: (i, 0, 0))] * groups,
-            out_specs=whole,
+            out_specs=[pl.BlockSpec((order // halves, order), lambda i, m: (0, 0))] * halves,
             scratch_shapes=[pltpu.VMEM((order, depth), BF16), pltpu.VMEM((order, depth), BF16),
                             pltpu.VMEM((order, order), F32), pltpu.VMEM((order, order), F32)],
         ),
-        out_shape=jax.ShapeDtypeStruct((order, order), F32),
+        out_shape=[jax.ShapeDtypeStruct((order // halves, order), F32)] * halves,
         compiler_params=pltpu.CompilerParams(vmem_limit_bytes=VMEM_LIMIT),
         cost_estimate=pl.CostEstimate(
             flops=4 * order * order * width * side * y_n,
@@ -274,7 +282,7 @@
 
 def gram_y_kernel(species, side, core_ref, *refs):
     mine, others = refs[:species], refs[species:2 * species]
-    full_ref, gram_ref, sum_hh, sum_hl = refs[2 * species:]
+    full_ref, keep_ref, send_ref, sum_hh, sum_hl = refs[2 * species:]
     step = pl.program_id(0)
     core = core_ref[0]
     x_tile, rank, two = mine[0].shape
@@ -298,7 +306,8 @@
     @pl.when(step == pl.num_programs(0) - 1)
     def _():
         cross = sum_hl[...]
-        gram_ref[...] = sum_hh[...] + (cross + cross.T)
+        sum_hh[...] = sum_hh[...] + (cross + cross.T)
+        store_halves((keep_ref, send_ref), sum_hh, core)
 
 
 def gram_y_full(mine, others, core, side):
@@ -314,11 +323,11 @@
             grid=(half // x_tile,),
             in_specs=[part] * (2 * species),
             out_specs=[pl.BlockSpec((species, x_tile, rank, order), lambda i, c: (0, i, 0, 0)),
-                       pl.BlockSpec((order, order), lambda i, c: (0, 0))],
+                       *[pl.BlockSpec((order // CORES, order), lambda i, c: (0, 0))] * CORES],
             scratch_shapes=[pltpu.VMEM((order, order), F32), pltpu.VMEM((order, order), F32)],
         ),
         out_shape=[jax.ShapeDtypeStruct((species, half, rank, order), F32),
-                   jax.ShapeDtypeStruct((order, order), F32)],
+                   *[jax.ShapeDtypeStruct((order // CORES, order), F32)] * CORES],
         compiler_params=pltpu.CompilerParams(vmem_limit_bytes=VMEM_LIMIT),
         name="gram_y",
     )(core, *mine, *others)
@@ -353,12 +362,13 @@
     return lax.ppermute(value, AXES, [(i, i ^ mask) for i in range(total)])
 
 
-def all_sum(value, me, total):
-    stages = [(1, 2)]
-    while stages[-1][0] * stages[-1][1] < total:
-        step = stages[-1][0] * stages[-1][1]
+def all_sum(keep, send, me, total):
+    stages = []
+    step = CORES
+    while step < total:
         stages.append((step, min(4, total // step)))
-    current = value
+        step *= stages[-1][1]
+    current = keep + permute(send, 1, total)
     for step, count in stages:
         place = (me // step) % count
         parts = current.reshape(count, -1, current.shape[1])
@@ -369,15 +379,12 @@
             current = current + part
     for step, count in reversed(stages):
         place = (me // step) % count
-        got = [current] + [permute(current, step * k, total) for k in range(1, count)]
-        if count == 2:
-            swap = place == 1
-            got = [jnp.where(swap, got[1], got[0]), jnp.where(swap, got[0], got[1])]
-        else:
-            stack = jnp.stack(got)
-            got = [lax.dynamic_index_in_dim(stack, place ^ j, 0, False) for j in range(count)]
-        current = jnp.concatenate(got)
-    return current
+        stack = jnp.stack([current] + [permute(current, step * k, total) for k in range(1, count)])
+        current = jnp.concatenate(
+            [lax.dynamic_index_in_dim(stack, place ^ j, 0, False) for j in range(count)])
+    other = permute(current, 1, total)
+    swap = me % CORES == 1
+    return jnp.concatenate([jnp.where(swap, other, current), jnp.where(swap, current, other)])
 
 
 def exchange(field, group, groups, total):
@@ -428,10 +435,12 @@
     start_t = start_table(grid_n, RANK).T
 
     pieces = exchange(field, group, groups, total)
-    gram = jnp.zeros((grid_n, grid_n), F32)
+    gram = [jnp.zeros((grid_n, grid_n), F32)]
+    place = jnp.stack([group, core]).astype(jnp.int32)
     for s in range(species):
-        gram = gram_z_step(gram, pieces[s], one(group), side)
-    gram = all_sum(gram, me, total)
+        halves = CORES if s == species - 1 else 1
+        gram = gram_z_step(gram[0], pieces[s], place, side, halves)
+    gram = all_sum(*gram, me, total)
     basis_z, turned_z = leaf_basis(gram, start_t, one(gz), gz_n)
 
     side_pos = gy // CORES
@@ -440,8 +449,8 @@
     leaving = reduce_half(turned_z, pieces, away, side)
     others = [permute(value, 1, total) for value in leaving]
     mine = reduce_half(tie(turned_z, leaving[0]), pieces, home, side)
-    full, gram = gram_y_full(mine, others, one(core), side)
-    gram = all_sum(gram, me, total)
+    full, *gram = gram_y_full(mine, others, one(core), side)
+    gram = all_sum(*gram, me, total)
     basis_y, _ = leaf_basis(gram, start_t, one(gz), 1)
     core_tensor = project_core(basis_y, full)
     core_tensor = core_tensor.reshape(species, x_n // total, RANK * RANK)

time: 1660 us -> 1660 us (level)
  transfers between devices with their start and end apart: 92 -> 92, of which waited for: 44 -> 45; matrix products, arithmetic and copies ran while one was open for 0% -> 0% of each run, Pallas kernels for 9% -> 9%
where the time goes in v5:
time: 1660 us; the launch traced here: 1650 us
  starting transfers between devices  719 us (43%)
  waiting for transfers between devices  673 us (41%)
  Pallas kernels  240 us (14%)
    ppermute x92, starting transfers between devices, permute(): return lax.ppermute(value, AXES, [(i, i ^ mask) for i in range(total)])  719 us
    ppermute x92, waiting for transfers between devices, permute(): return lax.ppermute(value, AXES, [(i, i ^ mask) for i in range(total)])  673 us
    pallas_call x9, Pallas kernels, pack(): pl.pallas_call(functools.partial(pack_kernel, count, width), grid_spec=pl...  91.6 us
    pallas_call x4, Pallas kernels, gram_z_step(): pl.pallas_call(functools.partial(gram_z_kernel, groups, side), grid_spec=...  69.8 us
  transfers between devices with their start and end apart: 92, of which 45 were waited for; matrix products, arithmetic and copies ran while one was open for 0% of the time, Pallas kernels for 9%

profile of v5, /device:TPU:0, one launch (start us, length us, event | category | flops | bytes accessed | tf_op | source)
XLA Modules:
  0.0 1648.4 jit_solution(6079904813388233050)
XLA Ops:
  1.4 8.3 pack.9
  9.7 4.0 collective-permute-start.1
  14.4 8.3 pack.10
  22.7 10.7 pack.11
  36.8 3.6 collective-permute-start.4
  40.4 20.9 %collective-permute-done.1.refs_8_ = f32[32,64,128]{2,1,0:T(8,128)S(1)} collective-permute-done((f32[32,64,128]{2,1,0:T(8,128)}, f32[32,64,128]{2,1,0:T(8,128)S(1)}, u32[]{:S(2)}, u32[]{:S(2)}) %collective-permute-start.1) | collective-permute-done | bytes 1048608 | tf_op jit(solution)/shard_map/ppermute | solution.py:362
  62.4 19.8 %collective-permute-done.2.refs_4_ = f32[32,64,128]{2,1,0:T(8,128)S(1)} collective-permute-done((f32[32,64,128]{2,1,0:T(8,128)}, f32[32,64,128]{2,1,0:T(8,128)S(1)}, u32[]{:S(2)}, u32[]{:S(2)}) %collective-permute-start.2) | collective-permute-done | bytes 1048608 | tf_op jit(solution)/shard_map/ppermute | solution.py:362
  82.2 4.7 collective-permute-start.3
  86.9 42.2 %collective-permute-done.7.refs_9_ = f32[32,64,128]{2,1,0:T(8,128)S(1)} collective-permute-done((f32[32,64,128]{2,1,0:T(8,128)}, f32[32,64,128]{2,1,0:T(8,128)S(1)}, u32[]{:S(2)}, u32[]{:S(2)}) %collective-permute-start.7) | collective-permute-done | bytes 1048608 | tf_op jit(solution)/shard_map/ppermute | solution.py:362
  129.7 3.3 collective-permute-start.8
  133.0 41.2 %collective-permute-done.4.refs_10_ = f32[32,64,128]{2,1,0:T(8,128)} collective-permute-done((f32[32,64,128]{2,1,0:T(8,128)}, f32[32,64,128]{2,1,0:T(8,128)}, u32[]{:S(2)}, u32[]{:S(2)}) %collective-permute-start.4) | collective-permute-done | bytes 1048608 | tf_op jit(solution)/shard_map/ppermute | solution.py:362
  179.2 63.4 %collective-permute-done.9.refs_11_ = f32[32,64,128]{2,1,0:T(8,128)} collective-permute-done((f32[32,64,128]{2,1,0:T(8,128)}, f32[32,64,128]{2,1,0:T(8,128)}, u32[]{:S(2)}, u32[]{:S(2)}) %collective-permute-start.9) | collective-permute-done | bytes 1048608 | tf_op jit(solution)/shard_map/ppermute | solution.py:362
  242.6 5.3 collective-permute-start.13
  248.0 10.7 pack.12
  258.8 10.7 pack.13
  269.5 64.6 %collective-permute-start.16 = (f32[32,64,128]{2,1,0:T(8,128)}, f32[32,64,128]{2,1,0:T(8,128)S(1)}, u32[]{:S(2)}, u32[]{:S(2)}) collective-permute-start(f32[32,64,128]{2,1,0:T(8,128)} %get-tuple-element.184), channel_id=1, source_target_pairs={{0,16},{1,17},{2,18},{3,19},{4,20},{5,21},{6,22},{7,23},{8,24},{9,... | collective-permute-start | bytes 3145736 | tf_op jit(solution)/shard_map/ppermute | solution.py:362
  338.6 86.2 %collective-permute-start.19 = (f32[32,64,128]{2,1,0:T(8,128)}, f32[32,64,128]{2,1,0:T(8,128)}, u32[]{:S(2)}, u32[]{:S(2)}) collective-permute-start(f32[32,64,128]{2,1,0:T(8,128)} %get-tuple-element.191), channel_id=1, source_target_pairs={{0,18},{1,19},{2,16},{3,17},{4,22},{5,23},{6,20},{7,21},{8,26},{9,... | collective-permute-start | bytes 3145736 | tf_op jit(solution)/shard_map/ppermute | solution.py:362
  424.8 44.0 %collective-permute-done.16.refs_8_.refs_24_ = f32[32,64,128]{2,1,0:T(8,128)S(1)} collective-permute-done((f32[32,64,128]{2,1,0:T(8,128)}, f32[32,64,128]{2,1,0:T(8,128)S(1)}, u32[]{:S(2)}, u32[]{:S(2)}) %collective-permute-start.16) | collective-permute-done | bytes 1048608 | tf_op jit(solution)/shard_map/ppermute | solution.py:362
  471.6 20.5 %collective-permute-start.23 = (f32[32,64,128]{2,1,0:T(8,128)}, f32[32,64,128]{2,1,0:T(8,128)}, u32[]{:S(2)}, u32[]{:S(2)}) collective-permute-start(f32[32,64,128]{2,1,0:T(8,128)} %get-tuple-element.197), channel_id=1, source_target_pairs={{0,12},{1,13},{2,14},{3,15},{4,8},{5,9},{6,10},{7,11},{8,4},{9,5},... | collective-permute-start | bytes 3145736 | tf_op jit(solution)/shard_map/ppermute | solution.py:362
  492.1 44.3 %collective-permute-done.19.refs_9_.refs_25_ = f32[32,64,128]{2,1,0:T(8,128)} collective-permute-done((f32[32,64,128]{2,1,0:T(8,128)}, f32[32,64,128]{2,1,0:T(8,128)}, u32[]{:S(2)}, u32[]{:S(2)}) %collective-permute-start.19) | collective-permute-done | bytes 1048608 | tf_op jit(solution)/shard_map/ppermute | solution.py:362
  536.4 4.7 collective-permute-done.20.refs_5_.refs_21_
  543.4 63.6 %collective-permute-start.25 = (f32[32,64,128]{2,1,0:T(8,128)}, f32[32,64,128]{2,1,0:T(8,128)}, u32[]{:S(2)}, u32[]{:S(2)}) collective-permute-start(f32[32,64,128]{2,1,0:T(8,128)} %get-tuple-element.201), channel_id=1, source_target_pairs={{0,14},{1,15},{2,12},{3,13},{4,10},{5,11},{6,8},{7,9},{8,6},{9,7},... | collective-permute-start | bytes 3145736 | tf_op jit(solution)/shard_map/ppermute | solution.py:362
  607.0 21.2 %collective-permute-done.23.refs_6_.refs_22_ = f32[32,64,128]{2,1,0:T(8,128)} collective-permute-done((f32[32,64,128]{2,1,0:T(8,128)}, f32[32,64,128]{2,1,0:T(8,128)}, u32[]{:S(2)}, u32[]{:S(2)}) %collective-permute-start.23) | collective-permute-done | bytes 1048608 | tf_op jit(solution)/shard_map/ppermute | solution.py:362
  632.6 10.7 pack.14
  643.4 10.7 pack.15
  654.1 42.4 %collective-permute-start.31 = (f32[32,64,128]{2,1,0:T(8,128)}, f32[32,64,128]{2,1,0:T(8,128)S(1)}, u32[]{:S(2)}, u32[]{:S(2)}) collective-permute-start(f32[32,64,128]{2,1,0:T(8,128)} %get-tuple-element.217), channel_id=1, source_target_pairs={{0,16},{1,17},{2,18},{3,19},{4,20},{5,21},{6,22},{7,23},{8,24},{9,... | collective-permute-start | bytes 3145736 | tf_op jit(solution)/shard_map/ppermute | solution.py:362
  697.3 43.0 %collective-permute-done.27.refs_11_.refs_27_ = f32[32,64,128]{2,1,0:T(8,128)} collective-permute-done((f32[32,64,128]{2,1,0:T(8,128)}, f32[32,64,128]{2,1,0:T(8,128)}, u32[]{:S(2)}, u32[]{:S(2)}) %collective-permute-start.27) | collective-permute-done | bytes 1048608 | tf_op jit(solution)/shard_map/ppermute | solution.py:362
  743.8 43.5 %collective-permute-start.34 = (f32[32,64,128]{2,1,0:T(8,128)}, f32[32,64,128]{2,1,0:T(8,128)}, u32[]{:S(2)}, u32[]{:S(2)}) collective-permute-start(f32[32,64,128]{2,1,0:T(8,128)} %get-tuple-element.224), channel_id=1, source_target_pairs={{0,18},{1,19},{2,16},{3,17},{4,22},{5,23},{6,20},{7,21},{8,26},{9,... | collective-permute-start | bytes 3145736 | tf_op jit(solution)/shard_map/ppermute | solution.py:362
  787.3 41.7 %collective-permute-done.31.refs_8_.refs_40_ = f32[32,64,128]{2,1,0:T(8,128)S(1)} collective-permute-done((f32[32,64,128]{2,1,0:T(8,128)}, f32[32,64,128]{2,1,0:T(8,128)S(1)}, u32[]{:S(2)}, u32[]{:S(2)}) %collective-permute-start.31) | collective-permute-done | bytes 1048608 | tf_op jit(solution)/shard_map/ppermute | solution.py:362
  829.1 3.1 collective-permute-start.33
  834.1 20.5 %collective-permute-start.38 = (f32[32,64,128]{2,1,0:T(8,128)}, f32[32,64,128]{2,1,0:T(8,128)}, u32[]{:S(2)}, u32[]{:S(2)}) collective-permute-start(f32[32,64,128]{2,1,0:T(8,128)} %get-tuple-element.230), channel_id=1, source_target_pairs={{0,12},{1,13},{2,14},{3,15},{4,8},{5,9},{6,10},{7,11},{8,4},{9,5},... | collective-permute-start | bytes 3145736 | tf_op jit(solution)/shard_map/ppermute | solution.py:362
  854.6 43.7 %collective-permute-done.34.refs_9_.refs_41_ = f32[32,64,128]{2,1,0:T(8,128)} collective-permute-done((f32[32,64,128]{2,1,0:T(8,128)}, f32[32,64,128]{2,1,0:T(8,128)}, u32[]{:S(2)}, u32[]{:S(2)}) %collective-permute-start.34) | collective-permute-done | bytes 1048608 | tf_op jit(solution)/shard_map/ppermute | solution.py:362
  901.0 4.3 collective-permute-start.43
  905.3 63.5 %collective-permute-start.40 = (f32[32,64,128]{2,1,0:T(8,128)}, f32[32,64,128]{2,1,0:T(8,128)}, u32[]{:S(2)}, u32[]{:S(2)}) collective-permute-start(f32[32,64,128]{2,1,0:T(8,128)} %get-tuple-element.234), channel_id=1, source_target_pairs={{0,14},{1,15},{2,12},{3,13},{4,10},{5,11},{6,8},{7,9},{8,6},{9,7},... | collective-permute-start | bytes 3145736 | tf_op jit(solution)/shard_map/ppermute | solution.py:362
  968.8 20.5 %collective-permute-done.38.refs_6_.refs_38_ = f32[32,64,128]{2,1,0:T(8,128)} collective-permute-done((f32[32,64,128]{2,1,0:T(8,128)}, f32[32,64,128]{2,1,0:T(8,128)}, u32[]{:S(2)}, u32[]{:S(2)}) %collective-permute-start.38) | collective-permute-done | bytes 1048608 | tf_op jit(solution)/shard_map/ppermute | solution.py:362
  989.3 3.0 collective-permute-start.42
  994.8 10.7 pack.16
  1005.5 10.7 pack.17
  1016.2 40.1 %collective-permute-start.46 = (f32[32,64,128]{2,1,0:T(8,128)}, f32[32,64,128]{2,1,0:T(8,128)S(1)}, u32[]{:S(2)}, u32[]{:S(2)}) collective-permute-start(f32[32,64,128]{2,1,0:T(8,128)} %get-tuple-element.250), channel_id=1, source_target_pairs={{0,16},{1,17},{2,18},{3,19},{4,20},{5,21},{6,22},{7,23},{8,24},{9,... | collective-permute-start | bytes 3145736 | tf_op jit(solution)/shard_map/ppermute | solution.py:362
  1059.2 42.7 %collective-permute-done.42.refs_11_.refs_43_ = f32[32,64,128]{2,1,0:T(8,128)} collective-permute-done((f32[32,64,128]{2,1,0:T(8,128)}, f32[32,64,128]{2,1,0:T(8,128)}, u32[]{:S(2)}, u32[]{:S(2)}) %collective-permute-start.42) | collective-permute-done | bytes 1048608 | tf_op jit(solution)/shard_map/ppermute | solution.py:362
  1101.9 3.2 collective-permute-start.45
  1105.1 43.0 %collective-permute-start.49 = (f32[32,64,128]{2,1,0:T(8,128)}, f32[32,64,128]{2,1,0:T(8,128)}, u32[]{:S(2)}, u32[]{:S(2)}) collective-permute-start(f32[32,64,128]{2,1,0:T(8,128)} %get-tuple-element.257), channel_id=1, source_target_pairs={{0,18},{1,19},{2,16},{3,17},{4,22},{5,23},{6,20},{7,21},{8,26},{9,... | collective-permute-start | bytes 3145736 | tf_op jit(solution)/shard_map/ppermute | solution.py:362
  1148.1 42.7 %collective-permute-done.46.refs_8_.refs_56_ = f32[32,64,128]{2,1,0:T(8,128)S(1)} collective-permute-done((f32[32,64,128]{2,1,0:T(8,128)}, f32[32,64,128]{2,1,0:T(8,128)S(1)}, u32[]{:S(2)}, u32[]{:S(2)}) %collective-permute-start.46) | collective-permute-done | bytes 1048608 | tf_op jit(solution)/shard_map/ppermute | solution.py:362
  1190.8 3.3 collective-permute-start.48
  1196.0 41.8 %collective-permute-start.53 = (f32[32,64,128]{2,1,0:T(8,128)}, f32[32,64,128]{2,1,0:T(8,128)}, u32[]{:S(2)}, u32[]{:S(2)}) collective-permute-start(f32[32,64,128]{2,1,0:T(8,128)} %get-tuple-element.263), channel_id=1, source_target_pairs={{0,12},{1,13},{2,14},{3,15},{4,8},{5,9},{6,10},{7,11},{8,4},{9,5},... | collective-permute-start | bytes 3145736 | tf_op jit(solution)/shard_map/ppermute | solution.py:362
  1237.8 23.1 %collective-permute-done.49.refs_9_.refs_57_ = f32[32,64,128]{2,1,0:T(8,128)} collective-permute-done((f32[32,64,128]{2,1,0:T(8,128)}, f32[32,64,128]{2,1,0:T(8,128)}, u32[]{:S(2)}, u32[]{:S(2)}) %collective-permute-start.49) | collective-permute-done | bytes 1048608 | tf_op jit(solution)/shard_map/ppermute | solution.py:362
  1262.6 17.6 %gram_z.4.prev_ref = f32[512,512]{1,0:T(8,128)} custom-call(s32[2]{0:T(128)} %get-tuple-element.326.me_ref, f32[512,512]{1,0:T(8,128)} %broadcast_in_dim.2.prev_ref, f32[32,64,128]{2,1,0:T(8,128)} %get-tuple-element.150.refs_0_, f32[32,64,128]{2,1,0:T(8,128)} %collective-permute-done.refs_1_, f32[32,64,128]{2,1,0:T(8,128)} %collective-permute-done.3.refs_2_, ...), custom_call_target="tpu_custom_call" | custom-call | flops 8589934592 | bytes 16777216 | tf_op jit(solution)/shard_map/gram_z/pallas_call | solution.py:130
  1283.5 46.4 %collective-permute-start.55 = (f32[32,64,128]{2,1,0:T(8,128)}, f32[32,64,128]{2,1,0:T(8,128)S(1)}, u32[]{:S(2)}, u32[]{:S(2)}) collective-permute-start(f32[32,64,128]{2,1,0:T(8,128)} %get-tuple-element.267), channel_id=1, source_target_pairs={{0,14},{1,15},{2,12},{3,13},{4,10},{5,11},{6,8},{7,9},{8,6},{9,7},... | collective-permute-start | bytes 3145736 | tf_op jit(solution)/shard_map/ppermute | solution.py:362
  1329.8 21.5 %collective-permute-done.56.refs_10_.refs_58_ = f32[32,64,128]{2,1,0:T(8,128)} collective-permute-done((f32[32,64,128]{2,1,0:T(8,128)}, f32[32,64,128]{2,1,0:T(8,128)}, u32[]{:S(2)}, u32[]{:S(2)}) %collective-permute-start.56) | collective-permute-done | bytes 1048608 | tf_op jit(solution)/shard_map/ppermute | solution.py:362
  1351.3 10.2 collective-permute-start.59
  1361.6 17.4 %gram_z.5.prev_ref = f32[512,512]{1,0:T(8,128)} custom-call(s32[2]{0:T(128)} %get-tuple-element.326.me_ref, f32[512,512]{1,0:T(8,128)} %gram_z.4.prev_ref, f32[32,64,128]{2,1,0:T(8,128)} %get-tuple-element.176.refs_0_.refs_16_, f32[32,64,128]{2,1,0:T(8,128)} %copy-done.5, f32[32,64,128]{2,1,0:T(8,128)} %collective-permute-done.18.refs_2_.refs_18_, ...), custom_call_target="tpu_custom_call" | custom-call | flops 8589934592 | bytes 16777216 | tf_op jit(solution)/shard_map/gram_z/pallas_call | solution.py:130
  1378.9 17.4 %gram_z.6.prev_ref = f32[512,512]{1,0:T(8,128)} custom-call(s32[2]{0:T(128)} %get-tuple-element.326.me_ref, f32[512,512]{1,0:T(8,128)} %gram_z.5.prev_ref, f32[32,64,128]{2,1,0:T(8,128)} %get-tuple-element.209.refs_0_.refs_32_, f32[32,64,128]{2,1,0:T(8,128)} %copy-done.8, f32[32,64,128]{2,1,0:T(8,128)} %collective-permute-done.33.refs_2_.refs_34_, ...), custom_call_target="tpu_custom_call" | custom-call | flops 8589934592 | bytes 16777216 | tf_op jit(solution)/shard_map/gram_z/pallas_call | solution.py:130
  1396.4 47.6 %collective-permute-done.57.refs_11_.refs_59_ = f32[32,64,128]{2,1,0:T(8,128)} collective-permute-done((f32[32,64,128]{2,1,0:T(8,128)}, f32[32,64,128]{2,1,0:T(8,128)}, u32[]{:S(2)}, u32[]{:S(2)}) %collective-permute-start.57) | collective-permute-done | bytes 1048608 | tf_op jit(solution)/shard_map/ppermute | solution.py:362
  1444.0 17.5 %gram_z.7 = (f32[256,512]{1,0:T(8,128)}, f32[256,512]{1,0:T(8,128)}) custom-call(s32[2]{0:T(128)} %get-tuple-element.326.me_ref, f32[512,512]{1,0:T(8,128)} %gram_z.6.prev_ref, f32[32,64,128]{2,1,0:T(8,128)} %get-tuple-element.242.refs_0_.refs_48_, f32[32,64,128]{2,1,0:T(8,128)} %copy-done.11, f32[32,64,128]{2,1,0:T(8,128)} %collective-permute-done.48.refs_2_.refs_50_, ...), custom_call_target="tpu_custom_call" | custom-call | flops 8589934592 | bytes 16777216 | tf_op jit(solution)/shard_map/gram_z/pallas_call | solution.py:130
  1465.0 4.6 collective-permute-start.63
  1470.5 5.6 collective-permute-done.63
  1477.5 22.0 %collective-permute-start.64 = (f32[16,512]{1,0:T(8,128)S(1)}, f32[16,512]{1,0:T(8,128)S(1)}, u32[]{:S(2)}, u32[]{:S(2)}) collective-permute-start(f32[16,512]{1,0:T(8,128)S(1)} %get-tuple-element.322), channel_id=1, source_target_pairs={{0,8},{1,9},{2,10},{3,11},{4,12},{5,13},{6,14},{7,15},{8,0},{9,1},... | collective-permute-start | bytes 98312 | tf_op jit(solution)/shard_map/ppermute | solution.py:362
  1501.3 3.8 collective-permute-done.66
  1524.2 14.5 leaf_basis.2
  1538.7 16.3 reduce_z.2
  1556.1 16.2 reduce_z.3
  1574.0 10.8 gram_y.1
  1624.6 14.5 leaf_basis.3
  1639.1 6.0 core.1
  (210 shorter events, 118.5 us)
Async XLA Ops:
  9.7 51.6 %collective-permute-start.1 = (f32[32,64,128]{2,1,0:T(8,128)}, f32[32,64,128]{2,1,0:T(8,128)S(1)}, u32[]{:S(2)}, u32[]{:S(2)}) collective-permute-start(f32[32,64,128]{2,1,0:T(8,128)} %get-tuple-element.146), channel_id=1, source_target_pairs={{0,16},{1,17},{2,18},{3,19},{4,20},{5,21},{6,22},{7,23},{8,24},{9,... | collective-permute-start | bytes 3145736 | tf_op jit(solution)/shard_map/ppermute | solution.py:362
  33.4 48.8 %collective-permute-start.2 = (f32[32,64,128]{2,1,0:T(8,128)}, f32[32,64,128]{2,1,0:T(8,128)S(1)}, u32[]{:S(2)}, u32[]{:S(2)}) collective-permute-start(f32[32,64,128]{2,1,0:T(8,128)} %get-tuple-element.154), channel_id=1, source_target_pairs={{0,8},{1,9},{2,10},{3,11},{4,12},{5,13},{6,14},{7,15},{8,0},{9,1},... | collective-permute-start | bytes 3145736 | tf_op jit(solution)/shard_map/ppermute | solution.py:362
  35.0 94.1 %collective-permute-start.7 = (f32[32,64,128]{2,1,0:T(8,128)}, f32[32,64,128]{2,1,0:T(8,128)S(1)}, u32[]{:S(2)}, u32[]{:S(2)}) collective-permute-start(f32[32,64,128]{2,1,0:T(8,128)} %get-tuple-element.163), channel_id=1, source_target_pairs={{0,18},{1,19},{2,16},{3,17},{4,22},{5,23},{6,20},{7,21},{8,26},{9,... | collective-permute-start | bytes 3145736 | tf_op jit(solution)/shard_map/ppermute | solution.py:362
  36.3 93.5 %collective-permute-start = (f32[32,64,128]{2,1,0:T(8,128)}, f32[32,64,128]{2,1,0:T(8,128)}, u32[]{:S(2)}, u32[]{:S(2)}) collective-permute-start(f32[32,64,128]{2,1,0:T(8,128)} %get-tuple-element.151), channel_id=1, source_target_pairs={{0,2},{1,3},{2,0},{3,1},{4,6},{5,7},{6,4},{7,5},{8,10},{9,11},{10,... | collective-permute-start | bytes 3145736 | tf_op jit(solution)/shard_map/ppermute | solution.py:362
  36.8 137.4 %collective-permute-start.4 = (f32[32,64,128]{2,1,0:T(8,128)}, f32[32,64,128]{2,1,0:T(8,128)}, u32[]{:S(2)}, u32[]{:S(2)}) collective-permute-start(f32[32,64,128]{2,1,0:T(8,128)} %get-tuple-element.158), channel_id=1, source_target_pairs={{0,20},{1,21},{2,22},{3,23},{4,16},{5,17},{6,18},{7,19},{8,28},{9,... | collective-permute-start | bytes 3145736 | tf_op jit(solution)/shard_map/ppermute | solution.py:362
  61.3 115.4 %collective-permute-start.5 = (f32[32,64,128]{2,1,0:T(8,128)}, f32[32,64,128]{2,1,0:T(8,128)}, u32[]{:S(2)}, u32[]{:S(2)}) collective-permute-start(f32[32,64,128]{2,1,0:T(8,128)} %get-tuple-element.159), channel_id=1, source_target_pairs={{0,10},{1,11},{2,8},{3,9},{4,14},{5,15},{6,12},{7,13},{8,2},{9,3},... | collective-permute-start | bytes 3145736 | tf_op jit(solution)/shard_map/ppermute | solution.py:362
  82.2 95.9 %collective-permute-start.3 = (f32[32,64,128]{2,1,0:T(8,128)}, f32[32,64,128]{2,1,0:T(8,128)}, u32[]{:S(2)}, u32[]{:S(2)}) collective-permute-start(f32[32,64,128]{2,1,0:T(8,128)} %get-tuple-element.155), channel_id=1, source_target_pairs={{0,4},{1,5},{2,6},{3,7},{4,0},{5,1},{6,2},{7,3},{8,12},{9,13},{10,... | collective-permute-start | bytes 3145736 | tf_op jit(solution)/shard_map/ppermute | solution.py:362
  129.1 113.5 %collective-permute-start.9 = (f32[32,64,128]{2,1,0:T(8,128)}, f32[32,64,128]{2,1,0:T(8,128)}, u32[]{:S(2)}, u32[]{:S(2)}) collective-permute-start(f32[32,64,128]{2,1,0:T(8,128)} %get-tuple-element.167), channel_id=1, source_target_pairs={{0,22},{1,23},{2,20},{3,21},{4,18},{5,19},{6,16},{7,17},{8,30},{9,... | collective-permute-start | bytes 3145736 | tf_op jit(solution)/shard_map/ppermute | solution.py:362
  129.7 112.9 %collective-permute-start.8 = (f32[32,64,128]{2,1,0:T(8,128)}, f32[32,64,128]{2,1,0:T(8,128)}, u32[]{:S(2)}, u32[]{:S(2)}) collective-permute-start(f32[32,64,128]{2,1,0:T(8,128)} %get-tuple-element.164), channel_id=1, source_target_pairs={{0,12},{1,13},{2,14},{3,15},{4,8},{5,9},{6,10},{7,11},{8,4},{9,5},... | collective-permute-start | bytes 3145736 | tf_op jit(solution)/shard_map/ppermute | solution.py:362
  174.2 73.8 %collective-permute-start.11 = (f32[32,64,128]{2,1,0:T(8,128)}, f32[32,64,128]{2,1,0:T(8,128)}, u32[]{:S(2)}, u32[]{:S(2)}) collective-permute-start(f32[32,64,128]{2,1,0:T(8,128)} %get-tuple-element.169), channel_id=1, source_target_pairs={{0,24},{1,25},{2,26},{3,27},{4,28},{5,29},{6,30},{7,31},{8,16},{9,... | collective-permute-start | bytes 3145736 | tf_op jit(solution)/shard_map/ppermute | solution.py:362
  176.7 92.8 %collective-permute-start.6 = (f32[32,64,128]{2,1,0:T(8,128)}, f32[32,64,128]{2,1,0:T(8,128)}, u32[]{:S(2)}, u32[]{:S(2)}) collective-permute-start(f32[32,64,128]{2,1,0:T(8,128)} %get-tuple-element.160), channel_id=1, source_target_pairs={{0,6},{1,7},{2,4},{3,5},{4,2},{5,3},{6,0},{7,1},{8,14},{9,15},{10,... | collective-permute-start | bytes 3145736 | tf_op jit(solution)/shard_map/ppermute | solution.py:362
  178.1 91.3 %collective-permute-start.12 = (f32[32,64,128]{2,1,0:T(8,128)}, f32[32,64,128]{2,1,0:T(8,128)}, u32[]{:S(2)}, u32[]{:S(2)}) collective-permute-start(f32[32,64,128]{2,1,0:T(8,128)} %get-tuple-element.170), channel_id=1, source_target_pairs={{0,26},{1,27},{2,24},{3,25},{4,30},{5,31},{6,28},{7,29},{8,18},{9,... | collective-permute-start | bytes 3145736 | tf_op jit(solution)/shard_map/ppermute | solution.py:362
  242.6 92.1 %collective-permute-start.10 = (f32[32,64,128]{2,1,0:T(8,128)}, f32[32,64,128]{2,1,0:T(8,128)}, u32[]{:S(2)}, u32[]{:S(2)}) collective-permute-start(f32[32,64,128]{2,1,0:T(8,128)} %get-tuple-element.168), channel_id=1, source_target_pairs={{0,14},{1,15},{2,12},{3,13},{4,10},{5,11},{6,8},{7,9},{8,6},{9,7},... | collective-permute-start | bytes 3145736 | tf_op jit(solution)/shard_map/ppermute | solution.py:362
  242.6 92.1 %collective-permute-start.13 = (f32[32,64,128]{2,1,0:T(8,128)}, f32[32,64,128]{2,1,0:T(8,128)}, u32[]{:S(2)}, u32[]{:S(2)}) collective-permute-start(f32[32,64,128]{2,1,0:T(8,128)} %get-tuple-element.171), channel_id=1, source_target_pairs={{0,28},{1,29},{2,30},{3,31},{4,24},{5,25},{6,26},{7,27},{8,20},{9,... | collective-permute-start | bytes 3145736 | tf_op jit(solution)/shard_map/ppermute | solution.py:362
  248.0 90.6 %collective-permute-start.14 = (f32[32,64,128]{2,1,0:T(8,128)}, f32[32,64,128]{2,1,0:T(8,128)}, u32[]{:S(2)}, u32[]{:S(2)}) collective-permute-start(f32[32,64,128]{2,1,0:T(8,128)} %get-tuple-element.172), channel_id=1, source_target_pairs={{0,30},{1,31},{2,28},{3,29},{4,26},{5,27},{6,24},{7,25},{8,22},{9,... | collective-permute-start | bytes 3145736 | tf_op jit(solution)/shard_map/ppermute | solution.py:362
  269.5 199.4 %collective-permute-start.16 = (f32[32,64,128]{2,1,0:T(8,128)}, f32[32,64,128]{2,1,0:T(8,128)S(1)}, u32[]{:S(2)}, u32[]{:S(2)}) collective-permute-start(f32[32,64,128]{2,1,0:T(8,128)} %get-tuple-element.184), channel_id=1, source_target_pairs={{0,16},{1,17},{2,18},{3,19},{4,20},{5,21},{6,22},{7,23},{8,24},{9,... | collective-permute-start | bytes 3145736 | tf_op jit(solution)/shard_map/ppermute | solution.py:362
  334.1 134.8 %collective-permute-start.17 = (f32[32,64,128]{2,1,0:T(8,128)}, f32[32,64,128]{2,1,0:T(8,128)S(1)}, u32[]{:S(2)}, u32[]{:S(2)}) collective-permute-start(f32[32,64,128]{2,1,0:T(8,128)} %get-tuple-element.185), channel_id=1, source_target_pairs={{0,8},{1,9},{2,10},{3,11},{4,12},{5,13},{6,14},{7,15},{8,0},{9,1},... | collective-permute-start | bytes 3145736 | tf_op jit(solution)/shard_map/ppermute | solution.py:362
  334.7 134.9 %collective-permute-start.15 = (f32[32,64,128]{2,1,0:T(8,128)}, f32[32,64,128]{2,1,0:T(8,128)S(1)}, u32[]{:S(2)}, u32[]{:S(2)}) collective-permute-start(f32[32,64,128]{2,1,0:T(8,128)} %get-tuple-element.179), channel_id=1, source_target_pairs={{0,2},{1,3},{2,0},{3,1},{4,6},{5,7},{6,4},{7,5},{8,10},{9,11},{10,... | collective-permute-start | bytes 3145736 | tf_op jit(solution)/shard_map/ppermute | solution.py:362
  336.2 135.4 %collective-permute-start.22 = (f32[32,64,128]{2,1,0:T(8,128)}, f32[32,64,128]{2,1,0:T(8,128)}, u32[]{:S(2)}, u32[]{:S(2)}) collective-permute-start(f32[32,64,128]{2,1,0:T(8,128)} %get-tuple-element.196), channel_id=1, source_target_pairs={{0,24},{1,25},{2,26},{3,27},{4,28},{5,29},{6,30},{7,31},{8,16},{9,... | collective-permute-start | bytes 3145736 | tf_op jit(solution)/shard_map/ppermute | solution.py:362
  338.6 197.8 %collective-permute-start.19 = (f32[32,64,128]{2,1,0:T(8,128)}, f32[32,64,128]{2,1,0:T(8,128)}, u32[]{:S(2)}, u32[]{:S(2)}) collective-permute-start(f32[32,64,128]{2,1,0:T(8,128)} %get-tuple-element.191), channel_id=1, source_target_pairs={{0,18},{1,19},{2,16},{3,17},{4,22},{5,23},{6,20},{7,21},{8,26},{9,... | collective-permute-start | bytes 3145736 | tf_op jit(solution)/shard_map/ppermute | solution.py:362
  468.9 72.3 %collective-permute-start.20 = (f32[32,64,128]{2,1,0:T(8,128)}, f32[32,64,128]{2,1,0:T(8,128)}, u32[]{:S(2)}, u32[]{:S(2)}) collective-permute-start(f32[32,64,128]{2,1,0:T(8,128)} %get-tuple-element.192), channel_id=1, source_target_pairs={{0,10},{1,11},{2,8},{3,9},{4,14},{5,15},{6,12},{7,13},{8,2},{9,3},... | collective-permute-start | bytes 3145736 | tf_op jit(solution)/shard_map/ppermute | solution.py:362
  468.9 72.2 %collective-permute-start.18 = (f32[32,64,128]{2,1,0:T(8,128)}, f32[32,64,128]{2,1,0:T(8,128)}, u32[]{:S(2)}, u32[]{:S(2)}) collective-permute-start(f32[32,64,128]{2,1,0:T(8,128)} %get-tuple-element.186), channel_id=1, source_target_pairs={{0,4},{1,5},{2,6},{3,7},{4,0},{5,1},{6,2},{7,3},{8,12},{9,13},{10,... | collective-permute-start | bytes 3145736 | tf_op jit(solution)/shard_map/ppermute | solution.py:362
  469.6 73.7 %collective-permute-start.24 = (f32[32,64,128]{2,1,0:T(8,128)}, f32[32,64,128]{2,1,0:T(8,128)}, u32[]{:S(2)}, u32[]{:S(2)}) collective-permute-start(f32[32,64,128]{2,1,0:T(8,128)} %get-tuple-element.200), channel_id=1, source_target_pairs={{0,26},{1,27},{2,24},{3,25},{4,30},{5,31},{6,28},{7,29},{8,18},{9,... | collective-permute-start | bytes 3145736 | tf_op jit(solution)/shard_map/ppermute | solution.py:362
  471.6 156.6 %collective-permute-start.23 = (f32[32,64,128]{2,1,0:T(8,128)}, f32[32,64,128]{2,1,0:T(8,128)}, u32[]{:S(2)}, u32[]{:S(2)}) collective-permute-start(f32[32,64,128]{2,1,0:T(8,128)} %get-tuple-element.197), channel_id=1, source_target_pairs={{0,12},{1,13},{2,14},{3,15},{4,8},{5,9},{6,10},{7,11},{8,4},{9,5},... | collective-permute-start | bytes 3145736 | tf_op jit(solution)/shard_map/ppermute | solution.py:362
  536.4 93.4 %collective-permute-start.26 = (f32[32,64,128]{2,1,0:T(8,128)}, f32[32,64,128]{2,1,0:T(8,128)}, u32[]{:S(2)}, u32[]{:S(2)}) collective-permute-start(f32[32,64,128]{2,1,0:T(8,128)} %get-tuple-element.202), channel_id=1, source_target_pairs={{0,20},{1,21},{2,22},{3,23},{4,16},{5,17},{6,18},{7,19},{8,28},{9,... | collective-permute-start | bytes 3145736 | tf_op jit(solution)/shard_map/ppermute | solution.py:362
  541.1 112.9 %collective-permute-start.21 = (f32[32,64,128]{2,1,0:T(8,128)}, f32[32,64,128]{2,1,0:T(8,128)}, u32[]{:S(2)}, u32[]{:S(2)}) collective-permute-start(f32[32,64,128]{2,1,0:T(8,128)} %get-tuple-element.193), channel_id=1, source_target_pairs={{0,6},{1,7},{2,4},{3,5},{4,2},{5,3},{6,0},{7,1},{8,14},{9,15},{10,... | collective-permute-start | bytes 3145736 | tf_op jit(solution)/shard_map/ppermute | solution.py:362
  541.1 112.9 %collective-permute-start.28 = (f32[32,64,128]{2,1,0:T(8,128)}, f32[32,64,128]{2,1,0:T(8,128)}, u32[]{:S(2)}, u32[]{:S(2)}) collective-permute-start(f32[32,64,128]{2,1,0:T(8,128)} %get-tuple-element.204), channel_id=1, source_target_pairs={{0,28},{1,29},{2,30},{3,31},{4,24},{5,25},{6,26},{7,27},{8,20},{9,... | collective-permute-start | bytes 3145736 | tf_op jit(solution)/shard_map/ppermute | solution.py:362
  543.4 153.9 %collective-permute-start.25 = (f32[32,64,128]{2,1,0:T(8,128)}, f32[32,64,128]{2,1,0:T(8,128)}, u32[]{:S(2)}, u32[]{:S(2)}) collective-permute-start(f32[32,64,128]{2,1,0:T(8,128)} %get-tuple-element.201), channel_id=1, source_target_pairs={{0,14},{1,15},{2,12},{3,13},{4,10},{5,11},{6,8},{7,9},{8,6},{9,7},... | collective-permute-start | bytes 3145736 | tf_op jit(solution)/shard_map/ppermute | solution.py:362
  628.2 112.0 %collective-permute-start.27 = (f32[32,64,128]{2,1,0:T(8,128)}, f32[32,64,128]{2,1,0:T(8,128)}, u32[]{:S(2)}, u32[]{:S(2)}) collective-permute-start(f32[32,64,128]{2,1,0:T(8,128)} %get-tuple-element.203), channel_id=1, source_target_pairs={{0,22},{1,23},{2,20},{3,21},{4,18},{5,19},{6,16},{7,17},{8,30},{9,... | collective-permute-start | bytes 3145736 | tf_op jit(solution)/shard_map/ppermute | solution.py:362
  629.8 114.0 %collective-permute-start.29 = (f32[32,64,128]{2,1,0:T(8,128)}, f32[32,64,128]{2,1,0:T(8,128)}, u32[]{:S(2)}, u32[]{:S(2)}) collective-permute-start(f32[32,64,128]{2,1,0:T(8,128)} %get-tuple-element.205), channel_id=1, source_target_pairs={{0,30},{1,31},{2,28},{3,29},{4,26},{5,27},{6,24},{7,25},{8,22},{9,... | collective-permute-start | bytes 3145736 | tf_op jit(solution)/shard_map/ppermute | solution.py:362
  654.1 174.9 %collective-permute-start.31 = (f32[32,64,128]{2,1,0:T(8,128)}, f32[32,64,128]{2,1,0:T(8,128)S(1)}, u32[]{:S(2)}, u32[]{:S(2)}) collective-permute-start(f32[32,64,128]{2,1,0:T(8,128)} %get-tuple-element.217), channel_id=1, source_target_pairs={{0,16},{1,17},{2,18},{3,19},{4,20},{5,21},{6,22},{7,23},{8,24},{9,... | collective-permute-start | bytes 3145736 | tf_op jit(solution)/shard_map/ppermute | solution.py:362
  696.4 132.6 %collective-permute-start.32 = (f32[32,64,128]{2,1,0:T(8,128)}, f32[32,64,128]{2,1,0:T(8,128)S(1)}, u32[]{:S(2)}, u32[]{:S(2)}) collective-permute-start(f32[32,64,128]{2,1,0:T(8,128)} %get-tuple-element.218), channel_id=1, source_target_pairs={{0,8},{1,9},{2,10},{3,11},{4,12},{5,13},{6,14},{7,15},{8,0},{9,1},... | collective-permute-start | bytes 3145736 | tf_op jit(solution)/shard_map/ppermute | solution.py:362
  740.3 91.9 %collective-permute-start.30 = (f32[32,64,128]{2,1,0:T(8,128)}, f32[32,64,128]{2,1,0:T(8,128)S(1)}, u32[]{:S(2)}, u32[]{:S(2)}) collective-permute-start(f32[32,64,128]{2,1,0:T(8,128)} %get-tuple-element.212), channel_id=1, source_target_pairs={{0,2},{1,3},{2,0},{3,1},{4,6},{5,7},{6,4},{7,5},{8,10},{9,11},{10,... | collective-permute-start | bytes 3145736 | tf_op jit(solution)/shard_map/ppermute | solution.py:362
  743.1 90.9 %collective-permute-start.37 = (f32[32,64,128]{2,1,0:T(8,128)}, f32[32,64,128]{2,1,0:T(8,128)}, u32[]{:S(2)}, u32[]{:S(2)}) collective-permute-start(f32[32,64,128]{2,1,0:T(8,128)} %get-tuple-element.229), channel_id=1, source_target_pairs={{0,24},{1,25},{2,26},{3,27},{4,28},{5,29},{6,30},{7,31},{8,16},{9,... | collective-permute-start | bytes 3145736 | tf_op jit(solution)/shard_map/ppermute | solution.py:362
  743.8 154.5 %collective-permute-start.34 = (f32[32,64,128]{2,1,0:T(8,128)}, f32[32,64,128]{2,1,0:T(8,128)}, u32[]{:S(2)}, u32[]{:S(2)}) collective-permute-start(f32[32,64,128]{2,1,0:T(8,128)} %get-tuple-element.224), channel_id=1, source_target_pairs={{0,18},{1,19},{2,16},{3,17},{4,22},{5,23},{6,20},{7,21},{8,26},{9,... | collective-permute-start | bytes 3145736 | tf_op jit(solution)/shard_map/ppermute | solution.py:362
  829.0 71.4 %collective-permute-start.35 = (f32[32,64,128]{2,1,0:T(8,128)}, f32[32,64,128]{2,1,0:T(8,128)}, u32[]{:S(2)}, u32[]{:S(2)}) collective-permute-start(f32[32,64,128]{2,1,0:T(8,128)} %get-tuple-element.225), channel_id=1, source_target_pairs={{0,10},{1,11},{2,8},{3,9},{4,14},{5,15},{6,12},{7,13},{8,2},{9,3},... | collective-permute-start | bytes 3145736 | tf_op jit(solution)/shard_map/ppermute | solution.py:362
  829.1 71.9 %collective-permute-start.33 = (f32[32,64,128]{2,1,0:T(8,128)}, f32[32,64,128]{2,1,0:T(8,128)}, u32[]{:S(2)}, u32[]{:S(2)}) collective-permute-start(f32[32,64,128]{2,1,0:T(8,128)} %get-tuple-element.219), channel_id=1, source_target_pairs={{0,4},{1,5},{2,6},{3,7},{4,0},{5,1},{6,2},{7,3},{8,12},{9,13},{10,... | collective-permute-start | bytes 3145736 | tf_op jit(solution)/shard_map/ppermute | solution.py:362
  832.2 73.1 %collective-permute-start.39 = (f32[32,64,128]{2,1,0:T(8,128)}, f32[32,64,128]{2,1,0:T(8,128)}, u32[]{:S(2)}, u32[]{:S(2)}) collective-permute-start(f32[32,64,128]{2,1,0:T(8,128)} %get-tuple-element.233), channel_id=1, source_target_pairs={{0,26},{1,27},{2,24},{3,25},{4,30},{5,31},{6,28},{7,29},{8,18},{9,... | collective-permute-start | bytes 3145736 | tf_op jit(solution)/shard_map/ppermute | solution.py:362
  834.1 155.2 %collective-permute-start.38 = (f32[32,64,128]{2,1,0:T(8,128)}, f32[32,64,128]{2,1,0:T(8,128)}, u32[]{:S(2)}, u32[]{:S(2)}) collective-permute-start(f32[32,64,128]{2,1,0:T(8,128)} %get-tuple-element.230), channel_id=1, source_target_pairs={{0,12},{1,13},{2,14},{3,15},{4,8},{5,9},{6,10},{7,11},{8,4},{9,5},... | collective-permute-start | bytes 3145736 | tf_op jit(solution)/shard_map/ppermute | solution.py:362
  898.3 94.0 %collective-permute-start.41 = (f32[32,64,128]{2,1,0:T(8,128)}, f32[32,64,128]{2,1,0:T(8,128)}, u32[]{:S(2)}, u32[]{:S(2)}) collective-permute-start(f32[32,64,128]{2,1,0:T(8,128)} %get-tuple-element.235), channel_id=1, source_target_pairs={{0,20},{1,21},{2,22},{3,23},{4,16},{5,17},{6,18},{7,19},{8,28},{9,... | collective-permute-start | bytes 3145736 | tf_op jit(solution)/shard_map/ppermute | solution.py:362
  900.4 115.8 %collective-permute-start.36 = (f32[32,64,128]{2,1,0:T(8,128)}, f32[32,64,128]{2,1,0:T(8,128)}, u32[]{:S(2)}, u32[]{:S(2)}) collective-permute-start(f32[32,64,128]{2,1,0:T(8,128)} %get-tuple-element.226), channel_id=1, source_target_pairs={{0,6},{1,7},{2,4},{3,5},{4,2},{5,3},{6,0},{7,1},{8,14},{9,15},{10,... | collective-permute-start | bytes 3145736 | tf_op jit(solution)/shard_map/ppermute | solution.py:362
  901.0 115.2 %collective-permute-start.43 = (f32[32,64,128]{2,1,0:T(8,128)}, f32[32,64,128]{2,1,0:T(8,128)}, u32[]{:S(2)}, u32[]{:S(2)}) collective-permute-start(f32[32,64,128]{2,1,0:T(8,128)} %get-tuple-element.237), channel_id=1, source_target_pairs={{0,28},{1,29},{2,30},{3,31},{4,24},{5,25},{6,26},{7,27},{8,20},{9,... | collective-permute-start | bytes 3145736 | tf_op jit(solution)/shard_map/ppermute | solution.py:362
  905.3 153.9 %collective-permute-start.40 = (f32[32,64,128]{2,1,0:T(8,128)}, f32[32,64,128]{2,1,0:T(8,128)}, u32[]{:S(2)}, u32[]{:S(2)}) collective-permute-start(f32[32,64,128]{2,1,0:T(8,128)} %get-tuple-element.234), channel_id=1, source_target_pairs={{0,14},{1,15},{2,12},{3,13},{4,10},{5,11},{6,8},{7,9},{8,6},{9,7},... | collective-permute-start | bytes 3145736 | tf_op jit(solution)/shard_map/ppermute | solution.py:362
  989.3 112.6 %collective-permute-start.42 = (f32[32,64,128]{2,1,0:T(8,128)}, f32[32,64,128]{2,1,0:T(8,128)}, u32[]{:S(2)}, u32[]{:S(2)}) collective-permute-start(f32[32,64,128]{2,1,0:T(8,128)} %get-tuple-element.236), channel_id=1, source_target_pairs={{0,22},{1,23},{2,20},{3,21},{4,18},{5,19},{6,16},{7,17},{8,30},{9,... | collective-permute-start | bytes 3145736 | tf_op jit(solution)/shard_map/ppermute | solution.py:362
  992.3 112.8 %collective-permute-start.44 = (f32[32,64,128]{2,1,0:T(8,128)}, f32[32,64,128]{2,1,0:T(8,128)}, u32[]{:S(2)}, u32[]{:S(2)}) collective-permute-start(f32[32,64,128]{2,1,0:T(8,128)} %get-tuple-element.238), channel_id=1, source_target_pairs={{0,30},{1,31},{2,28},{3,29},{4,26},{5,27},{6,24},{7,25},{8,22},{9,... | collective-permute-start | bytes 3145736 | tf_op jit(solution)/shard_map/ppermute | solution.py:362
  1016.2 174.5 %collective-permute-start.46 = (f32[32,64,128]{2,1,0:T(8,128)}, f32[32,64,128]{2,1,0:T(8,128)S(1)}, u32[]{:S(2)}, u32[]{:S(2)}) collective-permute-start(f32[32,64,128]{2,1,0:T(8,128)} %get-tuple-element.250), channel_id=1, source_target_pairs={{0,16},{1,17},{2,18},{3,19},{4,20},{5,21},{6,22},{7,23},{8,24},{9,... | collective-permute-start | bytes 3145736 | tf_op jit(solution)/shard_map/ppermute | solution.py:362
  1056.4 134.4 %collective-permute-start.47 = (f32[32,64,128]{2,1,0:T(8,128)}, f32[32,64,128]{2,1,0:T(8,128)S(1)}, u32[]{:S(2)}, u32[]{:S(2)}) collective-permute-start(f32[32,64,128]{2,1,0:T(8,128)} %get-tuple-element.251), channel_id=1, source_target_pairs={{0,8},{1,9},{2,10},{3,11},{4,12},{5,13},{6,14},{7,15},{8,0},{9,1},... | collective-permute-start | bytes 3145736 | tf_op jit(solution)/shard_map/ppermute | solution.py:362
  1101.9 92.2 %collective-permute-start.45 = (f32[32,64,128]{2,1,0:T(8,128)}, f32[32,64,128]{2,1,0:T(8,128)S(1)}, u32[]{:S(2)}, u32[]{:S(2)}) collective-permute-start(f32[32,64,128]{2,1,0:T(8,128)} %get-tuple-element.245), channel_id=1, source_target_pairs={{0,2},{1,3},{2,0},{3,1},{4,6},{5,7},{6,4},{7,5},{8,10},{9,11},{10,... | collective-permute-start | bytes 3145736 | tf_op jit(solution)/shard_map/ppermute | solution.py:362
  1105.1 90.9 %collective-permute-start.52 = (f32[32,64,128]{2,1,0:T(8,128)}, f32[32,64,128]{2,1,0:T(8,128)}, u32[]{:S(2)}, u32[]{:S(2)}) collective-permute-start(f32[32,64,128]{2,1,0:T(8,128)} %get-tuple-element.262), channel_id=1, source_target_pairs={{0,24},{1,25},{2,26},{3,27},{4,28},{5,29},{6,30},{7,31},{8,16},{9,... | collective-permute-start | bytes 3145736 | tf_op jit(solution)/shard_map/ppermute | solution.py:362
  1105.1 155.8 %collective-permute-start.49 = (f32[32,64,128]{2,1,0:T(8,128)}, f32[32,64,128]{2,1,0:T(8,128)}, u32[]{:S(2)}, u32[]{:S(2)}) collective-permute-start(f32[32,64,128]{2,1,0:T(8,128)} %get-tuple-element.257), channel_id=1, source_target_pairs={{0,18},{1,19},{2,16},{3,17},{4,22},{5,23},{6,20},{7,21},{8,26},{9,... | collective-permute-start | bytes 3145736 | tf_op jit(solution)/shard_map/ppermute | solution.py:362
  1190.7 89.5 %collective-permute-start.50 = (f32[32,64,128]{2,1,0:T(8,128)}, f32[32,64,128]{2,1,0:T(8,128)}, u32[]{:S(2)}, u32[]{:S(2)}) collective-permute-start(f32[32,64,128]{2,1,0:T(8,128)} %get-tuple-element.258), channel_id=1, source_target_pairs={{0,10},{1,11},{2,8},{3,9},{4,14},{5,15},{6,12},{7,13},{8,2},{9,3},... | collective-permute-start | bytes 3145736 | tf_op jit(solution)/shard_map/ppermute | solution.py:362
  1190.8 91.1 %collective-permute-start.48 = (f32[32,64,128]{2,1,0:T(8,128)}, f32[32,64,128]{2,1,0:T(8,128)}, u32[]{:S(2)}, u32[]{:S(2)}) collective-permute-start(f32[32,64,128]{2,1,0:T(8,128)} %get-tuple-element.252), channel_id=1, source_target_pairs={{0,4},{1,5},{2,6},{3,7},{4,0},{5,1},{6,2},{7,3},{8,12},{9,13},{10,... | collective-permute-start | bytes 3145736 | tf_op jit(solution)/shard_map/ppermute | solution.py:362
  1194.1 89.4 %collective-permute-start.54 = (f32[32,64,128]{2,1,0:T(8,128)}, f32[32,64,128]{2,1,0:T(8,128)}, u32[]{:S(2)}, u32[]{:S(2)}) collective-permute-start(f32[32,64,128]{2,1,0:T(8,128)} %get-tuple-element.266), channel_id=1, source_target_pairs={{0,26},{1,27},{2,24},{3,25},{4,30},{5,31},{6,28},{7,29},{8,18},{9,... | collective-permute-start | bytes 3145736 | tf_op jit(solution)/shard_map/ppermute | solution.py:362
  1196.0 133.8 %collective-permute-start.53 = (f32[32,64,128]{2,1,0:T(8,128)}, f32[32,64,128]{2,1,0:T(8,128)}, u32[]{:S(2)}, u32[]{:S(2)}) collective-permute-start(f32[32,64,128]{2,1,0:T(8,128)} %get-tuple-element.263), channel_id=1, source_target_pairs={{0,12},{1,13},{2,14},{3,15},{4,8},{5,9},{6,10},{7,11},{8,4},{9,5},... | collective-permute-start | bytes 3145736 | tf_op jit(solution)/shard_map/ppermute | solution.py:362
  1260.9 90.4 %collective-permute-start.56 = (f32[32,64,128]{2,1,0:T(8,128)}, f32[32,64,128]{2,1,0:T(8,128)}, u32[]{:S(2)}, u32[]{:S(2)}) collective-permute-start(f32[32,64,128]{2,1,0:T(8,128)} %get-tuple-element.268), channel_id=1, source_target_pairs={{0,20},{1,21},{2,22},{3,23},{4,16},{5,17},{6,18},{7,19},{8,28},{9,... | collective-permute-start | bytes 3145736 | tf_op jit(solution)/shard_map/ppermute | solution.py:362
  1280.2 116.1 %collective-permute-start.51 = (f32[32,64,128]{2,1,0:T(8,128)}, f32[32,64,128]{2,1,0:T(8,128)S(1)}, u32[]{:S(2)}, u32[]{:S(2)}) collective-permute-start(f32[32,64,128]{2,1,0:T(8,128)} %get-tuple-element.259), channel_id=1, source_target_pairs={{0,6},{1,7},{2,4},{3,5},{4,2},{5,3},{6,0},{7,1},{8,14},{9,15},{10,... | collective-permute-start | bytes 3145736 | tf_op jit(solution)/shard_map/ppermute | solution.py:362
  1281.9 114.5 %collective-permute-start.58 = (f32[32,64,128]{2,1,0:T(8,128)}, f32[32,64,128]{2,1,0:T(8,128)S(1)}, u32[]{:S(2)}, u32[]{:S(2)}) collective-permute-start(f32[32,64,128]{2,1,0:T(8,128)} %get-tuple-element.270), channel_id=1, source_target_pairs={{0,28},{1,29},{2,30},{3,31},{4,24},{5,25},{6,26},{7,27},{8,20},{9,... | collective-permute-start | bytes 3145736 | tf_op jit(solution)/shard_map/ppermute | solution.py:362
  1283.5 112.9 %collective-permute-start.55 = (f32[32,64,128]{2,1,0:T(8,128)}, f32[32,64,128]{2,1,0:T(8,128)S(1)}, u32[]{:S(2)}, u32[]{:S(2)}) collective-permute-start(f32[32,64,128]{2,1,0:T(8,128)} %get-tuple-element.267), channel_id=1, source_target_pairs={{0,14},{1,15},{2,12},{3,13},{4,10},{5,11},{6,8},{7,9},{8,6},{9,7},... | collective-permute-start | bytes 3145736 | tf_op jit(solution)/shard_map/ppermute | solution.py:362
  1329.8 114.2 %collective-permute-start.57 = (f32[32,64,128]{2,1,0:T(8,128)}, f32[32,64,128]{2,1,0:T(8,128)}, u32[]{:S(2)}, u32[]{:S(2)}) collective-permute-start(f32[32,64,128]{2,1,0:T(8,128)} %get-tuple-element.269), channel_id=1, source_target_pairs={{0,22},{1,23},{2,20},{3,21},{4,18},{5,19},{6,16},{7,17},{8,30},{9,... | collective-permute-start | bytes 3145736 | tf_op jit(solution)/shard_map/ppermute | solution.py:362
  1351.3 92.7 %collective-permute-start.59 = (f32[32,64,128]{2,1,0:T(8,128)}, f32[32,64,128]{2,1,0:T(8,128)}, u32[]{:S(2)}, u32[]{:S(2)}) collective-permute-start(f32[32,64,128]{2,1,0:T(8,128)} %get-tuple-element.271), channel_id=1, source_target_pairs={{0,30},{1,31},{2,28},{3,29},{4,26},{5,27},{6,24},{7,25},{8,22},{9,... | collective-permute-start | bytes 3145736 | tf_op jit(solution)/shard_map/ppermute | solution.py:362
  1477.5 23.9 %collective-permute-start.64 = (f32[16,512]{1,0:T(8,128)S(1)}, f32[16,512]{1,0:T(8,128)S(1)}, u32[]{:S(2)}, u32[]{:S(2)}) collective-permute-start(f32[16,512]{1,0:T(8,128)S(1)} %get-tuple-element.322), channel_id=1, source_target_pairs={{0,8},{1,9},{2,10},{3,11},{4,12},{5,13},{6,14},{7,15},{8,0},{9,1},... | collective-permute-start | bytes 98312 | tf_op jit(solution)/shard_map/ppermute | solution.py:362
  1555.0 17.3 %collective-permute-start.75 = (f32[16,64,256]{2,1,0:T(8,128)}, f32[16,64,256]{2,1,0:T(8,128)S(1)}, u32[]{:S(2)}, u32[]{:S(2)}) collective-permute-start(f32[16,64,256]{2,1,0:T(8,128)} %get-tuple-element.281), channel_id=1, source_target_pairs={{0,1},{1,0},{2,3},{3,2},{4,5},{5,4},{6,7},{7,6},{8,9},{9,8},{10,11... | collective-permute-start | bytes 3145736 | tf_op jit(solution)/shard_map/ppermute | solution.py:362
  1555.5 16.9 %collective-permute-start.76 = (f32[16,64,256]{2,1,0:T(8,128)}, f32[16,64,256]{2,1,0:T(8,128)S(1)}, u32[]{:S(2)}, u32[]{:S(2)}) collective-permute-start(f32[16,64,256]{2,1,0:T(8,128)} %get-tuple-element.282), channel_id=1, source_target_pairs={{0,1},{1,0},{2,3},{3,2},{4,5},{5,4},{6,7},{7,6},{8,9},{9,8},{10,11... | collective-permute-start | bytes 3145736 | tf_op jit(solution)/shard_map/ppermute | solution.py:362
  1555.6 16.8 %collective-permute-start.77 = (f32[16,64,256]{2,1,0:T(8,128)}, f32[16,64,256]{2,1,0:T(8,128)S(1)}, u32[]{:S(2)}, u32[]{:S(2)}) collective-permute-start(f32[16,64,256]{2,1,0:T(8,128)} %get-tuple-element.283), channel_id=1, source_target_pairs={{0,1},{1,0},{2,3},{3,2},{4,5},{5,4},{6,7},{7,6},{8,9},{9,8},{10,11... | collective-permute-start | bytes 3145736 | tf_op jit(solution)/shard_map/ppermute | solution.py:362
  (46 other events, 2126.6 us)
